TPU v7x, 512 devices: a whole 4x4x16 slice. The times are simulated.
512 devices in a mesh: blk: 16 (over z_lo, core), rows: 32 (over y, x, z_hi).
Axes of the slice: x: 4, y: 4, z: 16 (z_hi: 2, z_lo: 8; z = z_hi * 8 + z_lo), core: 2. Of those that a mesh axis runs over, the one named last changes fastest.
Arguments:
- p_vals: bfloat16 [64, 64, 8, 128, 128], P('blk', 'rows'), may hold values from -2.5 to 2.5
- p_cols: int32 [64, 64, 8], replicated, may hold values from 0 to 4095, as said below
- c_cols: int32 [64, 64, 12], P('blk', 'rows'), may hold values from 0 to 4095, as said below
Outputs:
- c_vals: bfloat16 [64, 64, 12, 128, 128], P('blk', 'rows')
Inputs may be any that keep to these rules, and one draw needn't show every extreme that they name: `p_cols`: each block row's 8 columns are distinct, the row's own site among them, and each lies within one site of the row's site along both lattice dimensions, cyclically. `c_cols`: each block row's 12 pattern columns are distinct, the row's own site among them, and each lies within two sites of the row's site along both lattice dimensions, cyclically.
All inputs are finite; a program needn't handle non-finite values.
Results may differ from a plain program's by a relative error of at most 0.001.
Values may be sent and summed in bfloat16 or wider, within the bound.
No kernel may reach another device: no remote copies, remote signals or barrier semaphores. Data moves between devices by JAX's collectives and lax.ppermute only.
A program may use at most 64 MiB of HBM per device.

v0:
```python
import jax
import jax.numpy as jnp
from jax import lax
from jax.sharding import PartitionSpec as P


def padded_2(block, sides, width):
    for axis, dim in sides:
        count = lax.axis_size(axis)
        forward = [(i, i + 1) for i in range(count - 1)]
        forward.append((count - 1, 0))
        backward = [(target, source) for source, target in forward]
        low = lax.ppermute(
            lax.slice_in_dim(block, block.shape[dim] - width, None, axis=dim), axis, forward
        )
        high = lax.ppermute(lax.slice_in_dim(block, 0, width, axis=dim), axis, backward)
        block = jnp.concatenate([low, block, high], axis=dim)
    return block


def contract_rows(left_blocks, right_blocks, right_cols, targets):
    hits = (right_cols[:, None, :, :] == targets[:, :, None, None]).astype(jnp.int32)
    which = jnp.argmax(hits, axis=3)
    present = jnp.max(hits, axis=3) > 0
    picked = jnp.take_along_axis(right_blocks[:, None], which[:, :, :, None, None, None], axis=3)[
        :, :, :, 0
    ]
    picked = jnp.where(present[:, :, :, None, None], picked, jnp.zeros_like(picked))
    merged = jnp.einsum("ymab,ynmbc->ynac", left_blocks, picked, preferred_element_type=jnp.float32)
    return merged.astype(jnp.bfloat16)


def on_device(p_vals, p_cols, c_cols):
    cells_x = p_vals.shape[0]
    cells_y = p_vals.shape[1]
    blocks = p_vals.shape[2]
    edge = p_vals.shape[3]
    total_x = p_cols.shape[0]
    total_y = p_cols.shape[1]
    widened = padded_2(p_vals, (("blk", 0),), 1)
    padded = padded_2(widened, (("rows", 1),), 1)
    stacked = padded.reshape((cells_x + 2) * (cells_y + 2), blocks, edge, edge)
    anchor_x = lax.axis_index("blk") * cells_x
    anchor_y = lax.axis_index("rows") * cells_y
    own_cols = lax.dynamic_slice(
        p_cols, (anchor_x, anchor_y, jnp.int32(0)), (cells_x, cells_y, blocks)
    )
    col_table = p_cols.reshape(total_x * total_y, blocks)

    def one_column(column):
        partners = lax.dynamic_index_in_dim(own_cols, column, 0, False)
        near_x = (partners // total_y - anchor_x + 1) % total_x
        near_y = (partners % total_y - anchor_y + 1) % total_y
        local_ids = near_x * (cells_y + 2) + near_y
        left_blocks = lax.dynamic_index_in_dim(p_vals, column, 0, False)
        targets = lax.dynamic_index_in_dim(c_cols, column, 0, False)
        return contract_rows(left_blocks, stacked[local_ids], col_table[partners], targets)

    return lax.map(one_column, jnp.arange(cells_x, dtype=jnp.int32))


def solution(mesh):
    placed = (P("blk", "rows", None, None, None), P(), P("blk", "rows", None))
    return jax.shard_map(
        on_device,
        mesh=mesh,
        in_specs=placed,
        out_specs=P("blk", "rows", None, None, None),
        check_vma=False,
    )
```

profile of v0, /device:TPU:101, one launch (start us, length us, event | category | flops | bytes accessed | tf_op | source)
XLA Modules:
  0.0 487.9 jit_solution(9256403629041561086)
XLA Ops:
  1.4 5.3 %collective-permute-start = (bf16[1,2,8,128,128]{4,3,2,1,0:T(8,128)(2,1)S(1)}, bf16[1,2,8,128,128]{4,3,2,1,0:T(8,128)(2,1)S(1)}, u32[]{:S(2)}, u32[]{:S(2)}) collective-permute-start(bf16[1,2,8,128,128]{4,3,2,1,0:T(8,128)(2,1)S(1)} %get-tuple-element.160), channel_id=1, source_target_pairs={{0,32},{32,64},{64,96},{96,128},{128,160},{160,192},{192,224},{224... | collective-permute-start | bytes 1572872 | tf_op jit(solution)/shard_map/ppermute | solution.py:13
  6.8 1.9 collective-permute-start.1
  8.7 4.2 collective-permute-done
  13.2 9.2 %collective-permute-done.1 = bf16[1,2,8,128,128]{4,3,2,1,0:T(8,128)(2,1)S(1)} collective-permute-done((bf16[1,2,8,128,128]{4,3,2,1,0:T(8,128)(2,1)S(1)}, bf16[1,2,8,128,128]{4,3,2,1,0:T(8,128)(2,1)S(1)}, u32[]{:S(2)}, u32[]{:S(2)}) %collective-permute-start.1) | collective-permute-done | bytes 524320 | tf_op jit(solution)/shard_map/ppermute | solution.py:16
  22.5 1.9 fusion.28
  24.4 11.5 %collective-permute-start.2 = (bf16[6,1,8,128,128]{4,3,2,1,0:T(8,128)(2,1)}, bf16[6,1,8,128,128]{4,3,2,1,0:T(8,128)(2,1)}, u32[]{:S(2)}, u32[]{:S(2)}) collective-permute-start(bf16[6,1,8,128,128]{4,3,2,1,0:T(8,128)(2,1)} %get-tuple-element.157), channel_id=1, source_target_pairs={{0,1},{1,2},{2,3},{3,4},{4,5},{5,6},{6,7},{7,8},{8,9},{9,10},{10,1... | collective-permute-start | bytes 4718600 | tf_op jit(solution)/shard_map/ppermute | solution.py:13
  35.9 3.4 collective-permute-start.3
  39.3 1.9 copy.22
  42.0 171.2 %collective-permute-done.2 = bf16[6,1,8,128,128]{4,3,2,1,0:T(8,128)(2,1)} collective-permute-done((bf16[6,1,8,128,128]{4,3,2,1,0:T(8,128)(2,1)}, bf16[6,1,8,128,128]{4,3,2,1,0:T(8,128)(2,1)}, u32[]{:S(2)}, u32[]{:S(2)}) %collective-permute-start.2) | collective-permute-done | bytes 1572896 | tf_op jit(solution)/shard_map/ppermute | solution.py:13
  213.2 93.9 %collective-permute-done.3 = bf16[6,1,8,128,128]{4,3,2,1,0:T(8,128)(2,1)} collective-permute-done((bf16[6,1,8,128,128]{4,3,2,1,0:T(8,128)(2,1)}, bf16[6,1,8,128,128]{4,3,2,1,0:T(8,128)(2,1)}, u32[]{:S(2)}, u32[]{:S(2)}) %collective-permute-start.3) | collective-permute-done | bytes 1572896 | tf_op jit(solution)/shard_map/ppermute | solution.py:16
  307.1 5.0 %pad_maximum_fusion = bf16[6,4,8,128,128]{4,3,2,1,0:T(8,128)(2,1)} fusion(bf16[6,1,8,128,128]{4,3,2,1,0:T(8,128)(2,1)} %collective-permute-done.3, bf16[6,2,8,128,128]{4,3,2,1,0:T(8,128)(2,1)S(1)} %constant_dynamic-update-slice_fusion.1, bf16[6,1,8,128,128]{4,3,2,1,0:T(8,128)(2,1)} %collective-permute-done.2), kind=kLoop, calls=%fused_computation.57 | loop fusion | flops 6291456 | bytes 12582912 | tf_op jit(solution)/shard_map/concatenate | solution.py:17
  312.1 175.8 %while.12 = (s32[]{:T(128)}, bf16[4,2,12,128,128]{4,3,2,1,0:T(8,128)(2,1)}, s32[4]{0:T(128)S(1)}, s32[4,2,8]{2,1,0:T(2,128)S(1)}, s32[4096,8]{1,0:T(8,128)}, /*i...) while((s32[]{:T(128)}, ...), condition=%wide.region_3.4_spmd, body=%wide.region_0.3_spmd.sunk | while | flops 812015424 | bytes 44335368 | solution.py:59
  315.3 2.2 gather_fusion.1
  318.8 5.8 %gather_fusion = bf16[16,8,128,128]{3,2,1,0:T(8,128)(2,1)} fusion(bf16[24,8,128,128]{3,2,1,0:T(8,128)(2,1)} %get-tuple-element.262, s32[1024]{0:T(1024)S(1)} %pad_clamp_fusion.4), kind=kCustom, calls=%fused_computation.1.clone.1 | custom fusion | bytes 8388672 | tf_op jit(solution)/shard_map/while/body/eval_jaxpr/gather | solution.py:57
  324.6 16.7 %gather_fusion.2 = bf16[192,128,128]{2,1,0:T(8,128)(2,1)} fusion(bf16[2,8,8,128,128]{4,3,2,1,0:T(8,128)(2,1)} %bitcast.74, s32[192]{0:T(256)S(1)} %reshape.316), kind=kCustom, calls=%fused_computation.2.clone.1 | custom fusion | bytes 12585216 | tf_op jit(solution)/shard_map/while/body/eval_jaxpr/jit(take_along_axis)/gather | solution.py:25
  341.3 8.7 %copy.36 = bf16[192,128,128]{1,2,0:T(8,128)(2,1)} copy(bf16[192,128,128]{2,1,0:T(8,128)(2,1)} %gather_fusion.2) | data formatting | bytes 12582912 | tf_op jit(solution)/shard_map/while/body/eval_jaxpr/jit(take_along_axis)/gather | solution.py:25
  350.0 4.7 fusion.39
  359.3 2.2 gather_fusion.1
  362.7 5.8 %gather_fusion = bf16[16,8,128,128]{3,2,1,0:T(8,128)(2,1)} fusion(bf16[24,8,128,128]{3,2,1,0:T(8,128)(2,1)} %get-tuple-element.262, s32[1024]{0:T(1024)S(1)} %pad_clamp_fusion.4), kind=kCustom, calls=%fused_computation.1.clone.1 | custom fusion | bytes 8388672 | tf_op jit(solution)/shard_map/while/body/eval_jaxpr/gather | solution.py:57
  368.6 16.7 %gather_fusion.2 = bf16[192,128,128]{2,1,0:T(8,128)(2,1)} fusion(bf16[2,8,8,128,128]{4,3,2,1,0:T(8,128)(2,1)} %bitcast.74, s32[192]{0:T(256)S(1)} %reshape.316), kind=kCustom, calls=%fused_computation.2.clone.1 | custom fusion | bytes 12585216 | tf_op jit(solution)/shard_map/while/body/eval_jaxpr/jit(take_along_axis)/gather | solution.py:25
  385.3 8.7 %copy.36 = bf16[192,128,128]{1,2,0:T(8,128)(2,1)} copy(bf16[192,128,128]{2,1,0:T(8,128)(2,1)} %gather_fusion.2) | data formatting | bytes 12582912 | tf_op jit(solution)/shard_map/while/body/eval_jaxpr/jit(take_along_axis)/gather | solution.py:25
  394.0 4.7 fusion.39
  403.2 2.2 gather_fusion.1
  406.7 5.8 %gather_fusion = bf16[16,8,128,128]{3,2,1,0:T(8,128)(2,1)} fusion(bf16[24,8,128,128]{3,2,1,0:T(8,128)(2,1)} %get-tuple-element.262, s32[1024]{0:T(1024)S(1)} %pad_clamp_fusion.4), kind=kCustom, calls=%fused_computation.1.clone.1 | custom fusion | bytes 8388672 | tf_op jit(solution)/shard_map/while/body/eval_jaxpr/gather | solution.py:57
  412.5 16.7 %gather_fusion.2 = bf16[192,128,128]{2,1,0:T(8,128)(2,1)} fusion(bf16[2,8,8,128,128]{4,3,2,1,0:T(8,128)(2,1)} %bitcast.74, s32[192]{0:T(256)S(1)} %reshape.316), kind=kCustom, calls=%fused_computation.2.clone.1 | custom fusion | bytes 12585216 | tf_op jit(solution)/shard_map/while/body/eval_jaxpr/jit(take_along_axis)/gather | solution.py:25
  429.3 8.7 %copy.36 = bf16[192,128,128]{1,2,0:T(8,128)(2,1)} copy(bf16[192,128,128]{2,1,0:T(8,128)(2,1)} %gather_fusion.2) | data formatting | bytes 12582912 | tf_op jit(solution)/shard_map/while/body/eval_jaxpr/jit(take_along_axis)/gather | solution.py:25
  437.9 4.7 fusion.39
  447.2 2.2 gather_fusion.1
  450.6 5.8 %gather_fusion = bf16[16,8,128,128]{3,2,1,0:T(8,128)(2,1)} fusion(bf16[24,8,128,128]{3,2,1,0:T(8,128)(2,1)} %get-tuple-element.262, s32[1024]{0:T(1024)S(1)} %pad_clamp_fusion.4), kind=kCustom, calls=%fused_computation.1.clone.1 | custom fusion | bytes 8388672 | tf_op jit(solution)/shard_map/while/body/eval_jaxpr/gather | solution.py:57
  456.5 16.7 %gather_fusion.2 = bf16[192,128,128]{2,1,0:T(8,128)(2,1)} fusion(bf16[2,8,8,128,128]{4,3,2,1,0:T(8,128)(2,1)} %bitcast.74, s32[192]{0:T(256)S(1)} %reshape.316), kind=kCustom, calls=%fused_computation.2.clone.1 | custom fusion | bytes 12585216 | tf_op jit(solution)/shard_map/while/body/eval_jaxpr/jit(take_along_axis)/gather | solution.py:25
  473.2 8.7 %copy.36 = bf16[192,128,128]{1,2,0:T(8,128)(2,1)} copy(bf16[192,128,128]{2,1,0:T(8,128)(2,1)} %gather_fusion.2) | data formatting | bytes 12582912 | tf_op jit(solution)/shard_map/while/body/eval_jaxpr/jit(take_along_axis)/gather | solution.py:25
  481.9 4.7 fusion.39
  (99 shorter events, 18.8 us)
Async XLA Ops:
  0.0 12.9 %copy-start = (bf16[4,2,8,128,128]{4,3,2,1,0:T(8,128)(2,1)S(1)}, bf16[4,2,8,128,128]{4,3,2,1,0:T(8,128)(2,1)}, u32[]{:S(2)}) copy-start(bf16[4,2,8,128,128]{4,3,2,1,0:T(8,128)(2,1)} %param.5) | copy-start | bytes 6291460
  1.4 11.4 %collective-permute-start = (bf16[1,2,8,128,128]{4,3,2,1,0:T(8,128)(2,1)S(1)}, bf16[1,2,8,128,128]{4,3,2,1,0:T(8,128)(2,1)S(1)}, u32[]{:S(2)}, u32[]{:S(2)}) collective-permute-start(bf16[1,2,8,128,128]{4,3,2,1,0:T(8,128)(2,1)S(1)} %get-tuple-element.160), channel_id=1, source_target_pairs={{0,32},{32,64},{64,96},{96,128},{128,160},{160,192},{192,224},{224... | collective-permute-start | bytes 1572872 | tf_op jit(solution)/shard_map/ppermute | solution.py:13
  6.8 15.7 %collective-permute-start.1 = (bf16[1,2,8,128,128]{4,3,2,1,0:T(8,128)(2,1)S(1)}, bf16[1,2,8,128,128]{4,3,2,1,0:T(8,128)(2,1)S(1)}, u32[]{:S(2)}, u32[]{:S(2)}) collective-permute-start(bf16[1,2,8,128,128]{4,3,2,1,0:T(8,128)(2,1)S(1)} %get-tuple-element.159), channel_id=1, source_target_pairs={{32,0},{64,32},{96,64},{128,96},{160,128},{192,160},{224,192},{256... | collective-permute-start | bytes 1572872 | tf_op jit(solution)/shard_map/ppermute | solution.py:16
  22.5 16.8 %copy-start.1 = (s32[64,64,8]{1,2,0:T(8,128)S(1)}, s32[64,64,8]{1,2,0:T(8,128)}, u32[]{:S(2)}) copy-start(s32[64,64,8]{1,2,0:T(8,128)} %param.6) | copy-start | bytes 393220
  24.4 188.8 %collective-permute-start.2 = (bf16[6,1,8,128,128]{4,3,2,1,0:T(8,128)(2,1)}, bf16[6,1,8,128,128]{4,3,2,1,0:T(8,128)(2,1)}, u32[]{:S(2)}, u32[]{:S(2)}) collective-permute-start(bf16[6,1,8,128,128]{4,3,2,1,0:T(8,128)(2,1)} %get-tuple-element.157), channel_id=1, source_target_pairs={{0,1},{1,2},{2,3},{3,4},{4,5},{5,6},{6,7},{7,8},{8,9},{9,10},{10,1... | collective-permute-start | bytes 4718600 | tf_op jit(solution)/shard_map/ppermute | solution.py:13
  35.9 271.2 %collective-permute-start.3 = (bf16[6,1,8,128,128]{4,3,2,1,0:T(8,128)(2,1)}, bf16[6,1,8,128,128]{4,3,2,1,0:T(8,128)(2,1)}, u32[]{:S(2)}, u32[]{:S(2)}) collective-permute-start(bf16[6,1,8,128,128]{4,3,2,1,0:T(8,128)(2,1)} %get-tuple-element.158), channel_id=1, source_target_pairs={{1,0},{2,1},{3,2},{4,3},{5,4},{6,5},{7,6},{8,7},{9,8},{10,9},{11,1... | collective-permute-start | bytes 4718600 | tf_op jit(solution)/shard_map/ppermute | solution.py:16
where the time goes:
time: 490 us; the launch traced here: 488 us
  waiting for transfers between devices  279 us (57%)
  local copies, waits for them, and re-layouts  152 us (31%)
  starting transfers between devices  22.1 us (5%)
  matrix products  18.8 us (4%)
  other arithmetic  8.69 us (2%)
  loops' own time  7.19 us (1%)
    ppermute x2, waiting for transfers between devices, padded_2(): lax.ppermute(lax.slice_in_dim(block, block.shape[dim] - width, None, axis...  175 us
    ppermute x2, waiting for transfers between devices, padded_2(): lax.ppermute(lax.slice_in_dim(block, 0, width, axis=dim), axis, backward)  103 us
    gather x16, local copies, waits for them, and re-layouts, contract_rows(): jnp.take_along_axis(right_blocks[:, None], which[:, :, :, None, None, Non...  102 us
    gather x4, local copies, waits for them, and re-layouts, one_column(): stacked[local_ids]  23.3 us
    dot_general x4, matrix products, contract_rows(): jnp.einsum('ymab,ynmbc->ynac', left_blocks, picked, preferred_element_typ...  18.8 us
    ppermute x2, starting transfers between devices, padded_2(): lax.ppermute(lax.slice_in_dim(block, block.shape[dim] - width, None, axis...  16.8 us
  transfers between devices with their start and end apart: 4, of which 4 were waited for; matrix products, arithmetic and copies ran while one was open for 1% of the time, Pallas kernels for 0%

commit v1 on v0

v1 whole, which is shorter than its diff:
```python
import jax
import jax.numpy as jnp
import numpy as np
from jax import lax
from jax.experimental import pallas as pl
from jax.experimental.pallas import tpu as pltpu
from jax.sharding import PartitionSpec as P

AXES = ("blk", "rows")
OWN, EARLY_LOW, EARLY_HIGH, EARLY_WRAP, SIDE_LOW, SIDE_HIGH, LATE_LOW, LATE_HIGH, LATE_WRAP, PIECES = (
    0, 8, 10, 12, 13, 17, 21, 23, 25, 26
)


def send(value, moves, n_rows):
    return lax.ppermute(value, AXES, [(a[0] * n_rows + a[1], b[0] * n_rows + b[1]) for a, b in moves])


def moves_y(shift, n_blk, n_rows):
    return [((b, r), (b, (r + shift) % n_rows)) for b in range(n_blk) for r in range(n_rows)]


def moves_x(shift, n_blk, n_rows):
    moves = []
    for b in range(n_blk):
        for r in range(n_rows):
            inside = 0 <= b + shift < n_blk
            moves.append(((b, r), ((b + shift) % n_blk, r if inside else (r + 1) % n_rows)))
    return moves


def moves_wrap(n_blk, n_rows):
    edges = ((n_blk - 1, 0), (0, n_blk - 1))
    return [((b, r), (to, (r - 1) % n_rows)) for b, to in edges for r in range(n_rows)]


def accumulate(table_m, table_q, own, x, col, pieces, write, unroll):
    site = x * 2 + col
    left = jnp.concatenate([own[x, col, table_m[site * PIECES + number]] for number, _ in pieces], axis=1)

    def pair(h, carry):
        halves = []
        for n in (2 * h, 2 * h + 1):
            rows = []
            for number, block_of in pieces:
                q = table_q[(site * PIECES + number) * 12 + n]
                block = block_of(jnp.minimum(q, 7))
                rows.append(jnp.where(q < 8, block, jnp.zeros_like(block)))
            halves.append(jnp.concatenate(rows, axis=0))
        right = jnp.concatenate(halves, axis=1)
        total = jnp.dot(left, right, preferred_element_type=jnp.float32)
        write(x, col, 2 * h, total[:, :128])
        write(x, col, 2 * h + 1, total[:, 128:])
        return carry

    lax.fori_loop(0, 6, pair, 0, unroll=unroll)


def block_from(ref, *lead):
    return lambda q: ref[(*lead, q)]


def first_kernel(table_m, table_q, own, up, down, wrap, acc):
    cells_x = own.shape[0]

    def write(x, col, n, total):
        acc[x, col, n] = total

    for x in range(cells_x):
        for col in range(2):
            pieces = []
            for near in (x - 1, x, x + 1):
                if near < 0:
                    pieces += [(EARLY_LOW + y, block_from(up, y)) for y in range(2)]
                elif near >= cells_x:
                    pieces += [(EARLY_HIGH + y, block_from(down, y)) for y in range(2)]
                else:
                    pieces += [(OWN + near * 2 + y, block_from(own, near, y)) for y in range(2)]
            if x in (0, cells_x - 1):
                pieces.append((EARLY_WRAP, block_from(wrap)))
            accumulate(table_m, table_q, own, x, col, pieces, write, 2)


def rim_kernel(table_m, table_q, own, acc, rim_low, rim_high, out):
    cells_x = own.shape[0]
    rims = (rim_low, rim_high)

    def write(x, col, n, total):
        out[x, col, n] = acc[x, col, n] + total

    for x in range(cells_x):
        for col in range(2):
            at = int(x >= cells_x // 2)
            number = (SIDE_LOW, SIDE_HIGH)[col] + at * (cells_x - 1)
            accumulate(table_m, table_q, own, x, col, [(number, block_from(rims[col], at))], write, 2)


def last_kernel(table_m, table_q, own, acc, mid_low, mid_high, up, down, wrap, out, held, sems):
    cells_x = own.shape[0]
    mids = (mid_low, mid_high)

    def write(x, col, n, total):
        held[x, col, n] = (acc[x, col, n] + total).astype(jnp.bfloat16)

    copies = []
    for x in (1, 2, 0, 3):
        for col in range(2):
            first = (SIDE_LOW, SIDE_HIGH)[col]
            pieces = [
                (first + near, block_from(mids[col], near - 1))
                for near in (x - 1, x, x + 1)
                if 0 < near < cells_x - 1
            ]
            if x == 0:
                pieces += [(LATE_LOW + y, block_from(up, y)) for y in range(2)]
            if x == cells_x - 1:
                pieces += [(LATE_HIGH + y, block_from(down, y)) for y in range(2)]
            if x in (0, cells_x - 1):
                pieces.append((LATE_WRAP, block_from(wrap)))
            accumulate(table_m, table_q, own, x, col, pieces, write, 6)
            copies.append(pltpu.make_async_copy(held.at[x, col], out.at[x, col], sems.at[x, col]))
            copies[-1].start()
    for copy in copies:
        copy.wait()


def run_kernel(body, tables, own, sites, flops, last=False):
    shape = (own.shape[0], 2, 12, 128, 128)
    return pl.pallas_call(
        body,
        out_shape=jax.ShapeDtypeStruct(shape, jnp.bfloat16 if last else jnp.float32),
        in_specs=[pl.BlockSpec(memory_space=pltpu.SMEM)] * 2
        + [pl.BlockSpec(memory_space=pltpu.VMEM)] * (1 + len(sites)),
        out_specs=pl.BlockSpec(memory_space=pl.ANY if last else pltpu.VMEM),
        scratch_shapes=[pltpu.VMEM(shape, jnp.bfloat16), pltpu.SemaphoreType.DMA(shape[:2])] if last else [],
        compiler_params=pltpu.CompilerParams(vmem_limit_bytes=32 * 2**20),
        cost_estimate=pl.CostEstimate(flops=flops, bytes_accessed=2**10, transcendentals=0),
    )(*tables, own, *sites)


def make_tables(p_cols, c_cols, cells_x, cells_y):
    total_x, total_y, blocks = p_cols.shape
    at_blk, at_row = lax.axis_index("blk"), lax.axis_index("rows")
    first, last = at_blk == 0, at_blk == lax.axis_size("blk") - 1
    near = [(x, y) for x in range(cells_x) for y in range(cells_y)]
    wide = [-1, -1, cells_x, cells_x]
    sides, side_y = list(range(cells_x)) * 2, [-1] * cells_x + [cells_y] * cells_x
    dx = [x for x, _ in near] + wide + [0] + sides + wide + [0]
    plain = [y for _, y in near] + [0, 1] * 2 + [2] + side_y + [-1, 2] * 2 + [1]
    turned = [y for _, y in near] + [-2, -1] * 2 + [2] + side_y + [-3, 0] * 2 + [1]
    dx, plain, turned = (np.array(v, np.int32) for v in (dx, plain, turned))
    numbers = np.arange(PIECES)
    is_wrap = (numbers == EARLY_WRAP) | (numbers == LATE_WRAP)
    dx = jnp.where(is_wrap, jnp.where(first, -1, cells_x), dx)
    swapped = ((dx < 0) & first) | ((dx >= cells_x) & last)
    dy = jnp.where(swapped, turned, plain)
    site_x = (at_blk * cells_x + dx + total_x) % total_x
    site_y = (at_row * cells_y + dy + total_y) % total_y
    ids = site_x * total_y + site_y
    cols = p_cols.reshape(total_x * total_y, blocks)[ids]
    ids = jnp.where(is_wrap & ~(first | last), -1, ids)
    own = cols[: cells_x * cells_y]
    slots = jnp.arange(blocks, dtype=jnp.int32)
    is_left = own[:, None, :] == ids[None, :, None]
    table_m = jnp.sum(jnp.where(is_left, slots, 0), axis=2)
    has_left = jnp.any(is_left, axis=2)
    targets = c_cols.reshape(cells_x * cells_y, -1)
    is_right = (cols[None, :, None, :] == targets[:, None, :, None]) & has_left[:, :, None, None]
    table_q = 8 + jnp.sum(jnp.where(is_right, slots - 8, 0), axis=3)
    return table_m.reshape(-1).astype(jnp.int32), table_q.reshape(-1).astype(jnp.int32)


def on_device(p_vals, p_cols, c_cols):
    cells_x, cells_y = p_vals.shape[:2]
    n_blk, n_rows = lax.axis_size("blk"), lax.axis_size("rows")
    last = cells_x - 1
    first = lax.axis_index("blk") == 0
    along_y = lambda value, shift: send(value, moves_y(shift, n_blk, n_rows), n_rows)
    along_x = lambda value, shift: send(value, moves_x(shift, n_blk, n_rows), n_rows)
    past_edge = lambda value: send(value, moves_wrap(n_blk, n_rows), n_rows)
    tie = lax.optimization_barrier

    rim_low = along_y(jnp.stack([p_vals[0, 1], p_vals[last, 1]]), 1)
    rim_high = along_y(jnp.stack([p_vals[0, 0], p_vals[last, 0]]), -1)

    edges, p_cols, c_cols = tie(((p_vals[last], p_vals[0]), p_cols, c_cols))
    tables = make_tables(p_cols, c_cols, cells_x, cells_y)
    single = jnp.where(first, edges[1][0], edges[0][0])
    early = [along_x(edges[0], 1), along_x(edges[1], -1), past_edge(single)]

    early, middle = tie((early, (p_vals[1:last, 1], p_vals[1:last, 0])))
    mid_low = along_y(middle[0], 1)
    mid_high = along_y(middle[1], -1)

    acc = run_kernel(first_kernel, tables, p_vals, early, 4 * 10**9)
    acc, rim_low, rim_high = tie((acc, rim_low, rim_high))
    single = jnp.where(first, rim_low[0], rim_low[1])
    late = [
        along_x(jnp.stack([rim_low[1], rim_high[1]]), 1),
        along_x(jnp.stack([rim_low[0], rim_high[0]]), -1),
        past_edge(single),
    ]
    acc = run_kernel(rim_kernel, tables, p_vals, [acc, rim_low, rim_high], 10**6)
    return run_kernel(last_kernel, tables, p_vals, [acc, mid_low, mid_high, *late], 10**6, last=True)


def solution(mesh):
    placed = (P("blk", "rows", None, None, None), P(), P("blk", "rows", None))
    return jax.shard_map(
        on_device,
        mesh=mesh,
        in_specs=placed,
        out_specs=P("blk", "rows", None, None, None),
        check_vma=False,
    )
```

time: 490 us -> 227 us (0.46)
  the two profiles are of different devices: /device:TPU:101 before, /device:TPU:24 now
where the time goes in v1:
time: 227 us
  waiting for transfers between devices  133 us (59%)
  starting transfers between devices  61.8 us (27%)
  Pallas kernels  18.2 us (8%)
  local copies, waits for them, and re-layouts  8.96 us (4%)
  other arithmetic  4.7 us (2%)
    ppermute x10, waiting for transfers between devices, send(): lax.ppermute(value, AXES, [(a[0] * n_rows + a[1], b[0] * n_rows + b[1]) f...  133 us
    ppermute x10, starting transfers between devices, send(): lax.ppermute(value, AXES, [(a[0] * n_rows + a[1], b[0] * n_rows + b[1]) f...  61.8 us
    pallas_call x3, Pallas kernels, run_kernel(): pl.pallas_call(body, out_shape=jax.ShapeDtypeStruct(shape, jnp.bfloat16 i...  18.2 us
  transfers between devices with their start and end apart: 10, of which 2 were waited for; matrix products, arithmetic and copies ran while one was open for 5% of the time, Pallas kernels for 6%

profile of v1, /device:TPU:24, one launch (start us, length us, event | category | flops | bytes accessed | tf_op | source)
XLA Modules:
  0.0 226.6 jit_solution(9314267633062544368)
XLA Ops:
  0.0 1.4 slice_bitcast_fusion.5
  1.4 0.8 pad_maximum_fusion
  2.3 15.9 %collective-permute-start.3 = (bf16[2,8,128,128]{3,2,1,0:T(8,128)(2,1)}, bf16[2,8,128,128]{3,2,1,0:T(8,128)(2,1)S(1)}, u32[]{:S(2)}, u32[]{:S(2)}) collective-permute-start(bf16[2,8,128,128]{3,2,1,0:T(8,128)(2,1)} %pad_maximum_fusion), channel_id=1, source_target_pairs={{0,1},{1,2},{2,3},{3,4},{4,5},{5,6},{6,7},{7,8},{8,9},{9,10},{10,1... | collective-permute-start | bytes 1572872 | tf_op jit(solution)/shard_map/ppermute | solution.py:16
  18.2 0.8 pad_maximum_fusion.1
  19.0 4.3 %collective-permute-start.4 = (bf16[2,8,128,128]{3,2,1,0:T(8,128)(2,1)}, bf16[2,8,128,128]{3,2,1,0:T(8,128)(2,1)S(1)}, u32[]{:S(2)}, u32[]{:S(2)}) collective-permute-start(bf16[2,8,128,128]{3,2,1,0:T(8,128)(2,1)} %pad_maximum_fusion.1), channel_id=1, source_target_pairs={{0,31},{1,0},{2,1},{3,2},{4,3},{5,4},{6,5},{7,6},{8,7},{9,8},{10,9... | collective-permute-start | bytes 1572872 | tf_op jit(solution)/shard_map/ppermute | solution.py:16
  23.3 1.1 slice_bitcast_fusion.2
  24.4 2.0 collective-permute-start
  26.5 4.8 %collective-permute-start.1 = (bf16[2,8,128,128]{3,2,1,0:T(8,128)(2,1)}, bf16[2,8,128,128]{3,2,1,0:T(8,128)(2,1)}, u32[]{:S(2)}, u32[]{:S(2)}) collective-permute-start(bf16[2,8,128,128]{3,2,1,0:T(8,128)(2,1)} %get-tuple-element.20), channel_id=1, source_target_pairs={{0,481},{1,482},{2,483},{3,484},{4,485},{5,486},{6,487},{7,488},{8... | collective-permute-start | bytes 1572872 | tf_op jit(solution)/shard_map/ppermute | solution.py:16
  31.3 1.8 select_bitcast_fusion.1
  33.1 5.5 %collective-permute-start.2 = (bf16[8,128,128]{2,1,0:T(8,128)(2,1)}, bf16[8,128,128]{2,1,0:T(8,128)(2,1)S(1)}, u32[]{:S(2)}, u32[]{:S(2)}) collective-permute-start(bf16[8,128,128]{2,1,0:T(8,128)(2,1)} %select_bitcast_fusion.1), channel_id=1, source_target_pairs={{480,31},{481,0},{482,1},{483,2},{484,3},{485,4},{486,5},{487,6},{... | collective-permute-start | bytes 786440 | tf_op jit(solution)/shard_map/ppermute | solution.py:16
  38.7 2.9 %copy.19 = s32[64,64,8]{2,1,0:T(8,128)} copy(s32[64,64,8]{1,2,0:T(8,128)} %param.8) | data formatting | bytes 262144 | tf_op jit(solution)/shard_map/optimization_barrier | solution.py:186
  41.6 2.2 gather_fusion
  43.8 0.1 copy.20
  43.8 0.1 compare_reduce_fusion
  43.9 0.2 select_reduce_fusion
  44.2 0.1 fusion
  44.3 0.1 reshape.20.table_m
  44.4 0.6 copy_add_fusion
  45.0 0.9 copy.22
  45.9 0.1 add.57.table_q
  46.0 0.1 slice_bitcast_fusion
  46.2 71.1 %collective-permute-done.2.wrap = bf16[8,128,128]{2,1,0:T(8,128)(2,1)S(1)} collective-permute-done((bf16[8,128,128]{2,1,0:T(8,128)(2,1)}, bf16[8,128,128]{2,1,0:T(8,128)(2,1)S(1)}, u32[]{:S(2)}, u32[]{:S(2)}) %collective-permute-start.2) | collective-permute-done | bytes 262176 | tf_op jit(solution)/shard_map/ppermute | solution.py:16
  117.2 9.6 %collective-permute-start.5 = (bf16[2,8,128,128]{3,2,1,0:T(8,128)(2,1)S(1)}, bf16[2,8,128,128]{3,2,1,0:T(8,128)(2,1)S(1)}, u32[]{:S(2)}, u32[]{:S(2)}) collective-permute-start(bf16[2,8,128,128]{3,2,1,0:T(8,128)(2,1)S(1)} %get-tuple-element.27), channel_id=1, source_target_pairs={{0,1},{1,2},{2,3},{3,4},{4,5},{5,6},{6,7},{7,8},{8,9},{9,10},{10,1... | collective-permute-start | bytes 1572872 | tf_op jit(solution)/shard_map/ppermute | solution.py:16
  126.8 8.0 %collective-permute-start.6 = (bf16[2,8,128,128]{3,2,1,0:T(8,128)(2,1)S(1)}, bf16[2,8,128,128]{3,2,1,0:T(8,128)(2,1)S(1)}, u32[]{:S(2)}, u32[]{:S(2)}) collective-permute-start(bf16[2,8,128,128]{3,2,1,0:T(8,128)(2,1)S(1)} %get-tuple-element.28), channel_id=1, source_target_pairs={{0,31},{1,0},{2,1},{3,2},{4,3},{5,4},{6,5},{7,6},{8,7},{9,8},{10,9... | collective-permute-start | bytes 1572872 | tf_op jit(solution)/shard_map/ppermute | solution.py:16
  134.8 9.2 %shard_map.73.acc = f32[4,2,12,128,128]{4,3,2,1,0:T(8,128)S(1)} custom-call(s32[208]{0:T(256)S(1)} %reshape.20.table_m, s32[2496]{0:T(1024)S(1)} %add.57.table_q, bf16[4,2,8,128,128]{4,3,2,1,0:T(8,128)(2,1)S(1)} %copy-done, bf16[2,8,128,128]{3,2,1,0:T(8,128)(2,1)} %collective-permute-done.up, bf16[2,8,128,128]{3,2,1,0:T(8,128)(2,1)} %collective-permute-done.1.down, ...), custom_call_target="tpu_custom_call" | custom-call | flops 4000000000 | bytes 1024 | tf_op jit(solution)/shard_map/pallas_call | solution.py:129
  144.1 0.1 select_bitcast_fusion
  144.2 1.9 collective-permute-start.7
  146.2 3.7 %collective-permute-start.8 = (bf16[2,8,128,128]{3,2,1,0:T(8,128)(2,1)S(1)}, bf16[2,8,128,128]{3,2,1,0:T(8,128)(2,1)S(1)}, u32[]{:S(2)}, u32[]{:S(2)}) collective-permute-start(bf16[2,8,128,128]{3,2,1,0:T(8,128)(2,1)S(1)} %pad_maximum_fusion.3), channel_id=1, source_target_pairs={{0,481},{1,482},{2,483},{3,484},{4,485},{5,486},{6,487},{7,488},{8... | collective-permute-start | bytes 1572872 | tf_op jit(solution)/shard_map/ppermute | solution.py:16
  149.9 6.1 %collective-permute-start.9 = (bf16[8,128,128]{2,1,0:T(8,128)(2,1)S(1)}, bf16[8,128,128]{2,1,0:T(8,128)(2,1)S(1)}, u32[]{:S(2)}, u32[]{:S(2)}) collective-permute-start(bf16[8,128,128]{2,1,0:T(8,128)(2,1)S(1)} %get-tuple-element.39), channel_id=1, source_target_pairs={{480,31},{481,0},{482,1},{483,2},{484,3},{485,4},{486,5},{487,6},{... | collective-permute-start | bytes 786440 | tf_op jit(solution)/shard_map/ppermute | solution.py:16
  156.0 5.2 %shard_map.74.acc = f32[4,2,12,128,128]{4,3,2,1,0:T(8,128)S(1)} custom-call(s32[208]{0:T(256)S(1)} %reshape.20.table_m, s32[2496]{0:T(1024)S(1)} %add.57.table_q, bf16[4,2,8,128,128]{4,3,2,1,0:T(8,128)(2,1)S(1)} %copy-done, f32[4,2,12,128,128]{4,3,2,1,0:T(8,128)S(1)} %shard_map.73.acc, bf16[2,8,128,128]{3,2,1,0:T(8,128)(2,1)S(1)} %collective-permute-done.3.rim_low, ...), custom_call_target="tpu_custom_call" | custom-call | flops 1000000 | bytes 1024 | tf_op jit(solution)/shard_map/pallas_call | solution.py:129
  161.2 61.5 %collective-permute-done.9.wrap = bf16[8,128,128]{2,1,0:T(8,128)(2,1)S(1)} collective-permute-done((bf16[8,128,128]{2,1,0:T(8,128)(2,1)S(1)}, bf16[8,128,128]{2,1,0:T(8,128)(2,1)S(1)}, u32[]{:S(2)}, u32[]{:S(2)}) %collective-permute-start.9) | collective-permute-done | bytes 262176 | tf_op jit(solution)/shard_map/ppermute | solution.py:16
  222.7 3.8 %shard_map.75 = bf16[4,2,12,128,128]{4,3,2,1,0:T(8,128)(2,1)} custom-call(s32[208]{0:T(256)S(1)} %reshape.20.table_m, s32[2496]{0:T(1024)S(1)} %add.57.table_q, bf16[4,2,8,128,128]{4,3,2,1,0:T(8,128)(2,1)S(1)} %copy-done, f32[4,2,12,128,128]{4,3,2,1,0:T(8,128)S(1)} %shard_map.74.acc, bf16[2,8,128,128]{3,2,1,0:T(8,128)(2,1)S(1)} %collective-permute-done.5.mid_low, ...), custom_call_target="tpu_custom_call" | custom-call | flops 1000000 | bytes 1024 | tf_op jit(solution)/shard_map/pallas_call | solution.py:129
  (28 shorter events, 0.2 us)
Async XLA Ops:
  0.0 23.3 %copy-start = (bf16[4,2,8,128,128]{4,3,2,1,0:T(8,128)(2,1)S(1)}, bf16[4,2,8,128,128]{4,3,2,1,0:T(8,128)(2,1)}, u32[]{:S(2)}) copy-start(bf16[4,2,8,128,128]{4,3,2,1,0:T(8,128)(2,1)} %own.5) | copy-start | bytes 6291460
  2.3 36.3 %copy-start.2 = (pred[26]{0:T(512)(128)(4,1)S(1)}, pred[26]{0:T(512)(128)(4,1)}, u32[]{:S(2)}) copy-start(pred[26]{0:T(512)(128)(4,1)} %constant.58.clone) | copy-start | bytes 82
  2.3 36.3 %copy-start.3 = (s32[26]{0:T(128)S(1)}, s32[26]{0:T(128)}, u32[]{:S(2)}) copy-start(s32[26]{0:T(128)} %constant.61.clone) | copy-start | bytes 316
  2.3 36.3 %copy-start.4 = (s32[26]{0:T(128)S(1)}, s32[26]{0:T(128)}, u32[]{:S(2)}) copy-start(s32[26]{0:T(128)} %constant.60.clone) | copy-start | bytes 316
  2.3 36.3 %copy-start.5 = (s32[26]{0:T(128)S(1)}, s32[26]{0:T(128)}, u32[]{:S(2)}) copy-start(s32[26]{0:T(128)} %constant.59.clone) | copy-start | bytes 316
  2.3 141.7 %collective-permute-start.3 = (bf16[2,8,128,128]{3,2,1,0:T(8,128)(2,1)}, bf16[2,8,128,128]{3,2,1,0:T(8,128)(2,1)S(1)}, u32[]{:S(2)}, u32[]{:S(2)}) collective-permute-start(bf16[2,8,128,128]{3,2,1,0:T(8,128)(2,1)} %pad_maximum_fusion), channel_id=1, source_target_pairs={{0,1},{1,2},{2,3},{3,4},{4,5},{5,6},{6,7},{7,8},{8,9},{9,10},{10,1... | collective-permute-start | bytes 1572872 | tf_op jit(solution)/shard_map/ppermute | solution.py:16
  19.0 125.0 %collective-permute-start.4 = (bf16[2,8,128,128]{3,2,1,0:T(8,128)(2,1)}, bf16[2,8,128,128]{3,2,1,0:T(8,128)(2,1)S(1)}, u32[]{:S(2)}, u32[]{:S(2)}) collective-permute-start(bf16[2,8,128,128]{3,2,1,0:T(8,128)(2,1)} %pad_maximum_fusion.1), channel_id=1, source_target_pairs={{0,31},{1,0},{2,1},{3,2},{4,3},{5,4},{6,5},{7,6},{8,7},{9,8},{10,9... | collective-permute-start | bytes 1572872 | tf_op jit(solution)/shard_map/ppermute | solution.py:16
  24.4 19.5 %copy-start.1 = (s32[4,2,12]{2,1,0:T(2,128)S(1)}, s32[4,2,12]{2,1,0:T(2,128)}, u32[]{:S(2)}) copy-start(s32[4,2,12]{2,1,0:T(2,128)} %param.9) | copy-start | bytes 1156
  24.4 92.8 %collective-permute-start = (bf16[2,8,128,128]{3,2,1,0:T(8,128)(2,1)}, bf16[2,8,128,128]{3,2,1,0:T(8,128)(2,1)}, u32[]{:S(2)}, u32[]{:S(2)}) collective-permute-start(bf16[2,8,128,128]{3,2,1,0:T(8,128)(2,1)} %get-tuple-element.19), channel_id=1, source_target_pairs={{0,32},{1,33},{2,34},{3,35},{4,36},{5,37},{6,38},{7,39},{8,40},{9,... | collective-permute-start | bytes 1572872 | tf_op jit(solution)/shard_map/ppermute | solution.py:16
  26.5 90.8 %collective-permute-start.1 = (bf16[2,8,128,128]{3,2,1,0:T(8,128)(2,1)}, bf16[2,8,128,128]{3,2,1,0:T(8,128)(2,1)}, u32[]{:S(2)}, u32[]{:S(2)}) collective-permute-start(bf16[2,8,128,128]{3,2,1,0:T(8,128)(2,1)} %get-tuple-element.20), channel_id=1, source_target_pairs={{0,481},{1,482},{2,483},{3,484},{4,485},{5,486},{6,487},{7,488},{8... | collective-permute-start | bytes 1572872 | tf_op jit(solution)/shard_map/ppermute | solution.py:16
  33.1 84.2 %collective-permute-start.2 = (bf16[8,128,128]{2,1,0:T(8,128)(2,1)}, bf16[8,128,128]{2,1,0:T(8,128)(2,1)S(1)}, u32[]{:S(2)}, u32[]{:S(2)}) collective-permute-start(bf16[8,128,128]{2,1,0:T(8,128)(2,1)} %select_bitcast_fusion.1), channel_id=1, source_target_pairs={{480,31},{481,0},{482,1},{483,2},{484,3},{485,4},{486,5},{487,6},{... | collective-permute-start | bytes 786440 | tf_op jit(solution)/shard_map/ppermute | solution.py:16
  117.2 105.5 %collective-permute-start.5 = (bf16[2,8,128,128]{3,2,1,0:T(8,128)(2,1)S(1)}, bf16[2,8,128,128]{3,2,1,0:T(8,128)(2,1)S(1)}, u32[]{:S(2)}, u32[]{:S(2)}) collective-permute-start(bf16[2,8,128,128]{3,2,1,0:T(8,128)(2,1)S(1)} %get-tuple-element.27), channel_id=1, source_target_pairs={{0,1},{1,2},{2,3},{3,4},{4,5},{5,6},{6,7},{7,8},{8,9},{9,10},{10,1... | collective-permute-start | bytes 1572872 | tf_op jit(solution)/shard_map/ppermute | solution.py:16
  126.8 95.9 %collective-permute-start.6 = (bf16[2,8,128,128]{3,2,1,0:T(8,128)(2,1)S(1)}, bf16[2,8,128,128]{3,2,1,0:T(8,128)(2,1)S(1)}, u32[]{:S(2)}, u32[]{:S(2)}) collective-permute-start(bf16[2,8,128,128]{3,2,1,0:T(8,128)(2,1)S(1)} %get-tuple-element.28), channel_id=1, source_target_pairs={{0,31},{1,0},{2,1},{3,2},{4,3},{5,4},{6,5},{7,6},{8,7},{9,8},{10,9... | collective-permute-start | bytes 1572872 | tf_op jit(solution)/shard_map/ppermute | solution.py:16
  144.2 78.5 %collective-permute-start.7 = (bf16[2,8,128,128]{3,2,1,0:T(8,128)(2,1)S(1)}, bf16[2,8,128,128]{3,2,1,0:T(8,128)(2,1)S(1)}, u32[]{:S(2)}, u32[]{:S(2)}) collective-permute-start(bf16[2,8,128,128]{3,2,1,0:T(8,128)(2,1)S(1)} %pad_maximum_fusion.2), channel_id=1, source_target_pairs={{0,32},{1,33},{2,34},{3,35},{4,36},{5,37},{6,38},{7,39},{8,40},{9,... | collective-permute-start | bytes 1572872 | tf_op jit(solution)/shard_map/ppermute | solution.py:16
  146.2 76.5 %collective-permute-start.8 = (bf16[2,8,128,128]{3,2,1,0:T(8,128)(2,1)S(1)}, bf16[2,8,128,128]{3,2,1,0:T(8,128)(2,1)S(1)}, u32[]{:S(2)}, u32[]{:S(2)}) collective-permute-start(bf16[2,8,128,128]{3,2,1,0:T(8,128)(2,1)S(1)} %pad_maximum_fusion.3), channel_id=1, source_target_pairs={{0,481},{1,482},{2,483},{3,484},{4,485},{5,486},{6,487},{7,488},{8... | collective-permute-start | bytes 1572872 | tf_op jit(solution)/shard_map/ppermute | solution.py:16
  149.9 72.8 %collective-permute-start.9 = (bf16[8,128,128]{2,1,0:T(8,128)(2,1)S(1)}, bf16[8,128,128]{2,1,0:T(8,128)(2,1)S(1)}, u32[]{:S(2)}, u32[]{:S(2)}) collective-permute-start(bf16[8,128,128]{2,1,0:T(8,128)(2,1)S(1)} %get-tuple-element.39), channel_id=1, source_target_pairs={{480,31},{481,0},{482,1},{483,2},{484,3},{485,4},{486,5},{487,6},{... | collective-permute-start | bytes 786440 | tf_op jit(solution)/shard_map/ppermute | solution.py:16

commit v2 on v1

v2 whole, which is shorter than its diff:
```python
import jax
import jax.numpy as jnp
import numpy as np
from jax import lax
from jax.experimental import pallas as pl
from jax.experimental.pallas import tpu as pltpu
from jax.sharding import PartitionSpec as P

AXES = ("blk", "rows")
OWN, SIDE_LOW, SIDE_HIGH, NEAR_LOW, NEAR_HIGH, WRAP, PIECES = 0, 8, 12, 16, 20, 24, 26
BLOCKS = (12, 128, 128)


def send(value, moves, n_rows):
    return lax.ppermute(value, AXES, [(a[0] * n_rows + a[1], b[0] * n_rows + b[1]) for a, b in moves])


def moves_y(shift, n_blk, n_rows):
    return [((b, r), (b, (r + shift) % n_rows)) for b in range(n_blk) for r in range(n_rows)]


def moves_x(shift, n_blk, n_rows):
    moves = []
    for b in range(n_blk):
        for r in range(n_rows):
            inside = 0 <= b + shift < n_blk
            moves.append(((b, r), ((b + shift) % n_blk, r if inside else (r + 1) % n_rows)))
    return moves


def moves_wrap(n_blk, n_rows):
    edges = ((n_blk - 1, 0), (0, n_blk - 1))
    return [((b, r), (to, (r - 1) % n_rows)) for b, to in edges for r in range(n_rows)]


def accumulate(table_m, table_q, own, x, col, pieces, write, unroll):
    site = x * 2 + col
    left = jnp.concatenate([own[x, col, table_m[site * PIECES + number]] for number, _ in pieces], axis=1)

    def pair(h, carry):
        halves = []
        for n in (2 * h, 2 * h + 1):
            rows = []
            for number, block_of in pieces:
                q = table_q[(site * PIECES + number) * 12 + n]
                block = block_of(jnp.minimum(q, 7))
                rows.append(jnp.where(q < 8, block, jnp.zeros_like(block)))
            halves.append(jnp.concatenate(rows, axis=0))
        right = jnp.concatenate(halves, axis=1)
        total = jnp.dot(left, right, preferred_element_type=jnp.float32)
        write(x, col, 2 * h, total[:, :128])
        write(x, col, 2 * h + 1, total[:, 128:])
        return carry

    lax.fori_loop(0, 6, pair, 0, unroll=unroll)


def block_from(ref, *lead):
    return lambda q: ref[(*lead, q)]


def every_site(tables, own, pieces_of, write):
    for x in range(own.shape[0]):
        for col in range(2):
            accumulate(*tables, own, x, col, pieces_of(x, col), write, 2)


def column_kernel(table_m, table_q, own, acc):
    def pieces_of(x, col):
        return [(OWN + x * 2 + y, block_from(own, x, y)) for y in range(2)]

    def write(x, col, n, total):
        acc[x, col, n] = total

    every_site((table_m, table_q), own, pieces_of, write)


def own_kernel(table_m, table_q, own, acc, out):
    def pieces_of(x, col):
        around = [near for near in (x - 1, x + 1) if 0 <= near < own.shape[0]]
        return [(OWN + near * 2 + y, block_from(own, near, y)) for near in around for y in range(2)]

    def write(x, col, n, total):
        out[x, col, n] = acc[x, col, n] + total

    every_site((table_m, table_q), own, pieces_of, write)


def rim_kernel(table_m, table_q, own, acc, rim_low, rim_high, out):
    cells_x = own.shape[0]
    rims = (rim_low, rim_high)

    def pieces_of(x, col):
        at = int(x >= cells_x // 2)
        return [((SIDE_LOW, SIDE_HIGH)[col] + at * (cells_x - 1), block_from(rims[col], at))]

    def write(x, col, n, total):
        out[x, col, n] = acc[x, col, n] + total

    every_site((table_m, table_q), own, pieces_of, write)


def middle_kernel(table_m, table_q, own, acc, mid_low, mid_high, out, rest, held, sems):
    cells_x = own.shape[0]
    mids = (mid_low, mid_high)

    def write(x, col, n, total):
        if 0 < x < cells_x - 1:
            held[x - 1, col, n] = (acc[x, col, n] + total).astype(jnp.bfloat16)
        else:
            rest[int(x > 0), col, n] = acc[x, col, n] + total

    copies = []
    for x in (1, 2, 0, 3):
        for col in range(2):
            first = (SIDE_LOW, SIDE_HIGH)[col]
            pieces = [
                (first + near, block_from(mids[col], near - 1))
                for near in (x - 1, x, x + 1)
                if 0 < near < cells_x - 1
            ]
            accumulate(table_m, table_q, own, x, col, pieces, write, 6)
            if 0 < x < cells_x - 1:
                copies.append(pltpu.make_async_copy(held.at[x - 1, col], out.at[x, col], sems.at[x - 1, col]))
                copies[-1].start()
    for copy in copies:
        copy.wait()


def edge_kernel(table_m, table_q, own, rest, near_low, near_high, wrap, begun, out, held, sems):
    cells_x = own.shape[0]

    def write(x, col, n, total):
        at = int(x > 0)
        held[at, col, n] = (rest[at, col, n] + total).astype(jnp.bfloat16)

    copies = []
    for at, x in enumerate((0, cells_x - 1)):
        first, near = ((NEAR_LOW, near_low), (NEAR_HIGH, near_high))[at]
        for col in range(2):
            pieces = [(first + y, block_from(near, y)) for y in range(4)]
            pieces += [(WRAP + y, block_from(wrap, y)) for y in range(2)]
            accumulate(table_m, table_q, own, x, col, pieces, write, 6)
            copies.append(pltpu.make_async_copy(held.at[at, col], out.at[x, col], sems.at[at, col]))
            copies[-1].start()
    for copy in copies:
        copy.wait()


def run_kernel(body, tables, own, sites, flops, begun=None, middle=False):
    whole, half = ((count, 2) + BLOCKS for count in (own.shape[0], 2))
    in_vmem, in_hbm = pl.BlockSpec(memory_space=pltpu.VMEM), pl.BlockSpec(memory_space=pl.ANY)
    out_shape, out_specs = jax.ShapeDtypeStruct(whole, jnp.float32), in_vmem
    in_specs = [pl.BlockSpec(memory_space=pltpu.SMEM)] * 2 + [in_vmem] * (1 + len(sites))
    held, aliases = [], {}
    if middle or begun is not None:
        out_shape, out_specs = jax.ShapeDtypeStruct(whole, jnp.bfloat16), in_hbm
        held = [pltpu.VMEM(half, jnp.bfloat16), pltpu.SemaphoreType.DMA((2, 2))]
    if middle:
        out_shape, out_specs = (out_shape, jax.ShapeDtypeStruct(half, jnp.float32)), (out_specs, in_vmem)
    if begun is not None:
        aliases = {len(in_specs): 0}
        in_specs, sites = in_specs + [in_hbm], [*sites, begun]
    return pl.pallas_call(
        body,
        out_shape=out_shape,
        in_specs=in_specs,
        out_specs=out_specs,
        scratch_shapes=held,
        input_output_aliases=aliases,
        compiler_params=pltpu.CompilerParams(vmem_limit_bytes=32 * 2**20),
        cost_estimate=pl.CostEstimate(flops=flops, bytes_accessed=2**10, transcendentals=0),
    )(*tables, own, *sites)


def make_tables(p_cols, c_cols, cells_x, cells_y):
    total_x, total_y, blocks = p_cols.shape
    at_blk, at_row = lax.axis_index("blk"), lax.axis_index("rows")
    first, last = at_blk == 0, at_blk == lax.axis_size("blk") - 1
    near = [(x, y) for x in range(cells_x) for y in range(cells_y)]
    wide = [-1] * 4 + [cells_x] * 4
    sides, side_y = list(range(cells_x)) * 2, [-1] * cells_x + [cells_y] * cells_x
    dx = [x for x, _ in near] + sides + wide + [0, 0]
    plain = [y for _, y in near] + side_y + [0, 1, -1, 2] * 2 + [2, 1]
    turned = [y for _, y in near] + side_y + [-2, -1, -3, 0] * 2 + [2, 1]
    dx, plain, turned = (np.array(v, np.int32) for v in (dx, plain, turned))
    is_wrap = np.arange(PIECES) >= WRAP
    dx = jnp.where(is_wrap, jnp.where(first, -1, cells_x), dx)
    swapped = ((dx < 0) & first) | ((dx >= cells_x) & last)
    dy = jnp.where(swapped, turned, plain)
    site_x = (at_blk * cells_x + dx + total_x) % total_x
    site_y = (at_row * cells_y + dy + total_y) % total_y
    ids = site_x * total_y + site_y
    cols = p_cols.reshape(total_x * total_y, blocks)[ids]
    ids = jnp.where(is_wrap & ~(first | last), -1, ids)
    own = cols[: cells_x * cells_y]
    slots = jnp.arange(blocks, dtype=jnp.int32)
    is_left = own[:, None, :] == ids[None, :, None]
    table_m = jnp.sum(jnp.where(is_left, slots, 0), axis=2)
    has_left = jnp.any(is_left, axis=2)
    targets = c_cols.reshape(cells_x * cells_y, -1)
    is_right = (cols[None, :, None, :] == targets[:, None, :, None]) & has_left[:, :, None, None]
    table_q = 8 + jnp.sum(jnp.where(is_right, slots - 8, 0), axis=3)
    return table_m.reshape(-1).astype(jnp.int32), table_q.reshape(-1).astype(jnp.int32)


def on_device(p_vals, p_cols, c_cols):
    cells_x, cells_y = p_vals.shape[:2]
    n_blk, n_rows = lax.axis_size("blk"), lax.axis_size("rows")
    last = cells_x - 1
    first = lax.axis_index("blk") == 0
    along_y = lambda value, shift: send(value, moves_y(shift, n_blk, n_rows), n_rows)
    along_x = lambda value, shift: send(value, moves_x(shift, n_blk, n_rows), n_rows)
    past_edge = lambda value: send(value, moves_wrap(n_blk, n_rows), n_rows)
    tie = lax.optimization_barrier

    rim_low = along_y(jnp.stack([p_vals[0, 1], p_vals[last, 1]]), 1)
    rim_high = along_y(jnp.stack([p_vals[0, 0], p_vals[last, 0]]), -1)

    tables = make_tables(p_cols, c_cols, cells_x, cells_y)
    acc = run_kernel(column_kernel, tables, p_vals, [], 4 * 10**9)
    acc, middle = tie((acc, (p_vals[1:last, 1], p_vals[1:last, 0])))
    mid_low = along_y(middle[0], 1)
    mid_high = along_y(middle[1], -1)

    acc = run_kernel(own_kernel, tables, p_vals, [acc], 4 * 10**9)
    acc, rim_low, rim_high = tie((acc, rim_low, rim_high))
    below = jnp.stack([p_vals[0, 0], p_vals[0, 1], rim_low[0], rim_high[0]])
    above = jnp.stack([p_vals[last, 0], p_vals[last, 1], rim_low[1], rim_high[1]])
    pair = jnp.where(first, below[0:3:2], above[0:3:2])
    near = [along_x(above, 1), along_x(below, -1), past_edge(pair)]

    acc = run_kernel(rim_kernel, tables, p_vals, [acc, rim_low, rim_high], 10**6)
    begun, rest = run_kernel(middle_kernel, tables, p_vals, [acc, mid_low, mid_high], 5 * 10**10, middle=True)
    return run_kernel(edge_kernel, tables, p_vals, [rest, *near], 10**6, begun=begun)


def solution(mesh):
    placed = (P("blk", "rows", None, None, None), P(), P("blk", "rows", None))
    return jax.shard_map(
        on_device,
        mesh=mesh,
        in_specs=placed,
        out_specs=P("blk", "rows", None, None, None),
        check_vma=False,
    )
```

time: 227 us -> 220 us (0.969)
  waiting for transfers between devices: 133 us -> 58.7 us
  starting transfers between devices: 61.8 us -> 126 us
  Pallas kernels: 18.2 us -> 23.4 us
    ppermute x10 -> x7, waiting for transfers between devices: 133 us -> 58.7 us  [send(): lax.ppermute(value, AXES, [(a[0] * n_rows + a[1], b[0] * n_rows + b[1]) f...]
    ppermute x10 -> x7, starting transfers between devices: 61.8 us -> 126 us  [send(): lax.ppermute(value, AXES, [(a[0] * n_rows + a[1], b[0] * n_rows + b[1]) f...]
    pallas_call x3 -> x5, Pallas kernels: 18.2 us -> 23.4 us  [run_kernel(): pl.pallas_call(body, out_shape=out_shape, in_specs=in_specs, out_specs=ou...]
    unnamed x12 -> x25, local copies, waits for them, and re-layouts: 0.02 us -> 3.75 us
    optimization_barrier x1 -> x0, local copies, waits for them, and re-layouts: 2.9 us -> none  [on_device(): edges, p_cols, c_cols = tie(((p_vals[last], p_vals[0]), p_cols, c_cols))]
  transfers between devices with their start and end apart: 10 -> 7, of which waited for: 2 -> 1; matrix products, arithmetic and copies ran while one was open for 5% -> 4% of each run, Pallas kernels for 6% -> 9%
where the time goes in v2:
time: 220 us
  starting transfers between devices  126 us (57%)
  waiting for transfers between devices  58.7 us (27%)
  Pallas kernels  23.4 us (11%)
  local copies, waits for them, and re-layouts  8.75 us (4%)
  other arithmetic  3.11 us (1%)
    ppermute x7, starting transfers between devices, send(): lax.ppermute(value, AXES, [(a[0] * n_rows + a[1], b[0] * n_rows + b[1]) f...  126 us
    ppermute x7, waiting for transfers between devices, send(): lax.ppermute(value, AXES, [(a[0] * n_rows + a[1], b[0] * n_rows + b[1]) f...  58.7 us
    pallas_call x5, Pallas kernels, run_kernel(): pl.pallas_call(body, out_shape=out_shape, in_specs=in_specs, out_specs=ou...  23.4 us
  transfers between devices with their start and end apart: 7, of which 1 were waited for; matrix products, arithmetic and copies ran while one was open for 4% of the time, Pallas kernels for 9%

profile of v2, /device:TPU:24, one launch (start us, length us, event | category | flops | bytes accessed | tf_op | source)
XLA Modules:
  0.0 219.9 jit_solution(10026614624169479149)
XLA Ops:
  0.0 1.4 slice_bitcast_fusion.3
  1.5 0.7 copy-done.1
  2.2 0.1 copy-done.5
  2.3 0.8 pad_maximum_fusion.2
  3.2 15.7 %collective-permute-start = (bf16[2,8,128,128]{3,2,1,0:T(8,128)(2,1)}, bf16[2,8,128,128]{3,2,1,0:T(8,128)(2,1)S(1)}, u32[]{:S(2)}, u32[]{:S(2)}) collective-permute-start(bf16[2,8,128,128]{3,2,1,0:T(8,128)(2,1)} %pad_maximum_fusion.2), channel_id=1, source_target_pairs={{0,1},{1,2},{2,3},{3,4},{4,5},{5,6},{6,7},{7,8},{8,9},{9,10},{10,1... | collective-permute-start | bytes 1572872 | tf_op jit(solution)/shard_map/ppermute | solution.py:15
  18.9 0.8 pad_maximum_fusion.3
  19.7 4.3 %collective-permute-start.1 = (bf16[2,8,128,128]{3,2,1,0:T(8,128)(2,1)}, bf16[2,8,128,128]{3,2,1,0:T(8,128)(2,1)S(1)}, u32[]{:S(2)}, u32[]{:S(2)}) collective-permute-start(bf16[2,8,128,128]{3,2,1,0:T(8,128)(2,1)} %pad_maximum_fusion.3), channel_id=1, source_target_pairs={{0,31},{1,0},{2,1},{3,2},{4,3},{5,4},{6,5},{7,6},{8,7},{9,8},{10,9... | collective-permute-start | bytes 1572872 | tf_op jit(solution)/shard_map/ppermute | solution.py:15
  24.1 2.9 %copy.20 = s32[64,64,8]{2,1,0:T(8,128)} copy(s32[64,64,8]{1,2,0:T(8,128)} %param.8) | data formatting | bytes 262144 | tf_op args[1]
  27.0 2.2 gather_fusion
  29.2 0.1 copy.21
  29.3 0.1 fusion
  29.4 0.1 compare_reduce_fusion
  29.5 0.1 reshape.16.table_m
  29.5 0.2 select_reduce_fusion
  29.8 0.6 copy_add_fusion
  30.4 0.9 copy.23
  31.4 0.1 add.57.table_q
  31.5 5.6 %shard_map.73.acc = f32[4,2,12,128,128]{4,3,2,1,0:T(8,128)S(1)} custom-call(s32[208]{0:T(256)S(1)} %reshape.16.table_m, s32[2496]{0:T(1024)S(1)} %add.57.table_q, bf16[4,2,8,128,128]{4,3,2,1,0:T(8,128)(2,1)S(1)} %copy-done), custom_call_target="tpu_custom_call" | custom-call | flops 4000000000 | bytes 1024 | tf_op jit(solution)/shard_map/pallas_call | solution.py:164
  37.1 0.1 slice_bitcast_fusion
  37.3 10.4 %collective-permute-start.2 = (bf16[2,8,128,128]{3,2,1,0:T(8,128)(2,1)S(1)}, bf16[2,8,128,128]{3,2,1,0:T(8,128)(2,1)S(1)}, u32[]{:S(2)}, u32[]{:S(2)}) collective-permute-start(bf16[2,8,128,128]{3,2,1,0:T(8,128)(2,1)S(1)} %get-tuple-element.17), channel_id=1, source_target_pairs={{0,1},{1,2},{2,3},{3,4},{4,5},{5,6},{6,7},{7,8},{8,9},{9,10},{10,1... | collective-permute-start | bytes 1572872 | tf_op jit(solution)/shard_map/ppermute | solution.py:15
  47.7 7.3 %collective-permute-start.3 = (bf16[2,8,128,128]{3,2,1,0:T(8,128)(2,1)S(1)}, bf16[2,8,128,128]{3,2,1,0:T(8,128)(2,1)S(1)}, u32[]{:S(2)}, u32[]{:S(2)}) collective-permute-start(bf16[2,8,128,128]{3,2,1,0:T(8,128)(2,1)S(1)} %get-tuple-element.18), channel_id=1, source_target_pairs={{0,31},{1,0},{2,1},{3,2},{4,3},{5,4},{6,5},{7,6},{8,7},{9,8},{10,9... | collective-permute-start | bytes 1572872 | tf_op jit(solution)/shard_map/ppermute | solution.py:15
  55.0 6.4 %shard_map.74.acc = f32[4,2,12,128,128]{4,3,2,1,0:T(8,128)S(1)} custom-call(s32[208]{0:T(256)S(1)} %reshape.16.table_m, s32[2496]{0:T(1024)S(1)} %add.57.table_q, bf16[4,2,8,128,128]{4,3,2,1,0:T(8,128)(2,1)S(1)} %copy-done, f32[4,2,12,128,128]{4,3,2,1,0:T(8,128)S(1)} %shard_map.73.acc), custom_call_target="tpu_custom_call" | custom-call | flops 4000000000 | bytes 1024 | tf_op jit(solution)/shard_map/pallas_call | solution.py:164
  61.4 0.1 fusion.7
  61.5 0.1 pad_maximum_fusion
  61.6 1.9 collective-permute-start.4
  63.6 0.1 pad_maximum_fusion.1
  63.7 74.5 %collective-permute-start.5 = (bf16[4,8,128,128]{3,2,1,0:T(8,128)(2,1)S(1)}, bf16[4,8,128,128]{3,2,1,0:T(8,128)(2,1)S(1)}, u32[]{:S(2)}, u32[]{:S(2)}) collective-permute-start(bf16[4,8,128,128]{3,2,1,0:T(8,128)(2,1)S(1)} %pad_maximum_fusion.1), channel_id=1, source_target_pairs={{0,481},{1,482},{2,483},{3,484},{4,485},{5,486},{6,487},{7,488},{8... | collective-permute-start | bytes 3145736 | tf_op jit(solution)/shard_map/ppermute | solution.py:15
  138.3 11.5 %collective-permute-start.6 = (bf16[2,8,128,128]{3,2,1,0:T(8,128)(2,1)S(1)}, bf16[2,8,128,128]{3,2,1,0:T(8,128)(2,1)S(1)}, u32[]{:S(2)}, u32[]{:S(2)}) collective-permute-start(bf16[2,8,128,128]{3,2,1,0:T(8,128)(2,1)S(1)} %slice_select_fusion), channel_id=1, source_target_pairs={{480,31},{481,0},{482,1},{483,2},{484,3},{485,4},{486,5},{487,6},{... | collective-permute-start | bytes 1572872 | tf_op jit(solution)/shard_map/ppermute | solution.py:15
  149.8 5.2 %shard_map.75.acc = f32[4,2,12,128,128]{4,3,2,1,0:T(8,128)S(1)} custom-call(s32[208]{0:T(256)S(1)} %reshape.16.table_m, s32[2496]{0:T(1024)S(1)} %add.57.table_q, bf16[4,2,8,128,128]{4,3,2,1,0:T(8,128)(2,1)S(1)} %copy-done, f32[4,2,12,128,128]{4,3,2,1,0:T(8,128)S(1)} %shard_map.74.acc, bf16[2,8,128,128]{3,2,1,0:T(8,128)(2,1)S(1)} %collective-permute-done.rim_low, ...), custom_call_target="tpu_custom_call" | custom-call | flops 1000000 | bytes 1024 | tf_op jit(solution)/shard_map/pallas_call | solution.py:164
  155.0 2.7 %shard_map.76 = (bf16[4,2,12,128,128]{4,3,2,1,0:T(8,128)(2,1)}, f32[2,2,12,128,128]{4,3,2,1,0:T(8,128)S(1)}) custom-call(s32[208]{0:T(256)S(1)} %reshape.16.table_m, s32[2496]{0:T(1024)S(1)} %add.57.table_q, bf16[4,2,8,128,128]{4,3,2,1,0:T(8,128)(2,1)S(1)} %copy-done, f32[4,2,12,128,128]{4,3,2,1,0:T(8,128)S(1)} %shard_map.75.acc, ...), custom_call_target="tpu_custom_call" | custom-call | flops 49999998976 | bytes 1024 | tf_op jit(solution)/shard_map/pallas_call | solution.py:164
  157.7 58.7 %collective-permute-done.6.wrap = bf16[2,8,128,128]{3,2,1,0:T(8,128)(2,1)S(1)} collective-permute-done((bf16[2,8,128,128]{3,2,1,0:T(8,128)(2,1)S(1)}, bf16[2,8,128,128]{3,2,1,0:T(8,128)(2,1)S(1)}, u32[]{:S(2)}, u32[]{:S(2)}) %collective-permute-start.6) | collective-permute-done | bytes 524320 | tf_op jit(solution)/shard_map/ppermute | solution.py:15
  216.3 3.6 %shard_map.77 = bf16[4,2,12,128,128]{4,3,2,1,0:T(8,128)(2,1)} custom-call(s32[208]{0:T(256)S(1)} %reshape.16.table_m, s32[2496]{0:T(1024)S(1)} %add.57.table_q, bf16[4,2,8,128,128]{4,3,2,1,0:T(8,128)(2,1)S(1)} %copy-done, f32[2,2,12,128,128]{4,3,2,1,0:T(8,128)S(1)} %get-tuple-element.19.rest, ...), custom_call_target="tpu_custom_call", output_to_operand_aliasing={{}: (7, {})} | custom-call | flops 1000000 | bytes 1024 | tf_op jit(solution)/shard_map/pallas_call | solution.py:164
  (34 shorter events, 0.2 us)
Async XLA Ops:
  0.0 27.0 %copy-start.8 = (pred[26]{0:T(512)(128)(4,1)S(1)}, pred[26]{0:T(512)(128)(4,1)}, u32[]{:S(2)}) copy-start(pred[26]{0:T(512)(128)(4,1)} %constant.58.clone) | copy-start | bytes 82
  0.0 27.0 %copy-start.9 = (s32[26]{0:T(128)S(1)}, s32[26]{0:T(128)}, u32[]{:S(2)}) copy-start(s32[26]{0:T(128)} %constant.60.clone) | copy-start | bytes 316
  0.0 27.0 %copy-start.10 = (s32[26]{0:T(128)S(1)}, s32[26]{0:T(128)}, u32[]{:S(2)}) copy-start(s32[26]{0:T(128)} %constant.61.clone) | copy-start | bytes 316
  0.0 27.0 %copy-start.11 = (s32[26]{0:T(128)S(1)}, s32[26]{0:T(128)}, u32[]{:S(2)}) copy-start(s32[26]{0:T(128)} %constant.59.clone) | copy-start | bytes 316
  0.0 31.4 %copy-start = (bf16[4,2,8,128,128]{4,3,2,1,0:T(8,128)(2,1)S(1)}, bf16[4,2,8,128,128]{4,3,2,1,0:T(8,128)(2,1)}, u32[]{:S(2)}) copy-start(bf16[4,2,8,128,128]{4,3,2,1,0:T(8,128)(2,1)} %own.9) | copy-start | bytes 6291460
  0.0 29.5 %copy-start.7 = (s32[4,2,12]{2,1,0:T(2,128)S(1)}, s32[4,2,12]{2,1,0:T(2,128)}, u32[]{:S(2)}) copy-start(s32[4,2,12]{2,1,0:T(2,128)} %param.9) | copy-start | bytes 1156
  1.5 0.7 copy-start.1
  1.5 0.8 copy-start.5
  1.5 17.4 %copy-start.3 = (bf16[1,8,128,128]{3,2,1,0:T(8,128)(2,1)}, bf16[1,8,128,128]{3,2,1,0:T(8,128)(2,1)S(1)}, u32[]{:S(2)}) copy-start(bf16[1,8,128,128]{3,2,1,0:T(8,128)(2,1)S(1)} %get-tuple-element.24) | copy-start | bytes 786436
  3.2 58.2 %collective-permute-start = (bf16[2,8,128,128]{3,2,1,0:T(8,128)(2,1)}, bf16[2,8,128,128]{3,2,1,0:T(8,128)(2,1)S(1)}, u32[]{:S(2)}, u32[]{:S(2)}) collective-permute-start(bf16[2,8,128,128]{3,2,1,0:T(8,128)(2,1)} %pad_maximum_fusion.2), channel_id=1, source_target_pairs={{0,1},{1,2},{2,3},{3,4},{4,5},{5,6},{6,7},{7,8},{8,9},{9,10},{10,1... | collective-permute-start | bytes 1572872 | tf_op jit(solution)/shard_map/ppermute | solution.py:15
  19.7 41.6 %collective-permute-start.1 = (bf16[2,8,128,128]{3,2,1,0:T(8,128)(2,1)}, bf16[2,8,128,128]{3,2,1,0:T(8,128)(2,1)S(1)}, u32[]{:S(2)}, u32[]{:S(2)}) collective-permute-start(bf16[2,8,128,128]{3,2,1,0:T(8,128)(2,1)} %pad_maximum_fusion.3), channel_id=1, source_target_pairs={{0,31},{1,0},{2,1},{3,2},{4,3},{5,4},{6,5},{7,6},{8,7},{9,8},{10,9... | collective-permute-start | bytes 1572872 | tf_op jit(solution)/shard_map/ppermute | solution.py:15
  37.2 24.2 %copy-start.4 = (bf16[1,8,128,128]{3,2,1,0:T(8,128)(2,1)S(1)}, bf16[1,8,128,128]{3,2,1,0:T(8,128)(2,1)}, u32[]{:S(2)}) copy-start(bf16[1,8,128,128]{3,2,1,0:T(8,128)(2,1)} %copy-done.3) | copy-start | bytes 786436
  37.2 24.2 %copy-start.6 = (bf16[1,8,128,128]{3,2,1,0:T(8,128)(2,1)S(1)}, bf16[1,8,128,128]{3,2,1,0:T(8,128)(2,1)}, u32[]{:S(2)}) copy-start(bf16[1,8,128,128]{3,2,1,0:T(8,128)(2,1)} %copy-done.5) | copy-start | bytes 786436
  37.3 117.7 %collective-permute-start.2 = (bf16[2,8,128,128]{3,2,1,0:T(8,128)(2,1)S(1)}, bf16[2,8,128,128]{3,2,1,0:T(8,128)(2,1)S(1)}, u32[]{:S(2)}, u32[]{:S(2)}) collective-permute-start(bf16[2,8,128,128]{3,2,1,0:T(8,128)(2,1)S(1)} %get-tuple-element.17), channel_id=1, source_target_pairs={{0,1},{1,2},{2,3},{3,4},{4,5},{5,6},{6,7},{7,8},{8,9},{9,10},{10,1... | collective-permute-start | bytes 1572872 | tf_op jit(solution)/shard_map/ppermute | solution.py:15
  47.7 107.3 %collective-permute-start.3 = (bf16[2,8,128,128]{3,2,1,0:T(8,128)(2,1)S(1)}, bf16[2,8,128,128]{3,2,1,0:T(8,128)(2,1)S(1)}, u32[]{:S(2)}, u32[]{:S(2)}) collective-permute-start(bf16[2,8,128,128]{3,2,1,0:T(8,128)(2,1)S(1)} %get-tuple-element.18), channel_id=1, source_target_pairs={{0,31},{1,0},{2,1},{3,2},{4,3},{5,4},{6,5},{7,6},{8,7},{9,8},{10,9... | collective-permute-start | bytes 1572872 | tf_op jit(solution)/shard_map/ppermute | solution.py:15
  61.3 2.2 %copy-start.2 = (bf16[1,8,128,128]{3,2,1,0:T(8,128)(2,1)S(1)}, bf16[1,8,128,128]{3,2,1,0:T(8,128)(2,1)}, u32[]{:S(2)}) copy-start(bf16[1,8,128,128]{3,2,1,0:T(8,128)(2,1)} %copy-done.1) | copy-start | bytes 786436
  61.6 154.7 %collective-permute-start.4 = (bf16[4,8,128,128]{3,2,1,0:T(8,128)(2,1)S(1)}, bf16[4,8,128,128]{3,2,1,0:T(8,128)(2,1)S(1)}, u32[]{:S(2)}, u32[]{:S(2)}) collective-permute-start(bf16[4,8,128,128]{3,2,1,0:T(8,128)(2,1)S(1)} %pad_maximum_fusion), channel_id=1, source_target_pairs={{0,32},{1,33},{2,34},{3,35},{4,36},{5,37},{6,38},{7,39},{8,40},{9,... | collective-permute-start | bytes 3145736 | tf_op jit(solution)/shard_map/ppermute | solution.py:15
  63.7 152.6 %collective-permute-start.5 = (bf16[4,8,128,128]{3,2,1,0:T(8,128)(2,1)S(1)}, bf16[4,8,128,128]{3,2,1,0:T(8,128)(2,1)S(1)}, u32[]{:S(2)}, u32[]{:S(2)}) collective-permute-start(bf16[4,8,128,128]{3,2,1,0:T(8,128)(2,1)S(1)} %pad_maximum_fusion.1), channel_id=1, source_target_pairs={{0,481},{1,482},{2,483},{3,484},{4,485},{5,486},{6,487},{7,488},{8... | collective-permute-start | bytes 3145736 | tf_op jit(solution)/shard_map/ppermute | solution.py:15
  138.3 78.0 %collective-permute-start.6 = (bf16[2,8,128,128]{3,2,1,0:T(8,128)(2,1)S(1)}, bf16[2,8,128,128]{3,2,1,0:T(8,128)(2,1)S(1)}, u32[]{:S(2)}, u32[]{:S(2)}) collective-permute-start(bf16[2,8,128,128]{3,2,1,0:T(8,128)(2,1)S(1)} %slice_select_fusion), channel_id=1, source_target_pairs={{480,31},{481,0},{482,1},{483,2},{484,3},{485,4},{486,5},{487,6},{... | collective-permute-start | bytes 1572872 | tf_op jit(solution)/shard_map/ppermute | solution.py:15

commit v3 on v2

--- a/solution.py
+++ b/solution.py
@@ -7,7 +7,7 @@
 from jax.sharding import PartitionSpec as P
 
 AXES = ("blk", "rows")
-OWN, SIDE_LOW, SIDE_HIGH, NEAR_LOW, NEAR_HIGH, WRAP, PIECES = 0, 8, 12, 16, 20, 24, 26
+OWN, EARLY_LOW, EARLY_HIGH, WRAP, SIDE_LOW, SIDE_HIGH, LATE_LOW, LATE_HIGH, PIECES = 0, 8, 10, 12, 13, 17, 21, 23, 25
 BLOCKS = (12, 128, 128)
 
 
@@ -19,12 +19,12 @@
     return [((b, r), (b, (r + shift) % n_rows)) for b in range(n_blk) for r in range(n_rows)]
 
 
-def moves_x(shift, n_blk, n_rows):
+def moves_x(shift, turn, n_blk, n_rows):
     moves = []
     for b in range(n_blk):
         for r in range(n_rows):
             inside = 0 <= b + shift < n_blk
-            moves.append(((b, r), ((b + shift) % n_blk, r if inside else (r + 1) % n_rows)))
+            moves.append(((b, r), ((b + shift) % n_blk, r if inside else (r + turn) % n_rows)))
     return moves
 
 
@@ -59,50 +59,22 @@
     return lambda q: ref[(*lead, q)]
 
 
-def every_site(tables, own, pieces_of, write):
-    for x in range(own.shape[0]):
-        for col in range(2):
-            accumulate(*tables, own, x, col, pieces_of(x, col), write, 2)
-
-
-def column_kernel(table_m, table_q, own, acc):
-    def pieces_of(x, col):
-        return [(OWN + x * 2 + y, block_from(own, x, y)) for y in range(2)]
+def own_kernel(table_m, table_q, own, acc):
+    cells_x = own.shape[0]
 
     def write(x, col, n, total):
         acc[x, col, n] = total
 
-    every_site((table_m, table_q), own, pieces_of, write)
-
-
-def own_kernel(table_m, table_q, own, acc, out):
-    def pieces_of(x, col):
-        around = [near for near in (x - 1, x + 1) if 0 <= near < own.shape[0]]
-        return [(OWN + near * 2 + y, block_from(own, near, y)) for near in around for y in range(2)]
-
-    def write(x, col, n, total):
-        out[x, col, n] = acc[x, col, n] + total
-
-    every_site((table_m, table_q), own, pieces_of, write)
-
-
-def rim_kernel(table_m, table_q, own, acc, rim_low, rim_high, out):
+    for x in range(cells_x):
+        around = [near for near in (x - 1, x, x + 1) if 0 <= near < cells_x]
+        for col in range(2):
+            pieces = [(OWN + near * 2 + y, block_from(own, near, y)) for near in around for y in range(2)]
+            accumulate(table_m, table_q, own, x, col, pieces, write, 2)
+
+
+def side_kernel(table_m, table_q, own, acc, up, down, wrap, low, high, out, rest, held, sems):
     cells_x = own.shape[0]
-    rims = (rim_low, rim_high)
-
-    def pieces_of(x, col):
-        at = int(x >= cells_x // 2)
-        return [((SIDE_LOW, SIDE_HIGH)[col] + at * (cells_x - 1), block_from(rims[col], at))]
-
-    def write(x, col, n, total):
-        out[x, col, n] = acc[x, col, n] + total
-
-    every_site((table_m, table_q), own, pieces_of, write)
-
-
-def middle_kernel(table_m, table_q, own, acc, mid_low, mid_high, out, rest, held, sems):
-    cells_x = own.shape[0]
-    mids = (mid_low, mid_high)
+    sides = (low, high)
 
     def write(x, col, n, total):
         if 0 < x < cells_x - 1:
@@ -114,11 +86,14 @@
     for x in (1, 2, 0, 3):
         for col in range(2):
             first = (SIDE_LOW, SIDE_HIGH)[col]
-            pieces = [
-                (first + near, block_from(mids[col], near - 1))
-                for near in (x - 1, x, x + 1)
-                if 0 < near < cells_x - 1
-            ]
+            around = [near for near in (x - 1, x, x + 1) if 0 <= near < cells_x]
+            pieces = [(first + near, block_from(sides[col], near)) for near in around]
+            if x == 0:
+                pieces += [(EARLY_LOW + y, block_from(up, y)) for y in range(2)]
+            if x == cells_x - 1:
+                pieces += [(EARLY_HIGH + y, block_from(down, y)) for y in range(2)]
+            if x in (0, cells_x - 1):
+                pieces.append((WRAP, block_from(wrap)))
             accumulate(table_m, table_q, own, x, col, pieces, write, 6)
             if 0 < x < cells_x - 1:
                 copies.append(pltpu.make_async_copy(held.at[x - 1, col], out.at[x, col], sems.at[x - 1, col]))
@@ -127,7 +102,7 @@
         copy.wait()
 
 
-def edge_kernel(table_m, table_q, own, rest, near_low, near_high, wrap, begun, out, held, sems):
+def edge_kernel(table_m, table_q, own, rest, ll0, ll1, lh0, lh1, begun, out, held, sems):
     cells_x = own.shape[0]
 
     def write(x, col, n, total):
@@ -136,10 +111,9 @@
 
     copies = []
     for at, x in enumerate((0, cells_x - 1)):
-        first, near = ((NEAR_LOW, near_low), (NEAR_HIGH, near_high))[at]
+        first, late = ((LATE_LOW, (ll0, ll1)), (LATE_HIGH, (lh0, lh1)))[at]
         for col in range(2):
-            pieces = [(first + y, block_from(near, y)) for y in range(4)]
-            pieces += [(WRAP + y, block_from(wrap, y)) for y in range(2)]
+            pieces = [(first + y, block_from(late[y])) for y in range(2)]
             accumulate(table_m, table_q, own, x, col, pieces, write, 6)
             copies.append(pltpu.make_async_copy(held.at[at, col], out.at[x, col], sems.at[at, col]))
             copies[-1].start()
@@ -178,13 +152,13 @@
     at_blk, at_row = lax.axis_index("blk"), lax.axis_index("rows")
     first, last = at_blk == 0, at_blk == lax.axis_size("blk") - 1
     near = [(x, y) for x in range(cells_x) for y in range(cells_y)]
-    wide = [-1] * 4 + [cells_x] * 4
+    wide = [-1, -1, cells_x, cells_x]
     sides, side_y = list(range(cells_x)) * 2, [-1] * cells_x + [cells_y] * cells_x
-    dx = [x for x, _ in near] + sides + wide + [0, 0]
-    plain = [y for _, y in near] + side_y + [0, 1, -1, 2] * 2 + [2, 1]
-    turned = [y for _, y in near] + side_y + [-2, -1, -3, 0] * 2 + [2, 1]
+    dx = [x for x, _ in near] + wide + [0] + sides + wide
+    plain = [y for _, y in near] + [0, 1] * 2 + [2] + side_y + [-1, 2] * 2
+    turned = [y for _, y in near] + [-2, -1] * 2 + [2] + side_y + [1, 0] * 2
     dx, plain, turned = (np.array(v, np.int32) for v in (dx, plain, turned))
-    is_wrap = np.arange(PIECES) >= WRAP
+    is_wrap = np.arange(PIECES) == WRAP
     dx = jnp.where(is_wrap, jnp.where(first, -1, cells_x), dx)
     swapped = ((dx < 0) & first) | ((dx >= cells_x) & last)
     dy = jnp.where(swapped, turned, plain)
@@ -210,29 +184,21 @@
     last = cells_x - 1
     first = lax.axis_index("blk") == 0
     along_y = lambda value, shift: send(value, moves_y(shift, n_blk, n_rows), n_rows)
-    along_x = lambda value, shift: send(value, moves_x(shift, n_blk, n_rows), n_rows)
+    along_x = lambda value, shift, turn: send(value, moves_x(shift, turn, n_blk, n_rows), n_rows)
     past_edge = lambda value: send(value, moves_wrap(n_blk, n_rows), n_rows)
     tie = lax.optimization_barrier
 
-    rim_low = along_y(jnp.stack([p_vals[0, 1], p_vals[last, 1]]), 1)
-    rim_high = along_y(jnp.stack([p_vals[0, 0], p_vals[last, 0]]), -1)
-
+    low = along_y(p_vals[:, 1], 1)
+    high = along_y(p_vals[:, 0], -1)
     tables = make_tables(p_cols, c_cols, cells_x, cells_y)
-    acc = run_kernel(column_kernel, tables, p_vals, [], 4 * 10**9)
-    acc, middle = tie((acc, (p_vals[1:last, 1], p_vals[1:last, 0])))
-    mid_low = along_y(middle[0], 1)
-    mid_high = along_y(middle[1], -1)
-
-    acc = run_kernel(own_kernel, tables, p_vals, [acc], 4 * 10**9)
-    acc, rim_low, rim_high = tie((acc, rim_low, rim_high))
-    below = jnp.stack([p_vals[0, 0], p_vals[0, 1], rim_low[0], rim_high[0]])
-    above = jnp.stack([p_vals[last, 0], p_vals[last, 1], rim_low[1], rim_high[1]])
-    pair = jnp.where(first, below[0:3:2], above[0:3:2])
-    near = [along_x(above, 1), along_x(below, -1), past_edge(pair)]
-
-    acc = run_kernel(rim_kernel, tables, p_vals, [acc, rim_low, rim_high], 10**6)
-    begun, rest = run_kernel(middle_kernel, tables, p_vals, [acc, mid_low, mid_high], 5 * 10**10, middle=True)
-    return run_kernel(edge_kernel, tables, p_vals, [rest, *near], 10**6, begun=begun)
+    tables, edges = tie((tables, (p_vals[last], p_vals[0])))
+    single = jnp.where(first, edges[1][0], edges[0][0])
+    early = [along_x(edges[0], 1, 1), along_x(edges[1], -1, 1), past_edge(single)]
+
+    acc = run_kernel(own_kernel, tables, p_vals, [], 10**6)
+    late = [along_x(side[edge], s, t) for edge, s in ((last, 1), (0, -1)) for side, t in ((low, -1), (high, 1))]
+    begun, rest = run_kernel(side_kernel, tables, p_vals, [acc, *early, low, high], 10**10, middle=True)
+    return run_kernel(edge_kernel, tables, p_vals, [rest, *late], 10**6, begun=begun)
 
 
 def solution(mesh):

time: 220 us -> 228 us (1.036); the launches traced: 220 us -> 225 us
  waiting for transfers between devices: 58.7 us -> 154 us
  starting transfers between devices: 126 us -> 46.2 us
  Pallas kernels: 23.4 us -> 14.6 us
  other arithmetic: 3.11 us -> 0.51 us
    ppermute x7 -> x9, waiting for transfers between devices: 58.7 us -> 154 us  [send(): lax.ppermute(value, AXES, [(a[0] * n_rows + a[1], b[0] * n_rows + b[1]) f...]
    ppermute x7 -> x9, starting transfers between devices: 126 us -> 46.2 us  [send(): lax.ppermute(value, AXES, [(a[0] * n_rows + a[1], b[0] * n_rows + b[1]) f...]
    pallas_call x5 -> x3, Pallas kernels: 23.4 us -> 14.6 us  [run_kernel(): pl.pallas_call(body, out_shape=out_shape, in_specs=in_specs, out_specs=ou...]
    squeeze x1 -> x4, local copies, waits for them, and re-layouts: 0.1 us -> 4.39 us  [the longest x1 3.17 us: on_device(): high = along_y(p_vals[:, 0], -1)]
  transfers between devices with their start and end apart: 7 -> 9, of which waited for: 1 -> 3; matrix products, arithmetic and copies ran while one was open for 4% -> 3% of each run, Pallas kernels for 9% -> 5%
where the time goes in v3:
time: 228 us; the launch traced here: 225 us
  waiting for transfers between devices  154 us (68%)
  starting transfers between devices  46.2 us (20%)
  Pallas kernels  14.6 us (6%)
  local copies, waits for them, and re-layouts  8.92 us (4%)
    ppermute x9, waiting for transfers between devices, send(): lax.ppermute(value, AXES, [(a[0] * n_rows + a[1], b[0] * n_rows + b[1]) f...  154 us
    ppermute x9, starting transfers between devices, send(): lax.ppermute(value, AXES, [(a[0] * n_rows + a[1], b[0] * n_rows + b[1]) f...  46.2 us
    pallas_call x3, Pallas kernels, run_kernel(): pl.pallas_call(body, out_shape=out_shape, in_specs=in_specs, out_specs=ou...  14.6 us
  transfers between devices with their start and end apart: 9, of which 3 were waited for; matrix products, arithmetic and copies ran while one was open for 3% of the time, Pallas kernels for 5%

profile of v3, /device:TPU:24, one launch (start us, length us, event | category | flops | bytes accessed | tf_op | source)
XLA Modules:
  0.0 225.0 jit_solution(16423032651273804113)
XLA Ops:
  0.0 0.0 copy-start.6
  0.0 3.2 %slice_bitcast_fusion = (bf16[4,8,128,128]{3,2,1,0:T(8,128)(2,1)}, bf16[4,8,128,128]{3,2,1,0:T(8,128)(2,1)}) fusion(bf16[4,2,8,128,128]{4,3,2,1,0:T(8,128)(2,1)} %own.5), kind=kLoop, calls=%fused_computation.1 | loop fusion | bytes 4194304 | tf_op jit(solution)/shard_map/squeeze | solution.py:192
  3.2 15.8 %collective-permute-start.3 = (bf16[4,8,128,128]{3,2,1,0:T(8,128)(2,1)}, bf16[4,8,128,128]{3,2,1,0:T(8,128)(2,1)S(1)}, u32[]{:S(2)}, u32[]{:S(2)}) collective-permute-start(bf16[4,8,128,128]{3,2,1,0:T(8,128)(2,1)} %get-tuple-element.20), channel_id=1, source_target_pairs={{0,1},{1,2},{2,3},{3,4},{4,5},{5,6},{6,7},{7,8},{8,9},{9,10},{10,1... | collective-permute-start | bytes 3145736 | tf_op jit(solution)/shard_map/ppermute | solution.py:15
  19.1 4.3 %collective-permute-start.4 = (bf16[4,8,128,128]{3,2,1,0:T(8,128)(2,1)}, bf16[4,8,128,128]{3,2,1,0:T(8,128)(2,1)}, u32[]{:S(2)}, u32[]{:S(2)}) collective-permute-start(bf16[4,8,128,128]{3,2,1,0:T(8,128)(2,1)} %get-tuple-element.19), channel_id=1, source_target_pairs={{0,31},{1,0},{2,1},{3,2},{4,3},{5,4},{6,5},{7,6},{8,7},{9,8},{10,9... | collective-permute-start | bytes 3145736 | tf_op jit(solution)/shard_map/ppermute | solution.py:15
  23.5 1.9 copy.20
  25.4 2.2 gather_fusion
  27.6 0.1 copy.21
  27.7 0.1 compare_reduce_fusion
  27.8 0.2 select_reduce_fusion
  28.0 0.1 copy.23
  28.2 0.1 add.57.table_q
  28.3 0.1 fusion
  28.4 0.1 reshape.18.table_m
  28.5 0.1 slice_bitcast_fusion.2
  28.6 1.9 collective-permute-start
  30.5 4.8 %collective-permute-start.1 = (bf16[2,8,128,128]{3,2,1,0:T(8,128)(2,1)S(1)}, bf16[2,8,128,128]{3,2,1,0:T(8,128)(2,1)S(1)}, u32[]{:S(2)}, u32[]{:S(2)}) collective-permute-start(bf16[2,8,128,128]{3,2,1,0:T(8,128)(2,1)S(1)} %get-tuple-element.14), channel_id=1, source_target_pairs={{0,481},{1,482},{2,483},{3,484},{4,485},{5,486},{6,487},{7,488},{8... | collective-permute-start | bytes 1572872 | tf_op jit(solution)/shard_map/ppermute | solution.py:15
  35.4 5.5 %collective-permute-start.2 = (bf16[8,128,128]{2,1,0:T(8,128)(2,1)S(1)}, bf16[8,128,128]{2,1,0:T(8,128)(2,1)S(1)}, u32[]{:S(2)}, u32[]{:S(2)}) collective-permute-start(bf16[8,128,128]{2,1,0:T(8,128)(2,1)S(1)} %select_bitcast_fusion), channel_id=1, source_target_pairs={{480,31},{481,0},{482,1},{483,2},{484,3},{485,4},{486,5},{487,6},{... | collective-permute-start | bytes 786440 | tf_op jit(solution)/shard_map/ppermute | solution.py:15
  40.9 7.5 %shard_map.73.acc = f32[4,2,12,128,128]{4,3,2,1,0:T(8,128)S(1)} custom-call(s32[200]{0:T(256)S(1)} %reshape.18.table_m, s32[2400]{0:T(1024)S(1)} %add.57.table_q, bf16[4,2,8,128,128]{4,3,2,1,0:T(8,128)(2,1)S(1)} %copy-done), custom_call_target="tpu_custom_call" | custom-call | flops 1000000 | bytes 1024 | tf_op jit(solution)/shard_map/pallas_call | solution.py:138
  48.5 11.0 %collective-permute-done.3.low = bf16[4,8,128,128]{3,2,1,0:T(8,128)(2,1)S(1)} collective-permute-done((bf16[4,8,128,128]{3,2,1,0:T(8,128)(2,1)}, bf16[4,8,128,128]{3,2,1,0:T(8,128)(2,1)S(1)}, u32[]{:S(2)}, u32[]{:S(2)}) %collective-permute-start.3) | collective-permute-done | bytes 1048608 | tf_op jit(solution)/shard_map/ppermute | solution.py:15
  59.5 1.9 collective-permute-start.5
  61.5 138.4 %collective-permute-done.4.high = bf16[4,8,128,128]{3,2,1,0:T(8,128)(2,1)} collective-permute-done((bf16[4,8,128,128]{3,2,1,0:T(8,128)(2,1)}, bf16[4,8,128,128]{3,2,1,0:T(8,128)(2,1)}, u32[]{:S(2)}, u32[]{:S(2)}) %collective-permute-start.4) | collective-permute-done | bytes 1048608 | tf_op jit(solution)/shard_map/ppermute | solution.py:15
  199.9 1.1 slice_bitcast_fusion.4
  200.9 1.9 collective-permute-start.6
  202.9 5.0 %collective-permute-done.2.wrap = bf16[8,128,128]{2,1,0:T(8,128)(2,1)S(1)} collective-permute-done((bf16[8,128,128]{2,1,0:T(8,128)(2,1)S(1)}, bf16[8,128,128]{2,1,0:T(8,128)(2,1)S(1)}, u32[]{:S(2)}, u32[]{:S(2)}) %collective-permute-start.2) | collective-permute-done | bytes 262176 | tf_op jit(solution)/shard_map/ppermute | solution.py:15
  207.9 8.0 %collective-permute-start.7 = (bf16[8,128,128]{2,1,0:T(8,128)(2,1)S(1)}, bf16[8,128,128]{2,1,0:T(8,128)(2,1)S(1)}, u32[]{:S(2)}, u32[]{:S(2)}) collective-permute-start(bf16[8,128,128]{2,1,0:T(8,128)(2,1)S(1)} %get-tuple-element.25), channel_id=1, source_target_pairs={{0,511},{1,480},{2,481},{3,482},{4,483},{5,484},{6,485},{7,486},{8... | collective-permute-start | bytes 786440 | tf_op jit(solution)/shard_map/ppermute | solution.py:15
  215.9 0.0 collective-permute-done.up
  215.9 1.9 collective-permute-start.8
  217.9 0.0 collective-permute-done.1.down
  217.9 4.7 %shard_map.74 = (bf16[4,2,12,128,128]{4,3,2,1,0:T(8,128)(2,1)}, f32[2,2,12,128,128]{4,3,2,1,0:T(8,128)S(1)}) custom-call(s32[200]{0:T(256)S(1)} %reshape.18.table_m, s32[2400]{0:T(1024)S(1)} %add.57.table_q, bf16[4,2,8,128,128]{4,3,2,1,0:T(8,128)(2,1)S(1)} %copy-done, f32[4,2,12,128,128]{4,3,2,1,0:T(8,128)S(1)} %shard_map.73.acc, ...), custom_call_target="tpu_custom_call" | custom-call | flops 10000000000 | bytes 1024 | tf_op jit(solution)/shard_map/pallas_call | solution.py:138
  222.6 0.0 collective-permute-done.6.ll1
  222.6 0.0 collective-permute-done.7.lh0
  222.6 2.4 %shard_map.75 = bf16[4,2,12,128,128]{4,3,2,1,0:T(8,128)(2,1)} custom-call(s32[200]{0:T(256)S(1)} %reshape.18.table_m, s32[2400]{0:T(1024)S(1)} %add.57.table_q, bf16[4,2,8,128,128]{4,3,2,1,0:T(8,128)(2,1)S(1)} %copy-done, f32[2,2,12,128,128]{4,3,2,1,0:T(8,128)S(1)} %get-tuple-element.15.rest, ...), custom_call_target="tpu_custom_call", output_to_operand_aliasing={{}: (8, {})} | custom-call | flops 1000000 | bytes 1024 | tf_op jit(solution)/shard_map/pallas_call | solution.py:138
  (23 shorter events, 0.2 us)
Async XLA Ops:
  0.0 23.4 %copy-start.3 = (pred[25]{0:T(512)(128)(4,1)S(1)}, pred[25]{0:T(512)(128)(4,1)}, u32[]{:S(2)}) copy-start(pred[25]{0:T(512)(128)(4,1)} %constant.58.clone) | copy-start | bytes 79
  0.0 23.4 %copy-start.4 = (s32[25]{0:T(128)S(1)}, s32[25]{0:T(128)}, u32[]{:S(2)}) copy-start(s32[25]{0:T(128)} %constant.59.clone) | copy-start | bytes 304
  0.0 23.4 %copy-start.5 = (s32[25]{0:T(128)S(1)}, s32[25]{0:T(128)}, u32[]{:S(2)}) copy-start(s32[25]{0:T(128)} %constant.60.clone) | copy-start | bytes 304
  0.0 23.4 %copy-start.6 = (s32[25]{0:T(128)S(1)}, s32[25]{0:T(128)}, u32[]{:S(2)}) copy-start(s32[25]{0:T(128)} %constant.61.clone) | copy-start | bytes 304
  0.0 23.4 %copy-start.1 = (s32[64,64,8]{1,2,0:T(8,128)S(1)}, s32[64,64,8]{1,2,0:T(8,128)}, u32[]{:S(2)}) copy-start(s32[64,64,8]{1,2,0:T(8,128)} %param.8) | copy-start | bytes 393220
  3.2 24.6 %copy-start.2 = (s32[4,2,12]{2,1,0:T(2,128)S(1)}, s32[4,2,12]{2,1,0:T(2,128)}, u32[]{:S(2)}) copy-start(s32[4,2,12]{2,1,0:T(2,128)} %param.9) | copy-start | bytes 1156
  3.2 25.3 %copy-start = (bf16[4,2,8,128,128]{4,3,2,1,0:T(8,128)(2,1)S(1)}, bf16[4,2,8,128,128]{4,3,2,1,0:T(8,128)(2,1)}, u32[]{:S(2)}) copy-start(bf16[4,2,8,128,128]{4,3,2,1,0:T(8,128)(2,1)} %own.5) | copy-start | bytes 6291460
  3.2 56.3 %collective-permute-start.3 = (bf16[4,8,128,128]{3,2,1,0:T(8,128)(2,1)}, bf16[4,8,128,128]{3,2,1,0:T(8,128)(2,1)S(1)}, u32[]{:S(2)}, u32[]{:S(2)}) collective-permute-start(bf16[4,8,128,128]{3,2,1,0:T(8,128)(2,1)} %get-tuple-element.20), channel_id=1, source_target_pairs={{0,1},{1,2},{2,3},{3,4},{4,5},{5,6},{6,7},{7,8},{8,9},{9,10},{10,1... | collective-permute-start | bytes 3145736 | tf_op jit(solution)/shard_map/ppermute | solution.py:15
  19.1 180.8 %collective-permute-start.4 = (bf16[4,8,128,128]{3,2,1,0:T(8,128)(2,1)}, bf16[4,8,128,128]{3,2,1,0:T(8,128)(2,1)}, u32[]{:S(2)}, u32[]{:S(2)}) collective-permute-start(bf16[4,8,128,128]{3,2,1,0:T(8,128)(2,1)} %get-tuple-element.19), channel_id=1, source_target_pairs={{0,31},{1,0},{2,1},{3,2},{4,3},{5,4},{6,5},{7,6},{8,7},{9,8},{10,9... | collective-permute-start | bytes 3145736 | tf_op jit(solution)/shard_map/ppermute | solution.py:15
  28.6 187.4 %collective-permute-start = (bf16[2,8,128,128]{3,2,1,0:T(8,128)(2,1)S(1)}, bf16[2,8,128,128]{3,2,1,0:T(8,128)(2,1)S(1)}, u32[]{:S(2)}, u32[]{:S(2)}) collective-permute-start(bf16[2,8,128,128]{3,2,1,0:T(8,128)(2,1)S(1)} %get-tuple-element.13), channel_id=1, source_target_pairs={{0,32},{1,33},{2,34},{3,35},{4,36},{5,37},{6,38},{7,39},{8,40},{9,... | collective-permute-start | bytes 1572872 | tf_op jit(solution)/shard_map/ppermute | solution.py:15
  30.5 187.4 %collective-permute-start.1 = (bf16[2,8,128,128]{3,2,1,0:T(8,128)(2,1)S(1)}, bf16[2,8,128,128]{3,2,1,0:T(8,128)(2,1)S(1)}, u32[]{:S(2)}, u32[]{:S(2)}) collective-permute-start(bf16[2,8,128,128]{3,2,1,0:T(8,128)(2,1)S(1)} %get-tuple-element.14), channel_id=1, source_target_pairs={{0,481},{1,482},{2,483},{3,484},{4,485},{5,486},{6,487},{7,488},{8... | collective-permute-start | bytes 1572872 | tf_op jit(solution)/shard_map/ppermute | solution.py:15
  35.4 172.5 %collective-permute-start.2 = (bf16[8,128,128]{2,1,0:T(8,128)(2,1)S(1)}, bf16[8,128,128]{2,1,0:T(8,128)(2,1)S(1)}, u32[]{:S(2)}, u32[]{:S(2)}) collective-permute-start(bf16[8,128,128]{2,1,0:T(8,128)(2,1)S(1)} %select_bitcast_fusion), channel_id=1, source_target_pairs={{480,31},{481,0},{482,1},{483,2},{484,3},{485,4},{486,5},{487,6},{... | collective-permute-start | bytes 786440 | tf_op jit(solution)/shard_map/ppermute | solution.py:15
  59.5 163.1 %collective-permute-start.5 = (bf16[8,128,128]{2,1,0:T(8,128)(2,1)S(1)}, bf16[8,128,128]{2,1,0:T(8,128)(2,1)S(1)}, u32[]{:S(2)}, u32[]{:S(2)}) collective-permute-start(bf16[8,128,128]{2,1,0:T(8,128)(2,1)S(1)} %get-tuple-element.26), channel_id=1, source_target_pairs={{0,32},{1,33},{2,34},{3,35},{4,36},{5,37},{6,38},{7,39},{8,40},{9,... | collective-permute-start | bytes 786440 | tf_op jit(solution)/shard_map/ppermute | solution.py:15
  200.9 21.7 %collective-permute-start.6 = (bf16[8,128,128]{2,1,0:T(8,128)(2,1)S(1)}, bf16[8,128,128]{2,1,0:T(8,128)(2,1)S(1)}, u32[]{:S(2)}, u32[]{:S(2)}) collective-permute-start(bf16[8,128,128]{2,1,0:T(8,128)(2,1)S(1)} %get-tuple-element.24), channel_id=1, source_target_pairs={{0,32},{1,33},{2,34},{3,35},{4,36},{5,37},{6,38},{7,39},{8,40},{9,... | collective-permute-start | bytes 786440 | tf_op jit(solution)/shard_map/ppermute | solution.py:15
  207.9 14.7 %collective-permute-start.7 = (bf16[8,128,128]{2,1,0:T(8,128)(2,1)S(1)}, bf16[8,128,128]{2,1,0:T(8,128)(2,1)S(1)}, u32[]{:S(2)}, u32[]{:S(2)}) collective-permute-start(bf16[8,128,128]{2,1,0:T(8,128)(2,1)S(1)} %get-tuple-element.25), channel_id=1, source_target_pairs={{0,511},{1,480},{2,481},{3,482},{4,483},{5,484},{6,485},{7,486},{8... | collective-permute-start | bytes 786440 | tf_op jit(solution)/shard_map/ppermute | solution.py:15
  215.9 6.7 %collective-permute-start.8 = (bf16[8,128,128]{2,1,0:T(8,128)(2,1)S(1)}, bf16[8,128,128]{2,1,0:T(8,128)(2,1)S(1)}, u32[]{:S(2)}, u32[]{:S(2)}) collective-permute-start(bf16[8,128,128]{2,1,0:T(8,128)(2,1)S(1)} %get-tuple-element.23), channel_id=1, source_target_pairs={{0,481},{1,482},{2,483},{3,484},{4,485},{5,486},{6,487},{7,488},{8... | collective-permute-start | bytes 786440 | tf_op jit(solution)/shard_map/ppermute | solution.py:15

commit v4 on v2

v4 whole, which is shorter than its diff:
```python
import jax
import jax.numpy as jnp
import numpy as np
from jax import lax
from jax.experimental import pallas as pl
from jax.experimental.pallas import tpu as pltpu
from jax.sharding import PartitionSpec as P

AXES = ("blk", "rows")
OWN, EARLY_LOW, EARLY_HIGH, SIDE_LOW, SIDE_HIGH, LATE_LOW, LATE_HIGH, PIECES = 0, 8, 10, 12, 16, 20, 22, 24
BLOCKS = (12, 128, 128)


def send(value, moves, n_rows):
    return lax.ppermute(value, AXES, [(a[0] * n_rows + a[1], b[0] * n_rows + b[1]) for a, b in moves])


def moves_y(shift, n_blk, n_rows):
    return [((b, r), (b, (r + shift) % n_rows)) for b in range(n_blk) for r in range(n_rows)]


def moves_x(shift, n_blk, n_rows):
    return [((b, r), ((b + shift) % n_blk, r)) for b in range(n_blk) for r in range(n_rows)]


def accumulate(table_m, table_q, own, x, col, pieces, write, unroll):
    site = x * 2 + col
    left = jnp.concatenate([own[x, col, table_m[site * PIECES + number]] for number, _ in pieces], axis=1)

    def pair(h, carry):
        halves = []
        for n in (2 * h, 2 * h + 1):
            rows = []
            for number, block_of in pieces:
                q = table_q[(site * PIECES + number) * 12 + n]
                block = block_of(jnp.minimum(q, 7))
                rows.append(jnp.where(q < 8, block, jnp.zeros_like(block)))
            halves.append(jnp.concatenate(rows, axis=0))
        right = jnp.concatenate(halves, axis=1)
        total = jnp.dot(left, right, preferred_element_type=jnp.float32)
        write(x, col, 2 * h, total[:, :128])
        write(x, col, 2 * h + 1, total[:, 128:])
        return carry

    lax.fori_loop(0, 6, pair, 0, unroll=unroll)


def block_from(ref, *lead):
    return lambda q: ref[(*lead, q)]


def column_kernel(table_m, table_q, own, acc):
    def write(x, col, n, total):
        acc[x, col, n] = total

    for x in range(own.shape[0]):
        for col in range(2):
            pieces = [(OWN + x * 2 + y, block_from(own, x, y)) for y in range(2)]
            accumulate(table_m, table_q, own, x, col, pieces, write, 2)


def own_kernel(table_m, table_q, own, acc, out):
    def write(x, col, n, total):
        out[x, col, n] = acc[x, col, n] + total

    for x in range(own.shape[0]):
        around = [near for near in (x - 1, x + 1) if 0 <= near < own.shape[0]]
        for col in range(2):
            pieces = [(OWN + near * 2 + y, block_from(own, near, y)) for near in around for y in range(2)]
            accumulate(table_m, table_q, own, x, col, pieces, write, 2)


def rim_kernel(table_m, table_q, own, acc, rim_low, rim_high, up, down, out):
    cells_x = own.shape[0]
    rims = (rim_low, rim_high)

    def write(x, col, n, total):
        out[x, col, n] = acc[x, col, n] + total

    for x in range(cells_x):
        for col in range(2):
            at = int(x >= cells_x // 2)
            pieces = [((SIDE_LOW, SIDE_HIGH)[col] + at * (cells_x - 1), block_from(rims[col], at))]
            if x in (0, cells_x - 1):
                first, near = ((EARLY_LOW, up), (EARLY_HIGH, down))[at]
                pieces += [(first + y, block_from(near, y)) for y in range(2)]
            accumulate(table_m, table_q, own, x, col, pieces, write, 2)


def middle_kernel(table_m, table_q, own, acc, mid_low, mid_high, out):
    cells_x = own.shape[0]

    def write(x, col, n, total):
        out[x, col, n] = acc[x, col, n] + total

    for x in range(cells_x):
        for col in range(2):
            first, mid, count = ((SIDE_LOW, mid_low, 2), (SIDE_HIGH, mid_high, 1))[col]
            pieces = [
                (first + near, block_from(mid, near - 1)) for near in (x - 1, x, x + 1) if 0 < near <= count
            ]
            if pieces:
                accumulate(table_m, table_q, own, x, col, pieces, write, 3)
            else:
                out[x, col] = acc[x, col]


def is_last(x, col):
    return x > 0 and col == 1


def late_kernel(table_m, table_q, own, acc, up, down, out, rest, held, sems):
    cells_x = own.shape[0]

    def write(x, col, n, total):
        if is_last(x, col):
            rest[x, n] = acc[x, col, n] + total
        else:
            held[x, col, n] = (acc[x, col, n] + total).astype(jnp.bfloat16)

    copies = []
    for x in (0, 1, 2, 3):
        for col in range(2):
            if 0 < x < cells_x - 1:
                if is_last(x, col):
                    rest[x] = acc[x, col]
                else:
                    held[x, col] = acc[x, col].astype(jnp.bfloat16)
            else:
                first, late = ((LATE_LOW, up), (LATE_HIGH, down))[int(x > 0)]
                pieces = [(first + y, block_from(late, y)) for y in range(2)]
                accumulate(table_m, table_q, own, x, col, pieces, write, 6)
            if not is_last(x, col):
                copies.append(pltpu.make_async_copy(held.at[x, col], out.at[x, col], sems.at[x, col]))
                copies[-1].start()
    for copy in copies:
        copy.wait()


def last_kernel(table_m, table_q, own, rest, site, begun, out, held, sems):
    cells_x = own.shape[0]

    def write(x, col, n, total):
        held[x, col, n] = (rest[x, n] + total).astype(jnp.bfloat16)

    copies = []
    for x in range(1, cells_x):
        pieces = [(SIDE_HIGH + 2, block_from(site))]
        accumulate(table_m, table_q, own, x, 1, pieces, write, 6)
        copies.append(pltpu.make_async_copy(held.at[x, 1], out.at[x, 1], sems.at[x, 1]))
        copies[-1].start()
    for copy in copies:
        copy.wait()


def run_kernel(body, tables, own, sites, flops, begun=None, rest=False):
    whole, part = (own.shape[0], 2) + BLOCKS, (own.shape[0],) + BLOCKS
    in_vmem, in_hbm = pl.BlockSpec(memory_space=pltpu.VMEM), pl.BlockSpec(memory_space=pl.ANY)
    out_shape, out_specs = jax.ShapeDtypeStruct(whole, jnp.float32), in_vmem
    in_specs = [pl.BlockSpec(memory_space=pltpu.SMEM)] * 2 + [in_vmem] * (1 + len(sites))
    held, aliases = [], {}
    if rest or begun is not None:
        out_shape, out_specs = jax.ShapeDtypeStruct(whole, jnp.bfloat16), in_hbm
        held = [pltpu.VMEM(whole, jnp.bfloat16), pltpu.SemaphoreType.DMA(whole[:2])]
    if rest:
        out_shape, out_specs = (out_shape, jax.ShapeDtypeStruct(part, jnp.float32)), (out_specs, in_vmem)
    if begun is not None:
        aliases = {len(in_specs): 0}
        in_specs, sites = in_specs + [in_hbm], [*sites, begun]
    return pl.pallas_call(
        body,
        out_shape=out_shape,
        in_specs=in_specs,
        out_specs=out_specs,
        scratch_shapes=held,
        input_output_aliases=aliases,
        compiler_params=pltpu.CompilerParams(vmem_limit_bytes=32 * 2**20),
        cost_estimate=pl.CostEstimate(flops=flops, bytes_accessed=2**10, transcendentals=0),
    )(*tables, own, *sites)


def make_tables(p_cols, c_cols, cells_x, cells_y):
    total_x, total_y, blocks = p_cols.shape
    at_blk, at_row = lax.axis_index("blk"), lax.axis_index("rows")
    near = [(x, y) for x in range(cells_x) for y in range(cells_y)]
    wide = [-1, -1, cells_x, cells_x]
    sides, side_y = list(range(cells_x)) * 2, [-1] * cells_x + [cells_y] * cells_x
    dx = np.array([x for x, _ in near] + wide + sides + wide, np.int32)
    dy = np.array([y for _, y in near] + [0, 1] * 2 + side_y + [-1, cells_y] * 2, np.int32)
    site_x = (at_blk * cells_x + dx + total_x) % total_x
    site_y = (at_row * cells_y + dy + total_y) % total_y
    ids = site_x * total_y + site_y
    cols = p_cols.reshape(total_x * total_y, blocks)[ids]
    own = cols[: cells_x * cells_y]
    slots = jnp.arange(blocks, dtype=jnp.int32)
    is_left = own[:, None, :] == ids[None, :, None]
    table_m = jnp.sum(jnp.where(is_left, slots, 0), axis=2)
    has_left = jnp.any(is_left, axis=2)
    targets = c_cols.reshape(cells_x * cells_y, -1)
    is_right = (cols[None, :, None, :] == targets[:, None, :, None]) & has_left[:, :, None, None]
    table_q = 8 + jnp.sum(jnp.where(is_right, slots - 8, 0), axis=3)
    return table_m.reshape(-1).astype(jnp.int32), table_q.reshape(-1).astype(jnp.int32)


def on_device(p_vals, p_cols, c_cols):
    cells_x, cells_y = p_vals.shape[:2]
    n_blk, n_rows = lax.axis_size("blk"), lax.axis_size("rows")
    last = cells_x - 1
    along_y = lambda value, shift: send(value, moves_y(shift, n_blk, n_rows), n_rows)
    along_x = lambda value, shift: send(value, moves_x(shift, n_blk, n_rows), n_rows)
    tie = lax.optimization_barrier

    rim_low = along_y(jnp.stack([p_vals[0, 1], p_vals[last, 1]]), 1)
    rim_high = along_y(jnp.stack([p_vals[0, 0], p_vals[last, 0]]), -1)

    tables = make_tables(p_cols, c_cols, cells_x, cells_y)
    tables, edges = tie((tables, (p_vals[last], p_vals[0])))
    early = [along_x(edges[0], 1), along_x(edges[1], -1)]
    acc = run_kernel(column_kernel, tables, p_vals, [], 4 * 10**9)
    acc, middle = tie((acc, (p_vals[1:last, 1], p_vals[1:2, 0])))
    mid_low = along_y(middle[0], 1)
    mid_high = along_y(middle[1], -1)

    acc = run_kernel(own_kernel, tables, p_vals, [acc], 4 * 10**9)
    acc, rim_low, rim_high = tie((acc, rim_low, rim_high))
    late = [along_x(jnp.stack([rim_low[at], rim_high[at]]), shift) for at, shift in ((1, 1), (0, -1))]
    acc = run_kernel(rim_kernel, tables, p_vals, [acc, rim_low, rim_high, *early], 10**6)
    acc, site = tie((acc, p_vals[2, 0]))
    final = along_y(site, -1)
    acc = run_kernel(middle_kernel, tables, p_vals, [acc, mid_low, mid_high], 5 * 10**9)
    begun, rest = run_kernel(late_kernel, tables, p_vals, [acc, *late], 10**6, rest=True)
    return run_kernel(last_kernel, tables, p_vals, [rest, final], 10**6, begun=begun)


def solution(mesh):
    placed = (P("blk", "rows", None, None, None), P(), P("blk", "rows", None))
    return jax.shard_map(
        on_device,
        mesh=mesh,
        in_specs=placed,
        out_specs=P("blk", "rows", None, None, None),
        check_vma=False,
    )
```

time: 220 us -> 224 us (1.018)
  waiting for transfers between devices: 58.7 us -> 129 us
  starting transfers between devices: 126 us -> 57.1 us
  Pallas kernels: 23.4 us -> 26.2 us
    ppermute x7 -> x9, waiting for transfers between devices: 58.7 us -> 129 us  [send(): lax.ppermute(value, AXES, [(a[0] * n_rows + a[1], b[0] * n_rows + b[1]) f...]
    ppermute x7 -> x9, starting transfers between devices: 126 us -> 57.1 us  [send(): lax.ppermute(value, AXES, [(a[0] * n_rows + a[1], b[0] * n_rows + b[1]) f...]
    squeeze x1 -> x3, local copies, waits for them, and re-layouts: 0.1 us -> 3.65 us  [the longest x1 2.49 us: on_device(): acc, site = tie((acc, p_vals[2, 0]))]
    pallas_call x5 -> x6, Pallas kernels: 23.4 us -> 26.2 us  [run_kernel(): pl.pallas_call(body, out_shape=out_shape, in_specs=in_specs, out_specs=ou...]
  transfers between devices with their start and end apart: 7 -> 9, of which waited for: 1 -> 4; matrix products, arithmetic and copies ran while one was open for 4% -> 3% of each run, Pallas kernels for 9% -> 11%
where the time goes in v4:
time: 224 us; the launch traced here: 223 us
  waiting for transfers between devices  129 us (58%)
  starting transfers between devices  57.1 us (25%)
  Pallas kernels  26.2 us (12%)
  local copies, waits for them, and re-layouts  8.23 us (4%)
  other arithmetic  2.27 us (1%)
    ppermute x9, waiting for transfers between devices, send(): lax.ppermute(value, AXES, [(a[0] * n_rows + a[1], b[0] * n_rows + b[1]) f...  129 us
    ppermute x9, starting transfers between devices, send(): lax.ppermute(value, AXES, [(a[0] * n_rows + a[1], b[0] * n_rows + b[1]) f...  57.1 us
    pallas_call x6, Pallas kernels, run_kernel(): pl.pallas_call(body, out_shape=out_shape, in_specs=in_specs, out_specs=ou...  26.2 us
  transfers between devices with their start and end apart: 9, of which 4 were waited for; matrix products, arithmetic and copies ran while one was open for 3% of the time, Pallas kernels for 11%

profile of v4, /device:TPU:24, one launch (start us, length us, event | category | flops | bytes accessed | tf_op | source)
XLA Modules:
  0.0 222.8 jit_solution(8933386438239799110)
XLA Ops:
  0.0 2.5 %slice_bitcast_fusion.3 = (bf16[8,128,128]{2,1,0:T(8,128)(2,1)}, bf16[1,8,128,128]{3,2,1,0:T(8,128)(2,1)S(1)}, bf16[1,8,128,128]{3,2,1,0:T(8,128)(2,1)S(1)}, bf1...) fusion(bf16[4,2,8,128,128]{4,3,2,1,0:T(8,128)(2,1)} %own.11), kind=kLoop, calls=%fused_computation.9 | loop fusion | bytes 3145728 | tf_op jit(solution)/shard_map/squeeze | solution.py:228
  2.5 0.9 pad_maximum_fusion
  3.4 15.7 %collective-permute-start = (bf16[2,8,128,128]{3,2,1,0:T(8,128)(2,1)}, bf16[2,8,128,128]{3,2,1,0:T(8,128)(2,1)S(1)}, u32[]{:S(2)}, u32[]{:S(2)}) collective-permute-start(bf16[2,8,128,128]{3,2,1,0:T(8,128)(2,1)} %pad_maximum_fusion), channel_id=1, source_target_pairs={{0,1},{1,2},{2,3},{3,4},{4,5},{5,6},{6,7},{7,8},{8,9},{9,10},{10,1... | collective-permute-start | bytes 1572872 | tf_op jit(solution)/shard_map/ppermute | solution.py:15
  19.1 0.8 pad_maximum_fusion.1
  19.9 4.3 %collective-permute-start.1 = (bf16[2,8,128,128]{3,2,1,0:T(8,128)(2,1)}, bf16[2,8,128,128]{3,2,1,0:T(8,128)(2,1)S(1)}, u32[]{:S(2)}, u32[]{:S(2)}) collective-permute-start(bf16[2,8,128,128]{3,2,1,0:T(8,128)(2,1)} %pad_maximum_fusion.1), channel_id=1, source_target_pairs={{0,31},{1,0},{2,1},{3,2},{4,3},{5,4},{6,5},{7,6},{8,7},{9,8},{10,9... | collective-permute-start | bytes 1572872 | tf_op jit(solution)/shard_map/ppermute | solution.py:15
  24.2 1.1 slice_bitcast_fusion.1
  25.4 1.9 copy.15
  27.3 2.2 gather_fusion
  29.6 0.1 compare_reduce_fusion
  29.7 0.1 fusion
  29.8 0.1 reshape.16.table_m
  29.9 0.2 select_reduce_fusion
  30.1 0.1 copy.18
  30.3 0.1 add.57.table_q
  30.4 2.1 collective-permute-start.2
  32.4 10.2 %collective-permute-start.3 = (bf16[2,8,128,128]{3,2,1,0:T(8,128)(2,1)}, bf16[2,8,128,128]{3,2,1,0:T(8,128)(2,1)S(1)}, u32[]{:S(2)}, u32[]{:S(2)}) collective-permute-start(bf16[2,8,128,128]{3,2,1,0:T(8,128)(2,1)} %get-tuple-element.26), channel_id=1, source_target_pairs={{0,480},{1,481},{2,482},{3,483},{4,484},{5,485},{6,486},{7,487},{8... | collective-permute-start | bytes 1572872 | tf_op jit(solution)/shard_map/ppermute | solution.py:15
  42.7 5.6 %shard_map.55.acc = f32[4,2,12,128,128]{4,3,2,1,0:T(8,128)S(1)} custom-call(s32[192]{0:T(256)S(1)} %reshape.16.table_m, s32[2304]{0:T(1024)S(1)} %add.57.table_q, bf16[4,2,8,128,128]{4,3,2,1,0:T(8,128)(2,1)S(1)} %copy-done), custom_call_target="tpu_custom_call" | custom-call | flops 4000000000 | bytes 1024 | tf_op jit(solution)/shard_map/pallas_call | solution.py:170
  48.4 12.6 %collective-permute-start.5 = (bf16[1,8,128,128]{3,2,1,0:T(8,128)(2,1)S(1)}, bf16[1,8,128,128]{3,2,1,0:T(8,128)(2,1)S(1)}, u32[]{:S(2)}, u32[]{:S(2)}) collective-permute-start(bf16[1,8,128,128]{3,2,1,0:T(8,128)(2,1)S(1)} %copy-done.3), channel_id=1, source_target_pairs={{0,31},{1,0},{2,1},{3,2},{4,3},{5,4},{6,5},{7,6},{8,7},{9,8},{10,9... | collective-permute-start | bytes 786440 | tf_op jit(solution)/shard_map/ppermute | solution.py:15
  61.0 6.3 %shard_map.56.acc = f32[4,2,12,128,128]{4,3,2,1,0:T(8,128)S(1)} custom-call(s32[192]{0:T(256)S(1)} %reshape.16.table_m, s32[2304]{0:T(1024)S(1)} %add.57.table_q, bf16[4,2,8,128,128]{4,3,2,1,0:T(8,128)(2,1)S(1)} %copy-done, f32[4,2,12,128,128]{4,3,2,1,0:T(8,128)S(1)} %shard_map.55.acc), custom_call_target="tpu_custom_call" | custom-call | flops 4000000000 | bytes 1024 | tf_op jit(solution)/shard_map/pallas_call | solution.py:170
  67.4 1.9 collective-permute-start.4
  69.3 0.1 fusion.6
  69.5 1.9 collective-permute-start.6
  71.5 71.7 %collective-permute-done.2.up = bf16[2,8,128,128]{3,2,1,0:T(8,128)(2,1)S(1)} collective-permute-done((bf16[2,8,128,128]{3,2,1,0:T(8,128)(2,1)}, bf16[2,8,128,128]{3,2,1,0:T(8,128)(2,1)S(1)}, u32[]{:S(2)}, u32[]{:S(2)}) %collective-permute-start.2) | collective-permute-done | bytes 524320 | tf_op jit(solution)/shard_map/ppermute | solution.py:15
  143.2 1.9 collective-permute-start.7
  145.1 5.9 %shard_map.57.acc = f32[4,2,12,128,128]{4,3,2,1,0:T(8,128)S(1)} custom-call(s32[192]{0:T(256)S(1)} %reshape.16.table_m, s32[2304]{0:T(1024)S(1)} %add.57.table_q, bf16[4,2,8,128,128]{4,3,2,1,0:T(8,128)(2,1)S(1)} %copy-done, f32[4,2,12,128,128]{4,3,2,1,0:T(8,128)S(1)} %shard_map.56.acc, bf16[2,8,128,128]{3,2,1,0:T(8,128)(2,1)S(1)} %collective-permute-done.rim_low, ...), custom_call_target="tpu_custom_call" | custom-call | flops 1000000 | bytes 1024 | tf_op jit(solution)/shard_map/pallas_call | solution.py:170
  151.0 6.4 %collective-permute-start.8 = (bf16[8,128,128]{2,1,0:T(8,128)(2,1)S(1)}, bf16[8,128,128]{2,1,0:T(8,128)(2,1)S(1)}, u32[]{:S(2)}, u32[]{:S(2)}) collective-permute-start(bf16[8,128,128]{2,1,0:T(8,128)(2,1)S(1)} %copy-done.2), channel_id=1, source_target_pairs={{0,31},{1,0},{2,1},{3,2},{4,3},{5,4},{6,5},{7,6},{8,7},{9,8},{10,9... | collective-permute-start | bytes 786440 | tf_op jit(solution)/shard_map/ppermute | solution.py:15
  157.5 11.4 %collective-permute-done.4.mid_low = bf16[2,8,128,128]{3,2,1,0:T(8,128)(2,1)S(1)} collective-permute-done((bf16[2,8,128,128]{3,2,1,0:T(8,128)(2,1)S(1)}, bf16[2,8,128,128]{3,2,1,0:T(8,128)(2,1)S(1)}, u32[]{:S(2)}, u32[]{:S(2)}) %collective-permute-start.4) | collective-permute-done | bytes 524320 | tf_op jit(solution)/shard_map/ppermute | solution.py:15
  168.9 3.7 %shard_map.58.acc = f32[4,2,12,128,128]{4,3,2,1,0:T(8,128)S(1)} custom-call(s32[192]{0:T(256)S(1)} %reshape.16.table_m, s32[2304]{0:T(1024)S(1)} %add.57.table_q, bf16[4,2,8,128,128]{4,3,2,1,0:T(8,128)(2,1)S(1)} %copy-done, f32[4,2,12,128,128]{4,3,2,1,0:T(8,128)S(1)} %shard_map.57.acc, bf16[2,8,128,128]{3,2,1,0:T(8,128)(2,1)S(1)} %collective-permute-done.4.mid_low, ...), custom_call_target="tpu_custom_call" | custom-call | flops 5000000000 | bytes 1024 | tf_op jit(solution)/shard_map/pallas_call | solution.py:170
  172.6 36.8 %collective-permute-done.6.up = bf16[2,8,128,128]{3,2,1,0:T(8,128)(2,1)S(1)} collective-permute-done((bf16[2,8,128,128]{3,2,1,0:T(8,128)(2,1)S(1)}, bf16[2,8,128,128]{3,2,1,0:T(8,128)(2,1)S(1)}, u32[]{:S(2)}, u32[]{:S(2)}) %collective-permute-start.6) | collective-permute-done | bytes 524320 | tf_op jit(solution)/shard_map/ppermute | solution.py:15
  209.4 2.6 %shard_map.59 = (bf16[4,2,12,128,128]{4,3,2,1,0:T(8,128)(2,1)}, f32[4,12,128,128]{3,2,1,0:T(8,128)S(1)}) custom-call(s32[192]{0:T(256)S(1)} %reshape.16.table_m, s32[2304]{0:T(1024)S(1)} %add.57.table_q, bf16[4,2,8,128,128]{4,3,2,1,0:T(8,128)(2,1)S(1)} %copy-done, f32[4,2,12,128,128]{4,3,2,1,0:T(8,128)S(1)} %shard_map.58.acc, ...), custom_call_target="tpu_custom_call" | custom-call | flops 1000000 | bytes 1024 | tf_op jit(solution)/shard_map/pallas_call | solution.py:170
  212.0 8.8 %collective-permute-done.8.site = bf16[8,128,128]{2,1,0:T(8,128)(2,1)S(1)} collective-permute-done((bf16[8,128,128]{2,1,0:T(8,128)(2,1)S(1)}, bf16[8,128,128]{2,1,0:T(8,128)(2,1)S(1)}, u32[]{:S(2)}, u32[]{:S(2)}) %collective-permute-start.8) | collective-permute-done | bytes 262176 | tf_op jit(solution)/shard_map/ppermute | solution.py:15
  220.8 2.0 shard_map.60
  (28 shorter events, 0.3 us)
Async XLA Ops:
  0.0 25.4 %copy-start.5 = (s32[24]{0:T(128)S(1)}, s32[24]{0:T(128)}, u32[]{:S(2)}) copy-start(s32[24]{0:T(128)} %constant.50.clone) | copy-start | bytes 292
  0.0 25.4 %copy-start.6 = (s32[24]{0:T(128)S(1)}, s32[24]{0:T(128)}, u32[]{:S(2)}) copy-start(s32[24]{0:T(128)} %constant.49.clone) | copy-start | bytes 292
  0.0 24.2 %copy-start = (bf16[4,2,8,128,128]{4,3,2,1,0:T(8,128)(2,1)S(1)}, bf16[4,2,8,128,128]{4,3,2,1,0:T(8,128)(2,1)}, u32[]{:S(2)}) copy-start(bf16[4,2,8,128,128]{4,3,2,1,0:T(8,128)(2,1)} %own.11) | copy-start | bytes 6291460
  0.0 25.4 %copy-start.1 = (s32[64,64,8]{1,2,0:T(8,128)S(1)}, s32[64,64,8]{1,2,0:T(8,128)}, u32[]{:S(2)}) copy-start(s32[64,64,8]{1,2,0:T(8,128)} %param.6) | copy-start | bytes 393220
  2.5 27.3 %copy-start.4 = (s32[4,2,12]{2,1,0:T(2,128)S(1)}, s32[4,2,12]{2,1,0:T(2,128)}, u32[]{:S(2)}) copy-start(s32[4,2,12]{2,1,0:T(2,128)} %param.7) | copy-start | bytes 1156
  3.4 64.0 %collective-permute-start = (bf16[2,8,128,128]{3,2,1,0:T(8,128)(2,1)}, bf16[2,8,128,128]{3,2,1,0:T(8,128)(2,1)S(1)}, u32[]{:S(2)}, u32[]{:S(2)}) collective-permute-start(bf16[2,8,128,128]{3,2,1,0:T(8,128)(2,1)} %pad_maximum_fusion), channel_id=1, source_target_pairs={{0,1},{1,2},{2,3},{3,4},{4,5},{5,6},{6,7},{7,8},{8,9},{9,10},{10,1... | collective-permute-start | bytes 1572872 | tf_op jit(solution)/shard_map/ppermute | solution.py:15
  19.9 49.4 %collective-permute-start.1 = (bf16[2,8,128,128]{3,2,1,0:T(8,128)(2,1)}, bf16[2,8,128,128]{3,2,1,0:T(8,128)(2,1)S(1)}, u32[]{:S(2)}, u32[]{:S(2)}) collective-permute-start(bf16[2,8,128,128]{3,2,1,0:T(8,128)(2,1)} %pad_maximum_fusion.1), channel_id=1, source_target_pairs={{0,31},{1,0},{2,1},{3,2},{4,3},{5,4},{6,5},{7,6},{8,7},{9,8},{10,9... | collective-permute-start | bytes 1572872 | tf_op jit(solution)/shard_map/ppermute | solution.py:15
  30.4 18.0 %copy-start.3 = (bf16[1,8,128,128]{3,2,1,0:T(8,128)(2,1)S(1)}, bf16[1,8,128,128]{3,2,1,0:T(8,128)(2,1)}, u32[]{:S(2)}) copy-start(bf16[1,8,128,128]{3,2,1,0:T(8,128)(2,1)} %get-tuple-element.29) | copy-start | bytes 786436
  30.4 112.8 %collective-permute-start.2 = (bf16[2,8,128,128]{3,2,1,0:T(8,128)(2,1)}, bf16[2,8,128,128]{3,2,1,0:T(8,128)(2,1)S(1)}, u32[]{:S(2)}, u32[]{:S(2)}) collective-permute-start(bf16[2,8,128,128]{3,2,1,0:T(8,128)(2,1)} %get-tuple-element.25), channel_id=1, source_target_pairs={{0,32},{1,33},{2,34},{3,35},{4,36},{5,37},{6,38},{7,39},{8,40},{9,... | collective-permute-start | bytes 1572872 | tf_op jit(solution)/shard_map/ppermute | solution.py:15
  32.4 112.6 %collective-permute-start.3 = (bf16[2,8,128,128]{3,2,1,0:T(8,128)(2,1)}, bf16[2,8,128,128]{3,2,1,0:T(8,128)(2,1)S(1)}, u32[]{:S(2)}, u32[]{:S(2)}) collective-permute-start(bf16[2,8,128,128]{3,2,1,0:T(8,128)(2,1)} %get-tuple-element.26), channel_id=1, source_target_pairs={{0,480},{1,481},{2,482},{3,483},{4,484},{5,485},{6,486},{7,487},{8... | collective-permute-start | bytes 1572872 | tf_op jit(solution)/shard_map/ppermute | solution.py:15
  48.4 109.1 %collective-permute-start.5 = (bf16[1,8,128,128]{3,2,1,0:T(8,128)(2,1)S(1)}, bf16[1,8,128,128]{3,2,1,0:T(8,128)(2,1)S(1)}, u32[]{:S(2)}, u32[]{:S(2)}) collective-permute-start(bf16[1,8,128,128]{3,2,1,0:T(8,128)(2,1)S(1)} %copy-done.3), channel_id=1, source_target_pairs={{0,31},{1,0},{2,1},{3,2},{4,3},{5,4},{6,5},{7,6},{8,7},{9,8},{10,9... | collective-permute-start | bytes 786440 | tf_op jit(solution)/shard_map/ppermute | solution.py:15
  67.4 101.5 %collective-permute-start.4 = (bf16[2,8,128,128]{3,2,1,0:T(8,128)(2,1)S(1)}, bf16[2,8,128,128]{3,2,1,0:T(8,128)(2,1)S(1)}, u32[]{:S(2)}, u32[]{:S(2)}) collective-permute-start(bf16[2,8,128,128]{3,2,1,0:T(8,128)(2,1)S(1)} %slice_bitcast_fusion), channel_id=1, source_target_pairs={{0,1},{1,2},{2,3},{3,4},{4,5},{5,6},{6,7},{7,8},{8,9},{9,10},{10,1... | collective-permute-start | bytes 1572872 | tf_op jit(solution)/shard_map/ppermute | solution.py:15
  69.5 139.9 %collective-permute-start.6 = (bf16[2,8,128,128]{3,2,1,0:T(8,128)(2,1)S(1)}, bf16[2,8,128,128]{3,2,1,0:T(8,128)(2,1)S(1)}, u32[]{:S(2)}, u32[]{:S(2)}) collective-permute-start(bf16[2,8,128,128]{3,2,1,0:T(8,128)(2,1)S(1)} %pad_maximum_fusion.2), channel_id=1, source_target_pairs={{0,32},{1,33},{2,34},{3,35},{4,36},{5,37},{6,38},{7,39},{8,40},{9,... | collective-permute-start | bytes 1572872 | tf_op jit(solution)/shard_map/ppermute | solution.py:15
  71.4 79.5 %copy-start.2 = (bf16[8,128,128]{2,1,0:T(8,128)(2,1)S(1)}, bf16[8,128,128]{2,1,0:T(8,128)(2,1)}, u32[]{:S(2)}) copy-start(bf16[8,128,128]{2,1,0:T(8,128)(2,1)} %get-tuple-element.31) | copy-start | bytes 786436
  143.2 66.2 %collective-permute-start.7 = (bf16[2,8,128,128]{3,2,1,0:T(8,128)(2,1)S(1)}, bf16[2,8,128,128]{3,2,1,0:T(8,128)(2,1)S(1)}, u32[]{:S(2)}, u32[]{:S(2)}) collective-permute-start(bf16[2,8,128,128]{3,2,1,0:T(8,128)(2,1)S(1)} %pad_maximum_fusion.3), channel_id=1, source_target_pairs={{0,480},{1,481},{2,482},{3,483},{4,484},{5,485},{6,486},{7,487},{8... | collective-permute-start | bytes 1572872 | tf_op jit(solution)/shard_map/ppermute | solution.py:15
  151.0 69.8 %collective-permute-start.8 = (bf16[8,128,128]{2,1,0:T(8,128)(2,1)S(1)}, bf16[8,128,128]{2,1,0:T(8,128)(2,1)S(1)}, u32[]{:S(2)}, u32[]{:S(2)}) collective-permute-start(bf16[8,128,128]{2,1,0:T(8,128)(2,1)S(1)} %copy-done.2), channel_id=1, source_target_pairs={{0,31},{1,0},{2,1},{3,2},{4,3},{5,4},{6,5},{7,6},{8,7},{9,8},{10,9... | collective-permute-start | bytes 786440 | tf_op jit(solution)/shard_map/ppermute | solution.py:15

commit v5 on v2

--- a/solution.py
+++ b/solution.py
@@ -7,7 +7,9 @@
 from jax.sharding import PartitionSpec as P
 
 AXES = ("blk", "rows")
-OWN, SIDE_LOW, SIDE_HIGH, NEAR_LOW, NEAR_HIGH, WRAP, PIECES = 0, 8, 12, 16, 20, 24, 26
+OWN, EARLY_LOW, EARLY_HIGH, EARLY_WRAP, SIDE_LOW, SIDE_HIGH, LATE_LOW, LATE_HIGH, LATE_WRAP, PIECES = (
+    0, 8, 10, 12, 13, 17, 21, 23, 25, 26
+)
 BLOCKS = (12, 128, 128)
 
 
@@ -59,45 +61,43 @@
     return lambda q: ref[(*lead, q)]
 
 
-def every_site(tables, own, pieces_of, write):
+def column_kernel(table_m, table_q, own, acc):
+    def write(x, col, n, total):
+        acc[x, col, n] = total
+
     for x in range(own.shape[0]):
         for col in range(2):
-            accumulate(*tables, own, x, col, pieces_of(x, col), write, 2)
-
-
-def column_kernel(table_m, table_q, own, acc):
-    def pieces_of(x, col):
-        return [(OWN + x * 2 + y, block_from(own, x, y)) for y in range(2)]
-
-    def write(x, col, n, total):
-        acc[x, col, n] = total
-
-    every_site((table_m, table_q), own, pieces_of, write)
+            pieces = [(OWN + x * 2 + y, block_from(own, x, y)) for y in range(2)]
+            accumulate(table_m, table_q, own, x, col, pieces, write, 2)
 
 
 def own_kernel(table_m, table_q, own, acc, out):
-    def pieces_of(x, col):
+    def write(x, col, n, total):
+        out[x, col, n] = acc[x, col, n] + total
+
+    for x in range(own.shape[0]):
         around = [near for near in (x - 1, x + 1) if 0 <= near < own.shape[0]]
-        return [(OWN + near * 2 + y, block_from(own, near, y)) for near in around for y in range(2)]
-
-    def write(x, col, n, total):
-        out[x, col, n] = acc[x, col, n] + total
-
-    every_site((table_m, table_q), own, pieces_of, write)
-
-
-def rim_kernel(table_m, table_q, own, acc, rim_low, rim_high, out):
+        for col in range(2):
+            pieces = [(OWN + near * 2 + y, block_from(own, near, y)) for near in around for y in range(2)]
+            accumulate(table_m, table_q, own, x, col, pieces, write, 2)
+
+
+def rim_kernel(table_m, table_q, own, acc, rim_low, rim_high, up, down, wrap, out):
     cells_x = own.shape[0]
     rims = (rim_low, rim_high)
 
-    def pieces_of(x, col):
-        at = int(x >= cells_x // 2)
-        return [((SIDE_LOW, SIDE_HIGH)[col] + at * (cells_x - 1), block_from(rims[col], at))]
-
     def write(x, col, n, total):
         out[x, col, n] = acc[x, col, n] + total
 
-    every_site((table_m, table_q), own, pieces_of, write)
+    for x in range(cells_x):
+        for col in range(2):
+            at = int(x >= cells_x // 2)
+            pieces = [((SIDE_LOW, SIDE_HIGH)[col] + at * (cells_x - 1), block_from(rims[col], at))]
+            if x in (0, cells_x - 1):
+                first, near = ((EARLY_LOW, up), (EARLY_HIGH, down))[at]
+                pieces += [(first + y, block_from(near, y)) for y in range(2)]
+                pieces.append((EARLY_WRAP, block_from(wrap)))
+            accumulate(table_m, table_q, own, x, col, pieces, write, 2)
 
 
 def middle_kernel(table_m, table_q, own, acc, mid_low, mid_high, out, rest, held, sems):
@@ -127,7 +127,7 @@
         copy.wait()
 
 
-def edge_kernel(table_m, table_q, own, rest, near_low, near_high, wrap, begun, out, held, sems):
+def edge_kernel(table_m, table_q, own, rest, up, down, wrap, begun, out, held, sems):
     cells_x = own.shape[0]
 
     def write(x, col, n, total):
@@ -136,10 +136,10 @@
 
     copies = []
     for at, x in enumerate((0, cells_x - 1)):
-        first, near = ((NEAR_LOW, near_low), (NEAR_HIGH, near_high))[at]
-        for col in range(2):
-            pieces = [(first + y, block_from(near, y)) for y in range(4)]
-            pieces += [(WRAP + y, block_from(wrap, y)) for y in range(2)]
+        first, late = ((LATE_LOW, up), (LATE_HIGH, down))[at]
+        for col in range(2):
+            pieces = [(first + y, block_from(late, y)) for y in range(2)]
+            pieces.append((LATE_WRAP, block_from(wrap)))
             accumulate(table_m, table_q, own, x, col, pieces, write, 6)
             copies.append(pltpu.make_async_copy(held.at[at, col], out.at[x, col], sems.at[at, col]))
             copies[-1].start()
@@ -178,13 +178,14 @@
     at_blk, at_row = lax.axis_index("blk"), lax.axis_index("rows")
     first, last = at_blk == 0, at_blk == lax.axis_size("blk") - 1
     near = [(x, y) for x in range(cells_x) for y in range(cells_y)]
-    wide = [-1] * 4 + [cells_x] * 4
+    wide = [-1, -1, cells_x, cells_x]
     sides, side_y = list(range(cells_x)) * 2, [-1] * cells_x + [cells_y] * cells_x
-    dx = [x for x, _ in near] + sides + wide + [0, 0]
-    plain = [y for _, y in near] + side_y + [0, 1, -1, 2] * 2 + [2, 1]
-    turned = [y for _, y in near] + side_y + [-2, -1, -3, 0] * 2 + [2, 1]
+    dx = [x for x, _ in near] + wide + [0] + sides + wide + [0]
+    plain = [y for _, y in near] + [0, 1] * 2 + [2] + side_y + [-1, 2] * 2 + [1]
+    turned = [y for _, y in near] + [-2, -1] * 2 + [2] + side_y + [-3, 0] * 2 + [1]
     dx, plain, turned = (np.array(v, np.int32) for v in (dx, plain, turned))
-    is_wrap = np.arange(PIECES) >= WRAP
+    numbers = np.arange(PIECES)
+    is_wrap = (numbers == EARLY_WRAP) | (numbers == LATE_WRAP)
     dx = jnp.where(is_wrap, jnp.where(first, -1, cells_x), dx)
     swapped = ((dx < 0) & first) | ((dx >= cells_x) & last)
     dy = jnp.where(swapped, turned, plain)
@@ -218,6 +219,9 @@
     rim_high = along_y(jnp.stack([p_vals[0, 0], p_vals[last, 0]]), -1)
 
     tables = make_tables(p_cols, c_cols, cells_x, cells_y)
+    tables, edges = tie((tables, (p_vals[last], p_vals[0])))
+    single = jnp.where(first, edges[1][0], edges[0][0])
+    early = [along_x(edges[0], 1), along_x(edges[1], -1), past_edge(single)]
     acc = run_kernel(column_kernel, tables, p_vals, [], 4 * 10**9)
     acc, middle = tie((acc, (p_vals[1:last, 1], p_vals[1:last, 0])))
     mid_low = along_y(middle[0], 1)
@@ -225,14 +229,13 @@
 
     acc = run_kernel(own_kernel, tables, p_vals, [acc], 4 * 10**9)
     acc, rim_low, rim_high = tie((acc, rim_low, rim_high))
-    below = jnp.stack([p_vals[0, 0], p_vals[0, 1], rim_low[0], rim_high[0]])
-    above = jnp.stack([p_vals[last, 0], p_vals[last, 1], rim_low[1], rim_high[1]])
-    pair = jnp.where(first, below[0:3:2], above[0:3:2])
-    near = [along_x(above, 1), along_x(below, -1), past_edge(pair)]
-
-    acc = run_kernel(rim_kernel, tables, p_vals, [acc, rim_low, rim_high], 10**6)
-    begun, rest = run_kernel(middle_kernel, tables, p_vals, [acc, mid_low, mid_high], 5 * 10**10, middle=True)
-    return run_kernel(edge_kernel, tables, p_vals, [rest, *near], 10**6, begun=begun)
+    single = jnp.where(first, rim_low[0], rim_low[1])
+    above, below = (jnp.stack([rim_low[at], rim_high[at]]) for at in (1, 0))
+    late = [along_x(above, 1), along_x(below, -1), past_edge(single)]
+
+    acc = run_kernel(rim_kernel, tables, p_vals, [acc, rim_low, rim_high, *early], 10**6)
+    begun, rest = run_kernel(middle_kernel, tables, p_vals, [acc, mid_low, mid_high], 10**6, middle=True)
+    return run_kernel(edge_kernel, tables, p_vals, [rest, *late], 10**6, begun=begun)
 
 
 def solution(mesh):

time: 220 us -> 231 us (1.050)
  waiting for transfers between devices: 58.7 us -> 128 us
  starting transfers between devices: 126 us -> 68.4 us
    ppermute x7 -> x10, waiting for transfers between devices: 58.7 us -> 128 us  [send(): lax.ppermute(value, AXES, [(a[0] * n_rows + a[1], b[0] * n_rows + b[1]) f...]
    ppermute x7 -> x10, starting transfers between devices: 126 us -> 68.4 us  [send(): lax.ppermute(value, AXES, [(a[0] * n_rows + a[1], b[0] * n_rows + b[1]) f...]
  transfers between devices with their start and end apart: 7 -> 10, of which waited for: 1 -> 2; matrix products, arithmetic and copies ran while one was open for 4% -> 4% of each run, Pallas kernels for 9% -> 9%
where the time goes in v5:
time: 231 us
  waiting for transfers between devices  128 us (55%)
  starting transfers between devices  68.4 us (30%)
  Pallas kernels  23.4 us (10%)
  local copies, waits for them, and re-layouts  7.22 us (3%)
  other arithmetic  3.38 us (1%)
    ppermute x10, waiting for transfers between devices, send(): lax.ppermute(value, AXES, [(a[0] * n_rows + a[1], b[0] * n_rows + b[1]) f...  128 us
    ppermute x10, starting transfers between devices, send(): lax.ppermute(value, AXES, [(a[0] * n_rows + a[1], b[0] * n_rows + b[1]) f...  68.4 us
    pallas_call x5, Pallas kernels, run_kernel(): pl.pallas_call(body, out_shape=out_shape, in_specs=in_specs, out_specs=ou...  23.4 us
  transfers between devices with their start and end apart: 10, of which 2 were waited for; matrix products, arithmetic and copies ran while one was open for 4% of the time, Pallas kernels for 9%

profile of v5, /device:TPU:24, one launch (start us, length us, event | category | flops | bytes accessed | tf_op | source)
XLA Modules:
  0.0 230.8 jit_solution(1307594824050739388)
XLA Ops:
  0.0 1.4 slice_bitcast_fusion.5
  1.5 0.8 pad_maximum_fusion
  2.3 15.7 %collective-permute-start = (bf16[2,8,128,128]{3,2,1,0:T(8,128)(2,1)}, bf16[2,8,128,128]{3,2,1,0:T(8,128)(2,1)S(1)}, u32[]{:S(2)}, u32[]{:S(2)}) collective-permute-start(bf16[2,8,128,128]{3,2,1,0:T(8,128)(2,1)} %pad_maximum_fusion), channel_id=1, source_target_pairs={{0,1},{1,2},{2,3},{3,4},{4,5},{5,6},{6,7},{7,8},{8,9},{9,10},{10,1... | collective-permute-start | bytes 1572872 | tf_op jit(solution)/shard_map/ppermute | solution.py:17
  18.1 0.8 pad_maximum_fusion.1
  18.9 4.3 %collective-permute-start.1 = (bf16[2,8,128,128]{3,2,1,0:T(8,128)(2,1)}, bf16[2,8,128,128]{3,2,1,0:T(8,128)(2,1)S(1)}, u32[]{:S(2)}, u32[]{:S(2)}) collective-permute-start(bf16[2,8,128,128]{3,2,1,0:T(8,128)(2,1)} %pad_maximum_fusion.1), channel_id=1, source_target_pairs={{0,31},{1,0},{2,1},{3,2},{4,3},{5,4},{6,5},{7,6},{8,7},{9,8},{10,9... | collective-permute-start | bytes 1572872 | tf_op jit(solution)/shard_map/ppermute | solution.py:17
  23.2 1.1 slice_bitcast_fusion.2
  24.4 1.9 copy.20
  26.3 2.2 gather_fusion
  28.5 0.1 copy.21
  28.6 0.1 compare_reduce_fusion
  28.7 0.1 fusion
  28.8 0.1 reshape.20.table_m
  28.9 0.2 select_reduce_fusion
  29.1 0.1 copy.23
  29.3 0.1 add.57.table_q
  29.4 1.9 collective-permute-start.2
  31.3 4.8 %collective-permute-start.3 = (bf16[2,8,128,128]{3,2,1,0:T(8,128)(2,1)}, bf16[2,8,128,128]{3,2,1,0:T(8,128)(2,1)S(1)}, u32[]{:S(2)}, u32[]{:S(2)}) collective-permute-start(bf16[2,8,128,128]{3,2,1,0:T(8,128)(2,1)} %get-tuple-element.24), channel_id=1, source_target_pairs={{0,481},{1,482},{2,483},{3,484},{4,485},{5,486},{6,487},{7,488},{8... | collective-permute-start | bytes 1572872 | tf_op jit(solution)/shard_map/ppermute | solution.py:17
  36.1 1.1 select_bitcast_fusion.1
  37.2 5.5 %collective-permute-start.4 = (bf16[8,128,128]{2,1,0:T(8,128)(2,1)S(1)}, bf16[8,128,128]{2,1,0:T(8,128)(2,1)S(1)}, u32[]{:S(2)}, u32[]{:S(2)}) collective-permute-start(bf16[8,128,128]{2,1,0:T(8,128)(2,1)S(1)} %select_bitcast_fusion.1), channel_id=1, source_target_pairs={{480,31},{481,0},{482,1},{483,2},{484,3},{485,4},{486,5},{487,6},{... | collective-permute-start | bytes 786440 | tf_op jit(solution)/shard_map/ppermute | solution.py:17
  42.7 5.6 %shard_map.73.acc = f32[4,2,12,128,128]{4,3,2,1,0:T(8,128)S(1)} custom-call(s32[208]{0:T(256)S(1)} %reshape.20.table_m, s32[2496]{0:T(1024)S(1)} %add.57.table_q, bf16[4,2,8,128,128]{4,3,2,1,0:T(8,128)(2,1)S(1)} %copy-done), custom_call_target="tpu_custom_call" | custom-call | flops 4000000000 | bytes 1024 | tf_op jit(solution)/shard_map/pallas_call | solution.py:164
  48.4 0.1 slice_bitcast_fusion
  48.5 6.4 %shard_map.74.acc = f32[4,2,12,128,128]{4,3,2,1,0:T(8,128)S(1)} custom-call(s32[208]{0:T(256)S(1)} %reshape.20.table_m, s32[2496]{0:T(1024)S(1)} %add.57.table_q, bf16[4,2,8,128,128]{4,3,2,1,0:T(8,128)(2,1)S(1)} %copy-done, f32[4,2,12,128,128]{4,3,2,1,0:T(8,128)S(1)} %shard_map.73.acc), custom_call_target="tpu_custom_call" | custom-call | flops 4000000000 | bytes 1024 | tf_op jit(solution)/shard_map/pallas_call | solution.py:164
  54.9 7.6 %collective-permute-start.5 = (bf16[2,8,128,128]{3,2,1,0:T(8,128)(2,1)S(1)}, bf16[2,8,128,128]{3,2,1,0:T(8,128)(2,1)S(1)}, u32[]{:S(2)}, u32[]{:S(2)}) collective-permute-start(bf16[2,8,128,128]{3,2,1,0:T(8,128)(2,1)S(1)} %get-tuple-element.25), channel_id=1, source_target_pairs={{0,1},{1,2},{2,3},{3,4},{4,5},{5,6},{6,7},{7,8},{8,9},{9,10},{10,1... | collective-permute-start | bytes 1572872 | tf_op jit(solution)/shard_map/ppermute | solution.py:17
  62.5 52.3 %collective-permute-done.1.rim_high = bf16[2,8,128,128]{3,2,1,0:T(8,128)(2,1)S(1)} collective-permute-done((bf16[2,8,128,128]{3,2,1,0:T(8,128)(2,1)}, bf16[2,8,128,128]{3,2,1,0:T(8,128)(2,1)S(1)}, u32[]{:S(2)}, u32[]{:S(2)}) %collective-permute-start.1) | collective-permute-done | bytes 524320 | tf_op jit(solution)/shard_map/ppermute | solution.py:17
  114.8 16.2 %collective-permute-start.6 = (bf16[2,8,128,128]{3,2,1,0:T(8,128)(2,1)S(1)}, bf16[2,8,128,128]{3,2,1,0:T(8,128)(2,1)S(1)}, u32[]{:S(2)}, u32[]{:S(2)}) collective-permute-start(bf16[2,8,128,128]{3,2,1,0:T(8,128)(2,1)S(1)} %get-tuple-element.26), channel_id=1, source_target_pairs={{0,31},{1,0},{2,1},{3,2},{4,3},{5,4},{6,5},{7,6},{8,7},{9,8},{10,9... | collective-permute-start | bytes 1572872 | tf_op jit(solution)/shard_map/ppermute | solution.py:17
  131.3 75.6 %collective-permute-done.4.wrap = bf16[8,128,128]{2,1,0:T(8,128)(2,1)S(1)} collective-permute-done((bf16[8,128,128]{2,1,0:T(8,128)(2,1)S(1)}, bf16[8,128,128]{2,1,0:T(8,128)(2,1)S(1)}, u32[]{:S(2)}, u32[]{:S(2)}) %collective-permute-start.4) | collective-permute-done | bytes 262176 | tf_op jit(solution)/shard_map/ppermute | solution.py:17
  206.9 1.9 collective-permute-start.7
  208.8 6.0 %collective-permute-start.8 = (bf16[2,8,128,128]{3,2,1,0:T(8,128)(2,1)S(1)}, bf16[2,8,128,128]{3,2,1,0:T(8,128)(2,1)S(1)}, u32[]{:S(2)}, u32[]{:S(2)}) collective-permute-start(bf16[2,8,128,128]{3,2,1,0:T(8,128)(2,1)S(1)} %pad_maximum_fusion.3), channel_id=1, source_target_pairs={{0,481},{1,482},{2,483},{3,484},{4,485},{5,486},{6,487},{7,488},{8... | collective-permute-start | bytes 1572872 | tf_op jit(solution)/shard_map/ppermute | solution.py:17
  214.8 4.5 %collective-permute-start.9 = (bf16[8,128,128]{2,1,0:T(8,128)(2,1)S(1)}, bf16[8,128,128]{2,1,0:T(8,128)(2,1)S(1)}, u32[]{:S(2)}, u32[]{:S(2)}) collective-permute-start(bf16[8,128,128]{2,1,0:T(8,128)(2,1)S(1)} %get-tuple-element.39), channel_id=1, source_target_pairs={{480,31},{481,0},{482,1},{483,2},{484,3},{485,4},{486,5},{487,6},{... | collective-permute-start | bytes 786440 | tf_op jit(solution)/shard_map/ppermute | solution.py:17
  219.3 6.1 %shard_map.75.acc = f32[4,2,12,128,128]{4,3,2,1,0:T(8,128)S(1)} custom-call(s32[208]{0:T(256)S(1)} %reshape.20.table_m, s32[2496]{0:T(1024)S(1)} %add.57.table_q, bf16[4,2,8,128,128]{4,3,2,1,0:T(8,128)(2,1)S(1)} %copy-done, f32[4,2,12,128,128]{4,3,2,1,0:T(8,128)S(1)} %shard_map.74.acc, bf16[2,8,128,128]{3,2,1,0:T(8,128)(2,1)S(1)} %collective-permute-done.rim_low, ...), custom_call_target="tpu_custom_call" | custom-call | flops 1000000 | bytes 1024 | tf_op jit(solution)/shard_map/pallas_call | solution.py:164
  225.4 2.7 %shard_map.76 = (bf16[4,2,12,128,128]{4,3,2,1,0:T(8,128)(2,1)}, f32[2,2,12,128,128]{4,3,2,1,0:T(8,128)S(1)}) custom-call(s32[208]{0:T(256)S(1)} %reshape.20.table_m, s32[2496]{0:T(1024)S(1)} %add.57.table_q, bf16[4,2,8,128,128]{4,3,2,1,0:T(8,128)(2,1)S(1)} %copy-done, f32[4,2,12,128,128]{4,3,2,1,0:T(8,128)S(1)} %shard_map.75.acc, ...), custom_call_target="tpu_custom_call" | custom-call | flops 1000000 | bytes 1024 | tf_op jit(solution)/shard_map/pallas_call | solution.py:164
  228.2 2.6 %shard_map.77 = bf16[4,2,12,128,128]{4,3,2,1,0:T(8,128)(2,1)} custom-call(s32[208]{0:T(256)S(1)} %reshape.20.table_m, s32[2496]{0:T(1024)S(1)} %add.57.table_q, bf16[4,2,8,128,128]{4,3,2,1,0:T(8,128)(2,1)S(1)} %copy-done, f32[2,2,12,128,128]{4,3,2,1,0:T(8,128)S(1)} %get-tuple-element.27.rest, ...), custom_call_target="tpu_custom_call", output_to_operand_aliasing={{}: (7, {})} | custom-call | flops 1000000 | bytes 1024 | tf_op jit(solution)/shard_map/pallas_call | solution.py:164
  (32 shorter events, 0.3 us)
Async XLA Ops:
  0.0 24.3 %copy-start.3 = (pred[26]{0:T(512)(128)(4,1)S(1)}, pred[26]{0:T(512)(128)(4,1)}, u32[]{:S(2)}) copy-start(pred[26]{0:T(512)(128)(4,1)} %constant.58.clone) | copy-start | bytes 82
  0.0 24.3 %copy-start.4 = (s32[26]{0:T(128)S(1)}, s32[26]{0:T(128)}, u32[]{:S(2)}) copy-start(s32[26]{0:T(128)} %constant.61.clone) | copy-start | bytes 316
  0.0 24.3 %copy-start.5 = (s32[26]{0:T(128)S(1)}, s32[26]{0:T(128)}, u32[]{:S(2)}) copy-start(s32[26]{0:T(128)} %constant.60.clone) | copy-start | bytes 316
  0.0 24.3 %copy-start.6 = (s32[26]{0:T(128)S(1)}, s32[26]{0:T(128)}, u32[]{:S(2)}) copy-start(s32[26]{0:T(128)} %constant.59.clone) | copy-start | bytes 316
  0.0 23.2 %copy-start = (bf16[4,2,8,128,128]{4,3,2,1,0:T(8,128)(2,1)S(1)}, bf16[4,2,8,128,128]{4,3,2,1,0:T(8,128)(2,1)}, u32[]{:S(2)}) copy-start(bf16[4,2,8,128,128]{4,3,2,1,0:T(8,128)(2,1)} %own.9) | copy-start | bytes 6291460
  0.0 24.4 %copy-start.1 = (s32[64,64,8]{1,2,0:T(8,128)S(1)}, s32[64,64,8]{1,2,0:T(8,128)}, u32[]{:S(2)}) copy-start(s32[64,64,8]{1,2,0:T(8,128)} %param.8) | copy-start | bytes 393220
  1.5 27.4 %copy-start.2 = (s32[4,2,12]{2,1,0:T(2,128)S(1)}, s32[4,2,12]{2,1,0:T(2,128)}, u32[]{:S(2)}) copy-start(s32[4,2,12]{2,1,0:T(2,128)} %param.9) | copy-start | bytes 1156
  2.3 52.5 %collective-permute-start = (bf16[2,8,128,128]{3,2,1,0:T(8,128)(2,1)}, bf16[2,8,128,128]{3,2,1,0:T(8,128)(2,1)S(1)}, u32[]{:S(2)}, u32[]{:S(2)}) collective-permute-start(bf16[2,8,128,128]{3,2,1,0:T(8,128)(2,1)} %pad_maximum_fusion), channel_id=1, source_target_pairs={{0,1},{1,2},{2,3},{3,4},{4,5},{5,6},{6,7},{7,8},{8,9},{9,10},{10,1... | collective-permute-start | bytes 1572872 | tf_op jit(solution)/shard_map/ppermute | solution.py:17
  18.9 95.9 %collective-permute-start.1 = (bf16[2,8,128,128]{3,2,1,0:T(8,128)(2,1)}, bf16[2,8,128,128]{3,2,1,0:T(8,128)(2,1)S(1)}, u32[]{:S(2)}, u32[]{:S(2)}) collective-permute-start(bf16[2,8,128,128]{3,2,1,0:T(8,128)(2,1)} %pad_maximum_fusion.1), channel_id=1, source_target_pairs={{0,31},{1,0},{2,1},{3,2},{4,3},{5,4},{6,5},{7,6},{8,7},{9,8},{10,9... | collective-permute-start | bytes 1572872 | tf_op jit(solution)/shard_map/ppermute | solution.py:17
  29.4 179.4 %collective-permute-start.2 = (bf16[2,8,128,128]{3,2,1,0:T(8,128)(2,1)}, bf16[2,8,128,128]{3,2,1,0:T(8,128)(2,1)S(1)}, u32[]{:S(2)}, u32[]{:S(2)}) collective-permute-start(bf16[2,8,128,128]{3,2,1,0:T(8,128)(2,1)} %get-tuple-element.23), channel_id=1, source_target_pairs={{0,32},{1,33},{2,34},{3,35},{4,36},{5,37},{6,38},{7,39},{8,40},{9,... | collective-permute-start | bytes 1572872 | tf_op jit(solution)/shard_map/ppermute | solution.py:17
  31.3 183.5 %collective-permute-start.3 = (bf16[2,8,128,128]{3,2,1,0:T(8,128)(2,1)}, bf16[2,8,128,128]{3,2,1,0:T(8,128)(2,1)S(1)}, u32[]{:S(2)}, u32[]{:S(2)}) collective-permute-start(bf16[2,8,128,128]{3,2,1,0:T(8,128)(2,1)} %get-tuple-element.24), channel_id=1, source_target_pairs={{0,481},{1,482},{2,483},{3,484},{4,485},{5,486},{6,487},{7,488},{8... | collective-permute-start | bytes 1572872 | tf_op jit(solution)/shard_map/ppermute | solution.py:17
  37.2 169.7 %collective-permute-start.4 = (bf16[8,128,128]{2,1,0:T(8,128)(2,1)S(1)}, bf16[8,128,128]{2,1,0:T(8,128)(2,1)S(1)}, u32[]{:S(2)}, u32[]{:S(2)}) collective-permute-start(bf16[8,128,128]{2,1,0:T(8,128)(2,1)S(1)} %select_bitcast_fusion.1), channel_id=1, source_target_pairs={{480,31},{481,0},{482,1},{483,2},{484,3},{485,4},{486,5},{487,6},{... | collective-permute-start | bytes 786440 | tf_op jit(solution)/shard_map/ppermute | solution.py:17
  54.9 170.5 %collective-permute-start.5 = (bf16[2,8,128,128]{3,2,1,0:T(8,128)(2,1)S(1)}, bf16[2,8,128,128]{3,2,1,0:T(8,128)(2,1)S(1)}, u32[]{:S(2)}, u32[]{:S(2)}) collective-permute-start(bf16[2,8,128,128]{3,2,1,0:T(8,128)(2,1)S(1)} %get-tuple-element.25), channel_id=1, source_target_pairs={{0,1},{1,2},{2,3},{3,4},{4,5},{5,6},{6,7},{7,8},{8,9},{9,10},{10,1... | collective-permute-start | bytes 1572872 | tf_op jit(solution)/shard_map/ppermute | solution.py:17
  114.8 110.6 %collective-permute-start.6 = (bf16[2,8,128,128]{3,2,1,0:T(8,128)(2,1)S(1)}, bf16[2,8,128,128]{3,2,1,0:T(8,128)(2,1)S(1)}, u32[]{:S(2)}, u32[]{:S(2)}) collective-permute-start(bf16[2,8,128,128]{3,2,1,0:T(8,128)(2,1)S(1)} %get-tuple-element.26), channel_id=1, source_target_pairs={{0,31},{1,0},{2,1},{3,2},{4,3},{5,4},{6,5},{7,6},{8,7},{9,8},{10,9... | collective-permute-start | bytes 1572872 | tf_op jit(solution)/shard_map/ppermute | solution.py:17
  206.9 21.2 %collective-permute-start.7 = (bf16[2,8,128,128]{3,2,1,0:T(8,128)(2,1)S(1)}, bf16[2,8,128,128]{3,2,1,0:T(8,128)(2,1)S(1)}, u32[]{:S(2)}, u32[]{:S(2)}) collective-permute-start(bf16[2,8,128,128]{3,2,1,0:T(8,128)(2,1)S(1)} %pad_maximum_fusion.2), channel_id=1, source_target_pairs={{0,32},{1,33},{2,34},{3,35},{4,36},{5,37},{6,38},{7,39},{8,40},{9,... | collective-permute-start | bytes 1572872 | tf_op jit(solution)/shard_map/ppermute | solution.py:17
  208.8 19.3 %collective-permute-start.8 = (bf16[2,8,128,128]{3,2,1,0:T(8,128)(2,1)S(1)}, bf16[2,8,128,128]{3,2,1,0:T(8,128)(2,1)S(1)}, u32[]{:S(2)}, u32[]{:S(2)}) collective-permute-start(bf16[2,8,128,128]{3,2,1,0:T(8,128)(2,1)S(1)} %pad_maximum_fusion.3), channel_id=1, source_target_pairs={{0,481},{1,482},{2,483},{3,484},{4,485},{5,486},{6,487},{7,488},{8... | collective-permute-start | bytes 1572872 | tf_op jit(solution)/shard_map/ppermute | solution.py:17
  214.8 13.3 %collective-permute-start.9 = (bf16[8,128,128]{2,1,0:T(8,128)(2,1)S(1)}, bf16[8,128,128]{2,1,0:T(8,128)(2,1)S(1)}, u32[]{:S(2)}, u32[]{:S(2)}) collective-permute-start(bf16[8,128,128]{2,1,0:T(8,128)(2,1)S(1)} %get-tuple-element.39), channel_id=1, source_target_pairs={{480,31},{481,0},{482,1},{483,2},{484,3},{485,4},{486,5},{487,6},{... | collective-permute-start | bytes 786440 | tf_op jit(solution)/shard_map/ppermute | solution.py:17

commit v6 on v2

--- a/solution.py
+++ b/solution.py
@@ -7,7 +7,7 @@
 from jax.sharding import PartitionSpec as P
 
 AXES = ("blk", "rows")
-OWN, SIDE_LOW, SIDE_HIGH, NEAR_LOW, NEAR_HIGH, WRAP, PIECES = 0, 8, 12, 16, 20, 24, 26
+OWN, SIDE_LOW, SIDE_HIGH, NEAR_LOW, NEAR_HIGH, PIECES = 0, 8, 12, 16, 20, 24
 BLOCKS = (12, 128, 128)
 
 
@@ -20,17 +20,7 @@
 
 
 def moves_x(shift, n_blk, n_rows):
-    moves = []
-    for b in range(n_blk):
-        for r in range(n_rows):
-            inside = 0 <= b + shift < n_blk
-            moves.append(((b, r), ((b + shift) % n_blk, r if inside else (r + 1) % n_rows)))
-    return moves
-
-
-def moves_wrap(n_blk, n_rows):
-    edges = ((n_blk - 1, 0), (0, n_blk - 1))
-    return [((b, r), (to, (r - 1) % n_rows)) for b, to in edges for r in range(n_rows)]
+    return [((b, r), ((b + shift) % n_blk, r)) for b in range(n_blk) for r in range(n_rows)]
 
 
 def accumulate(table_m, table_q, own, x, col, pieces, write, unroll):
@@ -127,7 +117,7 @@
         copy.wait()
 
 
-def edge_kernel(table_m, table_q, own, rest, near_low, near_high, wrap, begun, out, held, sems):
+def edge_kernel(table_m, table_q, own, rest, near_low, near_high, begun, out, held, sems):
     cells_x = own.shape[0]
 
     def write(x, col, n, total):
@@ -139,7 +129,6 @@
         first, near = ((NEAR_LOW, near_low), (NEAR_HIGH, near_high))[at]
         for col in range(2):
             pieces = [(first + y, block_from(near, y)) for y in range(4)]
-            pieces += [(WRAP + y, block_from(wrap, y)) for y in range(2)]
             accumulate(table_m, table_q, own, x, col, pieces, write, 6)
             copies.append(pltpu.make_async_copy(held.at[at, col], out.at[x, col], sems.at[at, col]))
             copies[-1].start()
@@ -176,23 +165,15 @@
 def make_tables(p_cols, c_cols, cells_x, cells_y):
     total_x, total_y, blocks = p_cols.shape
     at_blk, at_row = lax.axis_index("blk"), lax.axis_index("rows")
-    first, last = at_blk == 0, at_blk == lax.axis_size("blk") - 1
     near = [(x, y) for x in range(cells_x) for y in range(cells_y)]
     wide = [-1] * 4 + [cells_x] * 4
     sides, side_y = list(range(cells_x)) * 2, [-1] * cells_x + [cells_y] * cells_x
-    dx = [x for x, _ in near] + sides + wide + [0, 0]
-    plain = [y for _, y in near] + side_y + [0, 1, -1, 2] * 2 + [2, 1]
-    turned = [y for _, y in near] + side_y + [-2, -1, -3, 0] * 2 + [2, 1]
-    dx, plain, turned = (np.array(v, np.int32) for v in (dx, plain, turned))
-    is_wrap = np.arange(PIECES) >= WRAP
-    dx = jnp.where(is_wrap, jnp.where(first, -1, cells_x), dx)
-    swapped = ((dx < 0) & first) | ((dx >= cells_x) & last)
-    dy = jnp.where(swapped, turned, plain)
+    dx = np.array([x for x, _ in near] + sides + wide, np.int32)
+    dy = np.array([y for _, y in near] + side_y + [0, 1, -1, cells_y] * 2, np.int32)
     site_x = (at_blk * cells_x + dx + total_x) % total_x
     site_y = (at_row * cells_y + dy + total_y) % total_y
     ids = site_x * total_y + site_y
     cols = p_cols.reshape(total_x * total_y, blocks)[ids]
-    ids = jnp.where(is_wrap & ~(first | last), -1, ids)
     own = cols[: cells_x * cells_y]
     slots = jnp.arange(blocks, dtype=jnp.int32)
     is_left = own[:, None, :] == ids[None, :, None]
@@ -208,10 +189,8 @@
     cells_x, cells_y = p_vals.shape[:2]
     n_blk, n_rows = lax.axis_size("blk"), lax.axis_size("rows")
     last = cells_x - 1
-    first = lax.axis_index("blk") == 0
     along_y = lambda value, shift: send(value, moves_y(shift, n_blk, n_rows), n_rows)
     along_x = lambda value, shift: send(value, moves_x(shift, n_blk, n_rows), n_rows)
-    past_edge = lambda value: send(value, moves_wrap(n_blk, n_rows), n_rows)
     tie = lax.optimization_barrier
 
     rim_low = along_y(jnp.stack([p_vals[0, 1], p_vals[last, 1]]), 1)
@@ -227,8 +206,7 @@
     acc, rim_low, rim_high = tie((acc, rim_low, rim_high))
     below = jnp.stack([p_vals[0, 0], p_vals[0, 1], rim_low[0], rim_high[0]])
     above = jnp.stack([p_vals[last, 0], p_vals[last, 1], rim_low[1], rim_high[1]])
-    pair = jnp.where(first, below[0:3:2], above[0:3:2])
-    near = [along_x(above, 1), along_x(below, -1), past_edge(pair)]
+    near = [along_x(above, 1), along_x(below, -1)]
 
     acc = run_kernel(rim_kernel, tables, p_vals, [acc, rim_low, rim_high], 10**6)
     begun, rest = run_kernel(middle_kernel, tables, p_vals, [acc, mid_low, mid_high], 5 * 10**10, middle=True)

time: 220 us -> 227 us (1.032)
  waiting for transfers between devices: 58.7 us -> 81.7 us
  starting transfers between devices: 126 us -> 109 us
    ppermute x7 -> x6, waiting for transfers between devices: 58.7 us -> 81.7 us  [send(): lax.ppermute(value, AXES, [(a[0] * n_rows + a[1], b[0] * n_rows + b[1]) f...]
    ppermute x7 -> x6, starting transfers between devices: 126 us -> 109 us  [send(): lax.ppermute(value, AXES, [(a[0] * n_rows + a[1], b[0] * n_rows + b[1]) f...]
  transfers between devices with their start and end apart: 7 -> 6, of which waited for: 1 -> 2; matrix products, arithmetic and copies ran while one was open for 4% -> 4% of each run, Pallas kernels for 9% -> 9%
where the time goes in v6:
time: 227 us; the launch traced here: 225 us
  starting transfers between devices  109 us (48%)
  waiting for transfers between devices  81.7 us (36%)
  Pallas kernels  22.7 us (10%)
  local copies, waits for them, and re-layouts  8.65 us (4%)
  other arithmetic  3.05 us (1%)
    ppermute x6, starting transfers between devices, send(): lax.ppermute(value, AXES, [(a[0] * n_rows + a[1], b[0] * n_rows + b[1]) f...  109 us
    ppermute x6, waiting for transfers between devices, send(): lax.ppermute(value, AXES, [(a[0] * n_rows + a[1], b[0] * n_rows + b[1]) f...  81.7 us
    pallas_call x5, Pallas kernels, run_kernel(): pl.pallas_call(body, out_shape=out_shape, in_specs=in_specs, out_specs=ou...  22.7 us
  transfers between devices with their start and end apart: 6, of which 2 were waited for; matrix products, arithmetic and copies ran while one was open for 4% of the time, Pallas kernels for 9%

profile of v6, /device:TPU:24, one launch (start us, length us, event | category | flops | bytes accessed | tf_op | source)
XLA Modules:
  0.0 225.5 jit_solution(13284900474201831456)
XLA Ops:
  0.0 1.4 slice_bitcast_fusion.3
  1.5 0.7 copy-done.1
  2.2 0.1 copy-done.5
  2.3 0.9 pad_maximum_fusion.2
  3.1 15.7 %collective-permute-start = (bf16[2,8,128,128]{3,2,1,0:T(8,128)(2,1)}, bf16[2,8,128,128]{3,2,1,0:T(8,128)(2,1)S(1)}, u32[]{:S(2)}, u32[]{:S(2)}) collective-permute-start(bf16[2,8,128,128]{3,2,1,0:T(8,128)(2,1)} %pad_maximum_fusion.2), channel_id=1, source_target_pairs={{0,1},{1,2},{2,3},{3,4},{4,5},{5,6},{6,7},{7,8},{8,9},{9,10},{10,1... | collective-permute-start | bytes 1572872 | tf_op jit(solution)/shard_map/ppermute | solution.py:15
  18.9 0.8 pad_maximum_fusion.3
  19.7 4.3 %collective-permute-start.1 = (bf16[2,8,128,128]{3,2,1,0:T(8,128)(2,1)}, bf16[2,8,128,128]{3,2,1,0:T(8,128)(2,1)S(1)}, u32[]{:S(2)}, u32[]{:S(2)}) collective-permute-start(bf16[2,8,128,128]{3,2,1,0:T(8,128)(2,1)} %pad_maximum_fusion.3), channel_id=1, source_target_pairs={{0,31},{1,0},{2,1},{3,2},{4,3},{5,4},{6,5},{7,6},{8,7},{9,8},{10,9... | collective-permute-start | bytes 1572872 | tf_op jit(solution)/shard_map/ppermute | solution.py:15
  24.1 2.9 %copy.18 = s32[64,64,8]{2,1,0:T(8,128)} copy(s32[64,64,8]{1,2,0:T(8,128)} %param.6) | data formatting | bytes 262144 | tf_op args[1]
  27.0 2.2 gather_fusion
  29.1 0.1 copy.19
  29.2 0.1 compare_reduce_fusion
  29.3 0.1 fusion
  29.4 0.1 reshape.16.table_m
  29.5 0.2 select_reduce_fusion
  29.7 0.6 copy_add_fusion
  30.4 0.9 copy.21
  31.3 0.1 add.57.table_q
  31.4 5.6 %shard_map.55.acc = f32[4,2,12,128,128]{4,3,2,1,0:T(8,128)S(1)} custom-call(s32[192]{0:T(256)S(1)} %reshape.16.table_m, s32[2304]{0:T(1024)S(1)} %add.57.table_q, bf16[4,2,8,128,128]{4,3,2,1,0:T(8,128)(2,1)S(1)} %copy-done), custom_call_target="tpu_custom_call" | custom-call | flops 4000000000 | bytes 1024 | tf_op jit(solution)/shard_map/pallas_call | solution.py:153
  37.0 0.1 slice_bitcast_fusion
  37.2 10.4 %collective-permute-start.2 = (bf16[2,8,128,128]{3,2,1,0:T(8,128)(2,1)S(1)}, bf16[2,8,128,128]{3,2,1,0:T(8,128)(2,1)S(1)}, u32[]{:S(2)}, u32[]{:S(2)}) collective-permute-start(bf16[2,8,128,128]{3,2,1,0:T(8,128)(2,1)S(1)} %get-tuple-element.17), channel_id=1, source_target_pairs={{0,1},{1,2},{2,3},{3,4},{4,5},{5,6},{6,7},{7,8},{8,9},{9,10},{10,1... | collective-permute-start | bytes 1572872 | tf_op jit(solution)/shard_map/ppermute | solution.py:15
  47.6 7.3 %collective-permute-start.3 = (bf16[2,8,128,128]{3,2,1,0:T(8,128)(2,1)S(1)}, bf16[2,8,128,128]{3,2,1,0:T(8,128)(2,1)S(1)}, u32[]{:S(2)}, u32[]{:S(2)}) collective-permute-start(bf16[2,8,128,128]{3,2,1,0:T(8,128)(2,1)S(1)} %get-tuple-element.18), channel_id=1, source_target_pairs={{0,31},{1,0},{2,1},{3,2},{4,3},{5,4},{6,5},{7,6},{8,7},{9,8},{10,9... | collective-permute-start | bytes 1572872 | tf_op jit(solution)/shard_map/ppermute | solution.py:15
  54.9 6.3 %shard_map.56.acc = f32[4,2,12,128,128]{4,3,2,1,0:T(8,128)S(1)} custom-call(s32[192]{0:T(256)S(1)} %reshape.16.table_m, s32[2304]{0:T(1024)S(1)} %add.57.table_q, bf16[4,2,8,128,128]{4,3,2,1,0:T(8,128)(2,1)S(1)} %copy-done, f32[4,2,12,128,128]{4,3,2,1,0:T(8,128)S(1)} %shard_map.55.acc), custom_call_target="tpu_custom_call" | custom-call | flops 4000000000 | bytes 1024 | tf_op jit(solution)/shard_map/pallas_call | solution.py:153
  61.2 0.1 fusion.6
  61.3 0.1 pad_maximum_fusion
  61.5 1.9 collective-permute-start.4
  63.4 0.1 pad_maximum_fusion.1
  63.6 69.4 %collective-permute-start.5 = (bf16[4,8,128,128]{3,2,1,0:T(8,128)(2,1)S(1)}, bf16[4,8,128,128]{3,2,1,0:T(8,128)(2,1)S(1)}, u32[]{:S(2)}, u32[]{:S(2)}) collective-permute-start(bf16[4,8,128,128]{3,2,1,0:T(8,128)(2,1)S(1)} %pad_maximum_fusion.1), channel_id=1, source_target_pairs={{0,480},{1,481},{2,482},{3,483},{4,484},{5,485},{6,486},{7,487},{8... | collective-permute-start | bytes 3145736 | tf_op jit(solution)/shard_map/ppermute | solution.py:15
  132.9 5.1 %shard_map.57.acc = f32[4,2,12,128,128]{4,3,2,1,0:T(8,128)S(1)} custom-call(s32[192]{0:T(256)S(1)} %reshape.16.table_m, s32[2304]{0:T(1024)S(1)} %add.57.table_q, bf16[4,2,8,128,128]{4,3,2,1,0:T(8,128)(2,1)S(1)} %copy-done, f32[4,2,12,128,128]{4,3,2,1,0:T(8,128)S(1)} %shard_map.56.acc, bf16[2,8,128,128]{3,2,1,0:T(8,128)(2,1)S(1)} %collective-permute-done.rim_low, ...), custom_call_target="tpu_custom_call" | custom-call | flops 1000000 | bytes 1024 | tf_op jit(solution)/shard_map/pallas_call | solution.py:153
  138.1 60.2 %collective-permute-done.3.mid_high = bf16[2,8,128,128]{3,2,1,0:T(8,128)(2,1)S(1)} collective-permute-done((bf16[2,8,128,128]{3,2,1,0:T(8,128)(2,1)S(1)}, bf16[2,8,128,128]{3,2,1,0:T(8,128)(2,1)S(1)}, u32[]{:S(2)}, u32[]{:S(2)}) %collective-permute-start.3) | collective-permute-done | bytes 524320 | tf_op jit(solution)/shard_map/ppermute | solution.py:15
  198.3 2.7 %shard_map.58 = (bf16[4,2,12,128,128]{4,3,2,1,0:T(8,128)(2,1)}, f32[2,2,12,128,128]{4,3,2,1,0:T(8,128)S(1)}) custom-call(s32[192]{0:T(256)S(1)} %reshape.16.table_m, s32[2304]{0:T(1024)S(1)} %add.57.table_q, bf16[4,2,8,128,128]{4,3,2,1,0:T(8,128)(2,1)S(1)} %copy-done, f32[4,2,12,128,128]{4,3,2,1,0:T(8,128)S(1)} %shard_map.57.acc, ...), custom_call_target="tpu_custom_call" | custom-call | flops 49999998976 | bytes 1024 | tf_op jit(solution)/shard_map/pallas_call | solution.py:153
  201.0 21.5 %collective-permute-done.4.near_low = bf16[4,8,128,128]{3,2,1,0:T(8,128)(2,1)S(1)} collective-permute-done((bf16[4,8,128,128]{3,2,1,0:T(8,128)(2,1)S(1)}, bf16[4,8,128,128]{3,2,1,0:T(8,128)(2,1)S(1)}, u32[]{:S(2)}, u32[]{:S(2)}) %collective-permute-start.4) | collective-permute-done | bytes 1048608 | tf_op jit(solution)/shard_map/ppermute | solution.py:15
  222.5 3.0 %shard_map.59 = bf16[4,2,12,128,128]{4,3,2,1,0:T(8,128)(2,1)} custom-call(s32[192]{0:T(256)S(1)} %reshape.16.table_m, s32[2304]{0:T(1024)S(1)} %add.57.table_q, bf16[4,2,8,128,128]{4,3,2,1,0:T(8,128)(2,1)S(1)} %copy-done, f32[2,2,12,128,128]{4,3,2,1,0:T(8,128)S(1)} %get-tuple-element.19.rest, ...), custom_call_target="tpu_custom_call", output_to_operand_aliasing={{}: (6, {})} | custom-call | flops 1000000 | bytes 1024 | tf_op jit(solution)/shard_map/pallas_call | solution.py:153
  (26 shorter events, 0.1 us)
Async XLA Ops:
  0.0 24.0 %copy-start.8 = (s32[24]{0:T(128)S(1)}, s32[24]{0:T(128)}, u32[]{:S(2)}) copy-start(s32[24]{0:T(128)} %constant.50.clone) | copy-start | bytes 292
  0.0 24.0 %copy-start.9 = (s32[24]{0:T(128)S(1)}, s32[24]{0:T(128)}, u32[]{:S(2)}) copy-start(s32[24]{0:T(128)} %constant.49.clone) | copy-start | bytes 292
  0.0 31.4 %copy-start = (bf16[4,2,8,128,128]{4,3,2,1,0:T(8,128)(2,1)S(1)}, bf16[4,2,8,128,128]{4,3,2,1,0:T(8,128)(2,1)}, u32[]{:S(2)}) copy-start(bf16[4,2,8,128,128]{4,3,2,1,0:T(8,128)(2,1)} %own.9) | copy-start | bytes 6291460
  0.0 29.5 %copy-start.7 = (s32[4,2,12]{2,1,0:T(2,128)S(1)}, s32[4,2,12]{2,1,0:T(2,128)}, u32[]{:S(2)}) copy-start(s32[4,2,12]{2,1,0:T(2,128)} %param.7) | copy-start | bytes 1156
  1.5 0.7 copy-start.1
  1.5 0.8 copy-start.5
  1.5 17.4 %copy-start.3 = (bf16[1,8,128,128]{3,2,1,0:T(8,128)(2,1)}, bf16[1,8,128,128]{3,2,1,0:T(8,128)(2,1)S(1)}, u32[]{:S(2)}) copy-start(bf16[1,8,128,128]{3,2,1,0:T(8,128)(2,1)S(1)} %get-tuple-element.24) | copy-start | bytes 786436
  3.1 58.1 %collective-permute-start = (bf16[2,8,128,128]{3,2,1,0:T(8,128)(2,1)}, bf16[2,8,128,128]{3,2,1,0:T(8,128)(2,1)S(1)}, u32[]{:S(2)}, u32[]{:S(2)}) collective-permute-start(bf16[2,8,128,128]{3,2,1,0:T(8,128)(2,1)} %pad_maximum_fusion.2), channel_id=1, source_target_pairs={{0,1},{1,2},{2,3},{3,4},{4,5},{5,6},{6,7},{7,8},{8,9},{9,10},{10,1... | collective-permute-start | bytes 1572872 | tf_op jit(solution)/shard_map/ppermute | solution.py:15
  19.7 41.5 %collective-permute-start.1 = (bf16[2,8,128,128]{3,2,1,0:T(8,128)(2,1)}, bf16[2,8,128,128]{3,2,1,0:T(8,128)(2,1)S(1)}, u32[]{:S(2)}, u32[]{:S(2)}) collective-permute-start(bf16[2,8,128,128]{3,2,1,0:T(8,128)(2,1)} %pad_maximum_fusion.3), channel_id=1, source_target_pairs={{0,31},{1,0},{2,1},{3,2},{4,3},{5,4},{6,5},{7,6},{8,7},{9,8},{10,9... | collective-permute-start | bytes 1572872 | tf_op jit(solution)/shard_map/ppermute | solution.py:15
  37.1 24.2 %copy-start.4 = (bf16[1,8,128,128]{3,2,1,0:T(8,128)(2,1)S(1)}, bf16[1,8,128,128]{3,2,1,0:T(8,128)(2,1)}, u32[]{:S(2)}) copy-start(bf16[1,8,128,128]{3,2,1,0:T(8,128)(2,1)} %copy-done.3) | copy-start | bytes 786436
  37.1 24.2 %copy-start.6 = (bf16[1,8,128,128]{3,2,1,0:T(8,128)(2,1)S(1)}, bf16[1,8,128,128]{3,2,1,0:T(8,128)(2,1)}, u32[]{:S(2)}) copy-start(bf16[1,8,128,128]{3,2,1,0:T(8,128)(2,1)} %copy-done.5) | copy-start | bytes 786436
  37.2 101.0 %collective-permute-start.2 = (bf16[2,8,128,128]{3,2,1,0:T(8,128)(2,1)S(1)}, bf16[2,8,128,128]{3,2,1,0:T(8,128)(2,1)S(1)}, u32[]{:S(2)}, u32[]{:S(2)}) collective-permute-start(bf16[2,8,128,128]{3,2,1,0:T(8,128)(2,1)S(1)} %get-tuple-element.17), channel_id=1, source_target_pairs={{0,1},{1,2},{2,3},{3,4},{4,5},{5,6},{6,7},{7,8},{8,9},{9,10},{10,1... | collective-permute-start | bytes 1572872 | tf_op jit(solution)/shard_map/ppermute | solution.py:15
  47.6 150.8 %collective-permute-start.3 = (bf16[2,8,128,128]{3,2,1,0:T(8,128)(2,1)S(1)}, bf16[2,8,128,128]{3,2,1,0:T(8,128)(2,1)S(1)}, u32[]{:S(2)}, u32[]{:S(2)}) collective-permute-start(bf16[2,8,128,128]{3,2,1,0:T(8,128)(2,1)S(1)} %get-tuple-element.18), channel_id=1, source_target_pairs={{0,31},{1,0},{2,1},{3,2},{4,3},{5,4},{6,5},{7,6},{8,7},{9,8},{10,9... | collective-permute-start | bytes 1572872 | tf_op jit(solution)/shard_map/ppermute | solution.py:15
  61.2 2.2 copy-start.2
  61.5 161.0 %collective-permute-start.4 = (bf16[4,8,128,128]{3,2,1,0:T(8,128)(2,1)S(1)}, bf16[4,8,128,128]{3,2,1,0:T(8,128)(2,1)S(1)}, u32[]{:S(2)}, u32[]{:S(2)}) collective-permute-start(bf16[4,8,128,128]{3,2,1,0:T(8,128)(2,1)S(1)} %pad_maximum_fusion), channel_id=1, source_target_pairs={{0,32},{1,33},{2,34},{3,35},{4,36},{5,37},{6,38},{7,39},{8,40},{9,... | collective-permute-start | bytes 3145736 | tf_op jit(solution)/shard_map/ppermute | solution.py:15
  63.6 159.0 %collective-permute-start.5 = (bf16[4,8,128,128]{3,2,1,0:T(8,128)(2,1)S(1)}, bf16[4,8,128,128]{3,2,1,0:T(8,128)(2,1)S(1)}, u32[]{:S(2)}, u32[]{:S(2)}) collective-permute-start(bf16[4,8,128,128]{3,2,1,0:T(8,128)(2,1)S(1)} %pad_maximum_fusion.1), channel_id=1, source_target_pairs={{0,480},{1,481},{2,482},{3,483},{4,484},{5,485},{6,486},{7,487},{8... | collective-permute-start | bytes 3145736 | tf_op jit(solution)/shard_map/ppermute | solution.py:15

commit v7 on v2

--- a/solution.py
+++ b/solution.py
@@ -218,8 +218,8 @@
     rim_high = along_y(jnp.stack([p_vals[0, 0], p_vals[last, 0]]), -1)
 
     tables = make_tables(p_cols, c_cols, cells_x, cells_y)
+    tables, middle = tie((tables, (p_vals[1:last, 1], p_vals[1:last, 0])))
     acc = run_kernel(column_kernel, tables, p_vals, [], 4 * 10**9)
-    acc, middle = tie((acc, (p_vals[1:last, 1], p_vals[1:last, 0])))
     mid_low = along_y(middle[0], 1)
     mid_high = along_y(middle[1], -1)
 

time: 220 us -> 220 us (level)
  no operation moved by 1% of the time
where the time goes in v7:
time: 220 us
  starting transfers between devices  125 us (57%)
  waiting for transfers between devices  58.7 us (27%)
  Pallas kernels  23.4 us (11%)
  local copies, waits for them, and re-layouts  9.71 us (4%)
  other arithmetic  3.16 us (1%)
    ppermute x7, starting transfers between devices, send(): lax.ppermute(value, AXES, [(a[0] * n_rows + a[1], b[0] * n_rows + b[1]) f...  125 us
    ppermute x7, waiting for transfers between devices, send(): lax.ppermute(value, AXES, [(a[0] * n_rows + a[1], b[0] * n_rows + b[1]) f...  58.7 us
    pallas_call x5, Pallas kernels, run_kernel(): pl.pallas_call(body, out_shape=out_shape, in_specs=in_specs, out_specs=ou...  23.4 us
  transfers between devices with their start and end apart: 7, of which 1 were waited for; matrix products, arithmetic and copies ran while one was open for 4% of the time, Pallas kernels for 9%

profile of v7, /device:TPU:24, one launch (start us, length us, event | category | flops | bytes accessed | tf_op | source)
XLA Modules:
  0.0 219.9 jit_solution(2559613113170268503)
XLA Ops:
  0.0 1.4 slice_bitcast_fusion.3
  1.5 0.7 copy-done.1
  2.2 0.1 copy-done.5
  2.3 0.9 pad_maximum_fusion.2
  3.2 15.7 %collective-permute-start = (bf16[2,8,128,128]{3,2,1,0:T(8,128)(2,1)}, bf16[2,8,128,128]{3,2,1,0:T(8,128)(2,1)S(1)}, u32[]{:S(2)}, u32[]{:S(2)}) collective-permute-start(bf16[2,8,128,128]{3,2,1,0:T(8,128)(2,1)} %pad_maximum_fusion.2), channel_id=1, source_target_pairs={{0,1},{1,2},{2,3},{3,4},{4,5},{5,6},{6,7},{7,8},{8,9},{9,10},{10,1... | collective-permute-start | bytes 1572872 | tf_op jit(solution)/shard_map/ppermute | solution.py:15
  18.9 0.9 pad_maximum_fusion.3
  19.8 4.3 %collective-permute-start.1 = (bf16[2,8,128,128]{3,2,1,0:T(8,128)(2,1)}, bf16[2,8,128,128]{3,2,1,0:T(8,128)(2,1)S(1)}, u32[]{:S(2)}, u32[]{:S(2)}) collective-permute-start(bf16[2,8,128,128]{3,2,1,0:T(8,128)(2,1)} %pad_maximum_fusion.3), channel_id=1, source_target_pairs={{0,31},{1,0},{2,1},{3,2},{4,3},{5,4},{6,5},{7,6},{8,7},{9,8},{10,9... | collective-permute-start | bytes 1572872 | tf_op jit(solution)/shard_map/ppermute | solution.py:15
  24.1 1.1 slice_bitcast_fusion
  25.2 2.9 %copy.20 = s32[64,64,8]{2,1,0:T(8,128)} copy(s32[64,64,8]{1,2,0:T(8,128)} %param.8) | data formatting | bytes 262144 | tf_op args[1]
  28.1 2.2 gather_fusion
  30.3 0.1 copy.21
  30.4 0.1 compare_reduce_fusion
  30.5 0.1 fusion
  30.6 0.1 reshape.16.table_m
  30.6 0.2 select_reduce_fusion
  30.9 0.6 copy_add_fusion
  31.5 0.9 copy.23
  32.5 0.1 add.57.table_q
  32.6 10.3 %collective-permute-start.2 = (bf16[2,8,128,128]{3,2,1,0:T(8,128)(2,1)}, bf16[2,8,128,128]{3,2,1,0:T(8,128)(2,1)S(1)}, u32[]{:S(2)}, u32[]{:S(2)}) collective-permute-start(bf16[2,8,128,128]{3,2,1,0:T(8,128)(2,1)} %get-tuple-element.19), channel_id=1, source_target_pairs={{0,1},{1,2},{2,3},{3,4},{4,5},{5,6},{6,7},{7,8},{8,9},{9,10},{10,1... | collective-permute-start | bytes 1572872 | tf_op jit(solution)/shard_map/ppermute | solution.py:15
  42.8 7.3 %collective-permute-start.3 = (bf16[2,8,128,128]{3,2,1,0:T(8,128)(2,1)}, bf16[2,8,128,128]{3,2,1,0:T(8,128)(2,1)S(1)}, u32[]{:S(2)}, u32[]{:S(2)}) collective-permute-start(bf16[2,8,128,128]{3,2,1,0:T(8,128)(2,1)} %get-tuple-element.20), channel_id=1, source_target_pairs={{0,31},{1,0},{2,1},{3,2},{4,3},{5,4},{6,5},{7,6},{8,7},{9,8},{10,9... | collective-permute-start | bytes 1572872 | tf_op jit(solution)/shard_map/ppermute | solution.py:15
  50.2 5.6 %shard_map.73.acc = f32[4,2,12,128,128]{4,3,2,1,0:T(8,128)S(1)} custom-call(s32[208]{0:T(256)S(1)} %reshape.16.table_m, s32[2496]{0:T(1024)S(1)} %add.57.table_q, bf16[4,2,8,128,128]{4,3,2,1,0:T(8,128)(2,1)S(1)} %copy-done), custom_call_target="tpu_custom_call" | custom-call | flops 4000000000 | bytes 1024 | tf_op jit(solution)/shard_map/pallas_call | solution.py:164
  55.8 6.4 %shard_map.74.acc = f32[4,2,12,128,128]{4,3,2,1,0:T(8,128)S(1)} custom-call(s32[208]{0:T(256)S(1)} %reshape.16.table_m, s32[2496]{0:T(1024)S(1)} %add.57.table_q, bf16[4,2,8,128,128]{4,3,2,1,0:T(8,128)(2,1)S(1)} %copy-done, f32[4,2,12,128,128]{4,3,2,1,0:T(8,128)S(1)} %shard_map.73.acc), custom_call_target="tpu_custom_call" | custom-call | flops 4000000000 | bytes 1024 | tf_op jit(solution)/shard_map/pallas_call | solution.py:164
  62.2 0.1 fusion.7
  62.3 0.1 pad_maximum_fusion
  62.5 1.9 collective-permute-start.4
  64.4 0.1 pad_maximum_fusion.1
  64.6 73.7 %collective-permute-start.5 = (bf16[4,8,128,128]{3,2,1,0:T(8,128)(2,1)S(1)}, bf16[4,8,128,128]{3,2,1,0:T(8,128)(2,1)S(1)}, u32[]{:S(2)}, u32[]{:S(2)}) collective-permute-start(bf16[4,8,128,128]{3,2,1,0:T(8,128)(2,1)S(1)} %pad_maximum_fusion.1), channel_id=1, source_target_pairs={{0,481},{1,482},{2,483},{3,484},{4,485},{5,486},{6,487},{7,488},{8... | collective-permute-start | bytes 3145736 | tf_op jit(solution)/shard_map/ppermute | solution.py:15
  138.3 11.5 %collective-permute-start.6 = (bf16[2,8,128,128]{3,2,1,0:T(8,128)(2,1)S(1)}, bf16[2,8,128,128]{3,2,1,0:T(8,128)(2,1)S(1)}, u32[]{:S(2)}, u32[]{:S(2)}) collective-permute-start(bf16[2,8,128,128]{3,2,1,0:T(8,128)(2,1)S(1)} %slice_select_fusion), channel_id=1, source_target_pairs={{480,31},{481,0},{482,1},{483,2},{484,3},{485,4},{486,5},{487,6},{... | collective-permute-start | bytes 1572872 | tf_op jit(solution)/shard_map/ppermute | solution.py:15
  149.8 5.2 %shard_map.75.acc = f32[4,2,12,128,128]{4,3,2,1,0:T(8,128)S(1)} custom-call(s32[208]{0:T(256)S(1)} %reshape.16.table_m, s32[2496]{0:T(1024)S(1)} %add.57.table_q, bf16[4,2,8,128,128]{4,3,2,1,0:T(8,128)(2,1)S(1)} %copy-done, f32[4,2,12,128,128]{4,3,2,1,0:T(8,128)S(1)} %shard_map.74.acc, bf16[2,8,128,128]{3,2,1,0:T(8,128)(2,1)S(1)} %collective-permute-done.rim_low, ...), custom_call_target="tpu_custom_call" | custom-call | flops 1000000 | bytes 1024 | tf_op jit(solution)/shard_map/pallas_call | solution.py:164
  155.0 2.7 %shard_map.76 = (bf16[4,2,12,128,128]{4,3,2,1,0:T(8,128)(2,1)}, f32[2,2,12,128,128]{4,3,2,1,0:T(8,128)S(1)}) custom-call(s32[208]{0:T(256)S(1)} %reshape.16.table_m, s32[2496]{0:T(1024)S(1)} %add.57.table_q, bf16[4,2,8,128,128]{4,3,2,1,0:T(8,128)(2,1)S(1)} %copy-done, f32[4,2,12,128,128]{4,3,2,1,0:T(8,128)S(1)} %shard_map.75.acc, ...), custom_call_target="tpu_custom_call" | custom-call | flops 49999998976 | bytes 1024 | tf_op jit(solution)/shard_map/pallas_call | solution.py:164
  157.7 58.7 %collective-permute-done.6.wrap = bf16[2,8,128,128]{3,2,1,0:T(8,128)(2,1)S(1)} collective-permute-done((bf16[2,8,128,128]{3,2,1,0:T(8,128)(2,1)S(1)}, bf16[2,8,128,128]{3,2,1,0:T(8,128)(2,1)S(1)}, u32[]{:S(2)}, u32[]{:S(2)}) %collective-permute-start.6) | collective-permute-done | bytes 524320 | tf_op jit(solution)/shard_map/ppermute | solution.py:15
  216.3 3.6 %shard_map.77 = bf16[4,2,12,128,128]{4,3,2,1,0:T(8,128)(2,1)} custom-call(s32[208]{0:T(256)S(1)} %reshape.16.table_m, s32[2496]{0:T(1024)S(1)} %add.57.table_q, bf16[4,2,8,128,128]{4,3,2,1,0:T(8,128)(2,1)S(1)} %copy-done, f32[2,2,12,128,128]{4,3,2,1,0:T(8,128)S(1)} %get-tuple-element.21.rest, ...), custom_call_target="tpu_custom_call", output_to_operand_aliasing={{}: (7, {})} | custom-call | flops 1000000 | bytes 1024 | tf_op jit(solution)/shard_map/pallas_call | solution.py:164
  (34 shorter events, 0.2 us)
Async XLA Ops:
  0.0 25.2 %copy-start.8 = (pred[26]{0:T(512)(128)(4,1)S(1)}, pred[26]{0:T(512)(128)(4,1)}, u32[]{:S(2)}) copy-start(pred[26]{0:T(512)(128)(4,1)} %constant.58.clone) | copy-start | bytes 82
  0.0 25.2 %copy-start.9 = (s32[26]{0:T(128)S(1)}, s32[26]{0:T(128)}, u32[]{:S(2)}) copy-start(s32[26]{0:T(128)} %constant.61.clone) | copy-start | bytes 316
  0.0 25.2 %copy-start.10 = (s32[26]{0:T(128)S(1)}, s32[26]{0:T(128)}, u32[]{:S(2)}) copy-start(s32[26]{0:T(128)} %constant.60.clone) | copy-start | bytes 316
  0.0 25.2 %copy-start.11 = (s32[26]{0:T(128)S(1)}, s32[26]{0:T(128)}, u32[]{:S(2)}) copy-start(s32[26]{0:T(128)} %constant.59.clone) | copy-start | bytes 316
  0.0 24.0 %copy-start = (bf16[4,2,8,128,128]{4,3,2,1,0:T(8,128)(2,1)S(1)}, bf16[4,2,8,128,128]{4,3,2,1,0:T(8,128)(2,1)}, u32[]{:S(2)}) copy-start(bf16[4,2,8,128,128]{4,3,2,1,0:T(8,128)(2,1)} %own.9) | copy-start | bytes 6291460
  1.5 0.7 copy-start.1
  1.5 0.8 copy-start.5
  1.5 17.4 %copy-start.3 = (bf16[1,8,128,128]{3,2,1,0:T(8,128)(2,1)}, bf16[1,8,128,128]{3,2,1,0:T(8,128)(2,1)S(1)}, u32[]{:S(2)}) copy-start(bf16[1,8,128,128]{3,2,1,0:T(8,128)(2,1)S(1)} %get-tuple-element.26) | copy-start | bytes 786436
  2.3 28.4 %copy-start.7 = (s32[4,2,12]{2,1,0:T(2,128)S(1)}, s32[4,2,12]{2,1,0:T(2,128)}, u32[]{:S(2)}) copy-start(s32[4,2,12]{2,1,0:T(2,128)} %param.9) | copy-start | bytes 1156
  3.2 59.0 %collective-permute-start = (bf16[2,8,128,128]{3,2,1,0:T(8,128)(2,1)}, bf16[2,8,128,128]{3,2,1,0:T(8,128)(2,1)S(1)}, u32[]{:S(2)}, u32[]{:S(2)}) collective-permute-start(bf16[2,8,128,128]{3,2,1,0:T(8,128)(2,1)} %pad_maximum_fusion.2), channel_id=1, source_target_pairs={{0,1},{1,2},{2,3},{3,4},{4,5},{5,6},{6,7},{7,8},{8,9},{9,10},{10,1... | collective-permute-start | bytes 1572872 | tf_op jit(solution)/shard_map/ppermute | solution.py:15
  19.8 42.5 %collective-permute-start.1 = (bf16[2,8,128,128]{3,2,1,0:T(8,128)(2,1)}, bf16[2,8,128,128]{3,2,1,0:T(8,128)(2,1)S(1)}, u32[]{:S(2)}, u32[]{:S(2)}) collective-permute-start(bf16[2,8,128,128]{3,2,1,0:T(8,128)(2,1)} %pad_maximum_fusion.3), channel_id=1, source_target_pairs={{0,31},{1,0},{2,1},{3,2},{4,3},{5,4},{6,5},{7,6},{8,7},{9,8},{10,9... | collective-permute-start | bytes 1572872 | tf_op jit(solution)/shard_map/ppermute | solution.py:15
  32.6 122.4 %collective-permute-start.2 = (bf16[2,8,128,128]{3,2,1,0:T(8,128)(2,1)}, bf16[2,8,128,128]{3,2,1,0:T(8,128)(2,1)S(1)}, u32[]{:S(2)}, u32[]{:S(2)}) collective-permute-start(bf16[2,8,128,128]{3,2,1,0:T(8,128)(2,1)} %get-tuple-element.19), channel_id=1, source_target_pairs={{0,1},{1,2},{2,3},{3,4},{4,5},{5,6},{6,7},{7,8},{8,9},{9,10},{10,1... | collective-permute-start | bytes 1572872 | tf_op jit(solution)/shard_map/ppermute | solution.py:15
  42.8 112.1 %collective-permute-start.3 = (bf16[2,8,128,128]{3,2,1,0:T(8,128)(2,1)}, bf16[2,8,128,128]{3,2,1,0:T(8,128)(2,1)S(1)}, u32[]{:S(2)}, u32[]{:S(2)}) collective-permute-start(bf16[2,8,128,128]{3,2,1,0:T(8,128)(2,1)} %get-tuple-element.20), channel_id=1, source_target_pairs={{0,31},{1,0},{2,1},{3,2},{4,3},{5,4},{6,5},{7,6},{8,7},{9,8},{10,9... | collective-permute-start | bytes 1572872 | tf_op jit(solution)/shard_map/ppermute | solution.py:15
  55.8 6.5 %copy-start.4 = (bf16[1,8,128,128]{3,2,1,0:T(8,128)(2,1)S(1)}, bf16[1,8,128,128]{3,2,1,0:T(8,128)(2,1)}, u32[]{:S(2)}) copy-start(bf16[1,8,128,128]{3,2,1,0:T(8,128)(2,1)} %copy-done.3) | copy-start | bytes 786436
  55.8 6.5 %copy-start.6 = (bf16[1,8,128,128]{3,2,1,0:T(8,128)(2,1)S(1)}, bf16[1,8,128,128]{3,2,1,0:T(8,128)(2,1)}, u32[]{:S(2)}) copy-start(bf16[1,8,128,128]{3,2,1,0:T(8,128)(2,1)} %copy-done.5) | copy-start | bytes 786436
  62.2 2.2 %copy-start.2 = (bf16[1,8,128,128]{3,2,1,0:T(8,128)(2,1)S(1)}, bf16[1,8,128,128]{3,2,1,0:T(8,128)(2,1)}, u32[]{:S(2)}) copy-start(bf16[1,8,128,128]{3,2,1,0:T(8,128)(2,1)} %copy-done.1) | copy-start | bytes 786436
  62.5 153.9 %collective-permute-start.4 = (bf16[4,8,128,128]{3,2,1,0:T(8,128)(2,1)S(1)}, bf16[4,8,128,128]{3,2,1,0:T(8,128)(2,1)S(1)}, u32[]{:S(2)}, u32[]{:S(2)}) collective-permute-start(bf16[4,8,128,128]{3,2,1,0:T(8,128)(2,1)S(1)} %pad_maximum_fusion), channel_id=1, source_target_pairs={{0,32},{1,33},{2,34},{3,35},{4,36},{5,37},{6,38},{7,39},{8,40},{9,... | collective-permute-start | bytes 3145736 | tf_op jit(solution)/shard_map/ppermute | solution.py:15
  64.6 151.8 %collective-permute-start.5 = (bf16[4,8,128,128]{3,2,1,0:T(8,128)(2,1)S(1)}, bf16[4,8,128,128]{3,2,1,0:T(8,128)(2,1)S(1)}, u32[]{:S(2)}, u32[]{:S(2)}) collective-permute-start(bf16[4,8,128,128]{3,2,1,0:T(8,128)(2,1)S(1)} %pad_maximum_fusion.1), channel_id=1, source_target_pairs={{0,481},{1,482},{2,483},{3,484},{4,485},{5,486},{6,487},{7,488},{8... | collective-permute-start | bytes 3145736 | tf_op jit(solution)/shard_map/ppermute | solution.py:15
  138.3 78.0 %collective-permute-start.6 = (bf16[2,8,128,128]{3,2,1,0:T(8,128)(2,1)S(1)}, bf16[2,8,128,128]{3,2,1,0:T(8,128)(2,1)S(1)}, u32[]{:S(2)}, u32[]{:S(2)}) collective-permute-start(bf16[2,8,128,128]{3,2,1,0:T(8,128)(2,1)S(1)} %slice_select_fusion), channel_id=1, source_target_pairs={{480,31},{481,0},{482,1},{483,2},{484,3},{485,4},{486,5},{487,6},{... | collective-permute-start | bytes 1572872 | tf_op jit(solution)/shard_map/ppermute | solution.py:15
